TPU v7x, 32 devices: a whole 2x2x4 slice. The times are simulated.
32 devices in a mesh: occ: 2 (over core), aux: 16 (over z, y, x).
Axes of the slice: x: 2, y: 2, z: 4, core: 2. Of those that a mesh axis runs over, the one named last changes fastest.
Arguments:
- coeffs: bfloat16 [2, 256, 65536], P('occ', None, 'aux'), may hold values from -0.375 to 0.375
- occ_energy: bfloat16 [2], P('occ'), may hold values from -1.5 to -0.29882812
- virt_energy: bfloat16 [256], replicated, may hold values from 0.19921875 to 3
- screen: int32 [2, 512], P('occ', 'aux'), may hold values 0 or 1
- owner: int32 [512], P('aux'), may hold values from 0 to 127
- positions: float32 [3, 128], replicated, may hold values from -1 to 1
Outputs:
- gamma: bfloat16 [2, 256, 65536], P('occ', None, 'aux')
- virial: float32 [9, 65536], P(None, 'aux')
All inputs are finite; a program needn't handle non-finite values. No bound on the sum of `screen` on one device may be relied on, other than what follows from the above.
Results may differ from a plain program's by a relative error of at most 0.0049.
Values may be sent and summed in bfloat16 or wider, within the bound.
No kernel may reach another device: no remote copies, remote signals or barrier semaphores. Data moves between devices by JAX's collectives and lax.ppermute only.
A program may use at most 64 MiB of HBM per device.

v0:
```python
import jax
import jax.numpy as jnp
from jax import lax
from jax.sharding import PartitionSpec as P

ABLK = 128


def body(coeffs, occ_energy, virt_energy, screen, owner, positions):
    occ_dev, virt, aux_dev = coeffs.shape
    column_mask = jnp.repeat(screen[0], ABLK).astype(jnp.bfloat16)
    masked = coeffs * column_mask[None, None, :]
    whole, energies = (
        lax.all_gather(masked, "occ", axis=0, tiled=True),
        lax.all_gather(occ_energy, "occ", axis=0, tiled=True),
    )
    all_rows = whole.reshape(-1, aux_dev)
    local = masked.reshape(-1, aux_dev)
    virt_f = virt_energy.astype(jnp.float32)
    spread_local = (virt_f[None, :] - occ_energy.astype(jnp.float32)[:, None]).reshape(-1)
    spread_all = (virt_f[None, :] - energies.astype(jnp.float32)[:, None]).reshape(-1)
    contract_last = (((1,), (1,)), ((), ()))
    contract_first = (((0,), (0,)), ((), ()))
    summed = lax.psum(
        lax.dot_general(all_rows, local, contract_last, preferred_element_type=jnp.float32), "aux"
    )
    amps = (summed / (spread_all[:, None] + spread_local[None, :])).astype(jnp.bfloat16)
    gamma = lax.dot_general(amps, all_rows, contract_first, preferred_element_type=jnp.float32)
    gamma_out = gamma.astype(jnp.bfloat16)
    partial_weight = jnp.sum(gamma_out.astype(jnp.float32) * local.astype(jnp.float32), axis=0)
    weight = lax.psum(partial_weight, "occ")
    atom_ids = jnp.arange(positions.shape[1], dtype=jnp.int32)
    onehot = (owner[:, None] == atom_ids[None, :]).astype(jnp.float32)
    block_where = jnp.dot(onehot, positions.T, precision=lax.Precision.HIGHEST)
    where = jnp.repeat(block_where.T, ABLK, axis=1)
    virial = (where[:, None, :] * where[None, :, :]).reshape(9, aux_dev) * weight[None, :]
    return (gamma_out.reshape(occ_dev, virt, aux_dev), virial)


def solution(mesh):
    placed = (P("occ", None, "aux"), P("occ"), P(), P("occ", "aux"), P("aux"), P())
    return jax.shard_map(
        body,
        mesh=mesh,
        in_specs=placed,
        out_specs=(P("occ", None, "aux"), P(None, "aux")),
        check_vma=False,
    )
```

profile of v0, /device:TPU:0, one launch (start us, length us, event | category | flops | bytes accessed | tf_op | source)
XLA Modules:
  0.0 158.6 jit_solution(17306978146444016541)
XLA Ops:
  7.2 0.0 copy-start
  7.2 0.0 copy-start.4
  7.2 0.0 copy-start.3
  7.2 0.0 all-gather.2.cloned.1.call-start
  7.2 0.7 convert_bitcast_fusion
  7.9 0.1 broadcast_bitcast_fusion.1
  8.0 3.1 %broadcast_multiply_fusion = bf16[1,256,4096]{2,1,0:T(8,128)(2,1)} fusion(bf16[1,256,4096]{2,1,0:T(8,128)(2,1)} %param.6, bf16[4096]{0:T(1024)(128)(2,1)S(1)} %broadcast_bitcast_fusion.1), kind=kLoop, calls=%fused_computation.5 | loop fusion | flops 1048576 | bytes 4202496 | tf_op jit(solution)/shard_map/mul | solution.py:12
  11.0 0.0 all-gather.2.cloned.1.call-update
  11.1 0.0 all-reduce.3.cloned.1.call-start
  11.8 0.0 copy-done
  11.8 0.0 copy-done.3
  11.8 0.2 convolution_bitcast_fusion
  12.0 0.1 broadcast_bitcast_fusion
  12.1 0.1 copy.11
  12.1 0.0 copy-done.4
  12.1 0.6 dynamic-slice
  12.8 0.7 dynamic-update-slice
  13.5 14.2 %all-gather.2.cloned.1.call-done = bf16[2,256,4096]{2,1,0:T(8,128)(2,1)} async-done(((bf16[1,256,4096]{2,1,0:T(8,128)(2,1)}), bf16[2,256,4096]{2,1,0:T(8,128)(2,1)}) %all-gather.2.cloned.1.call-update) | async-done | bytes 4194320 | tf_op jit(solution)/shard_map/all_gather | solution.py:14
  27.7 0.0 copy-start.2
  27.7 0.0 copy-start.1
  27.7 5.1 %fusion = f32[512,256]{1,0:T(8,128)} fusion(bf16[512,4096]{1,0:T(8,128)(2,1)} %bitcast.27, bf16[1,256,4096]{2,1,0:T(8,128)(2,1)} %broadcast_multiply_fusion), kind=kOutput, calls=%fused_computation.2 | convolution fusion | flops 1073741824 | bytes 6815744 | tf_op jit(solution)/shard_map/dot_general | solution.py:25
  32.8 0.0 all-reduce.3.cloned.1.call-update
  32.8 2.5 %all-reduce = bf16[2]{0:T(256)(128)(2,1)S(1)} all-reduce(bf16[2]{0:T(256)(128)(2,1)S(1)} %dynamic-update-slice), channel_id=1, replica_groups=mesh['occ'=2,'aux'=16] {'occ'}, use_global_device_ids=true, to_apply=%add | all-reduce | flops 2 | bytes 8
  35.3 0.0 copy-done.2
  35.3 0.1 subtract_bitcast_fusion
  35.4 0.1 mul.44
  35.5 106.9 %all-reduce.3.cloned.1.call-done = f32[512,256]{1,0:T(8,128)} async-done(((f32[512,256]{1,0:T(8,128)}), f32[512,256]{1,0:T(8,128)}) %all-reduce.3.cloned.1.call-update) | async-done | bytes 524304 | tf_op jit(solution)/shard_map/psum | solution.py:24
  142.4 0.0 copy-done.1
  142.4 5.3 %multiply_reduce_fusion = (f32[4096]{0:T(1024)S(1)}, bf16[256,4096]{1,0:T(8,128)(2,1)}) fusion(bf16[1,256,4096]{2,1,0:T(8,128)(2,1)S(1)} %copy-done.1, bf16[512,4096]{1,0:T(8,128)(2,1)} %bitcast.28, f32[512,256]{1,0:T(8,128)} %all-reduce.3.cloned.1.call-done, f32[256]{0:T(256)S(1)} %broadcast_subtract_fusion, f32[512]{0:T(512)S(1)} %bitcast.31), kind=kOutput, calls=%fused_computation.1 | convolution fusion | flops 1079373824 | bytes 8932352 | tf_op jit(solution)/shard_map/dot_general | solution.py:28
  147.7 3.3 %psum.15 = f32[4096]{0:T(1024)S(1)} all-reduce(f32[4096]{0:T(1024)S(1)} %get-tuple-element.2), channel_id=1, replica_groups=mesh['occ'=2,'aux'=16] {'occ'}, use_global_device_ids=true, to_apply=%region_2.0 | all-reduce | flops 4096 | bytes 32768 | tf_op jit(solution)/shard_map/psum | solution.py:31
  151.1 0.7 broadcast_multiply_fusion.1
  (6 shorter events, 0.1 us)
Async XLA Ops:
  7.2 4.6 %copy-start = (f32[3,128]{1,0:T(4,128)S(1)}, f32[3,128]{1,0:T(4,128)}, u32[]{:S(2)}) copy-start(f32[3,128]{1,0:T(4,128)} %param.11) | copy-start | bytes 4612
  7.2 5.0 %copy-start.4 = (u32[32]{0:T(128)S(1)}, u32[32]{0:T(128)}, u32[]{:S(2)}) copy-start(u32[32]{0:T(128)} %constant.7) | copy-start | bytes 388
  7.2 4.6 %copy-start.3 = (s32[32]{0:T(128)S(1)}, s32[32]{0:T(128)}, u32[]{:S(2)}) copy-start(s32[32]{0:T(128)} %param.10) | copy-start | bytes 388
  7.2 20.5 %all-gather.2.cloned.1.call-start = ((), (), s32[]{:S(2)}) async-start(), calls=%async_computation | async-start | bytes 6291456 | tf_op jit(solution)/shard_map/all_gather | solution.py:14
  11.1 131.4 %all-reduce.3.cloned.1.call-start = ((), (), s32[]{:S(2)}) async-start(), calls=%async_computation.1 | async-start | bytes 1048576 | tf_op jit(solution)/shard_map/psum | solution.py:24
  27.7 7.7 %copy-start.2 = (bf16[256]{0:T(256)(128)(2,1)S(1)}, bf16[256]{0:T(256)(128)(2,1)}, u32[]{:S(2)}) copy-start(bf16[256]{0:T(256)(128)(2,1)} %param.8) | copy-start | bytes 1540
  27.7 114.8 %copy-start.1 = (bf16[1,256,4096]{2,1,0:T(8,128)(2,1)S(1)}, bf16[1,256,4096]{2,1,0:T(8,128)(2,1)}, u32[]{:S(2)}) copy-start(bf16[1,256,4096]{2,1,0:T(8,128)(2,1)} %broadcast_multiply_fusion) | copy-start | bytes 6291460
Sparse Core Ops, SparseCore 0:
  11.2 16.4 all-gather.1
  32.9 109.4 all-reduce.2
where the time goes:
time: 159 us
  waiting for transfers between devices  121 us (76%)
  between operations  14.8 us (9%)
  matrix products  10.6 us (7%)
  blocking collectives  5.82 us (4%)
  other arithmetic  4.57 us (3%)
  local copies, waits for them, and re-layouts  1.65 us (1%)
    psum x1, waiting for transfers between devices, body(): lax.psum(lax.dot_general(all_rows, local, contract_last, preferred_elemen...  107 us
    all_gather x1, waiting for transfers between devices, body(): lax.all_gather(masked, 'occ', axis=0, tiled=True)  14.2 us
    dot_general x1, matrix products, body(): lax.dot_general(amps, all_rows, contract_first, preferred_element_type=jn...  5.29 us
    dot_general x1, matrix products, body(): lax.dot_general(all_rows, local, contract_last, preferred_element_type=jn...  5.1 us
    psum x1, blocking collectives, body(): weight = lax.psum(partial_weight, 'occ')  3.35 us
  transfers between devices with their start and end apart: 2, of which 2 were waited for; matrix products, arithmetic and copies ran while one was open for 1% of the time, Pallas kernels for 0%

commit v1 on v0

v1 whole, which is shorter than its diff:
```python
import functools

import jax
import jax.numpy as jnp
from jax import lax
from jax.experimental import pallas as pl
from jax.experimental.pallas import tpu as pltpu
from jax.sharding import PartitionSpec as P

F32 = jnp.float32
BF16 = jnp.bfloat16
CONTRACT_LAST = (((1,), (1,)), ((), ()))
SMEM = pltpu.MemorySpace.SMEM
VMEM = pltpu.MemorySpace.VMEM


def mask_row(screen_ref, first, count, width):
    pieces = [
        jnp.full((1, width), screen_ref[0, first + k].astype(F32), F32) for k in range(count)
    ]
    return jnp.concatenate(pieces, axis=1).astype(BF16)


def own_pairs_kernel(blocks, width, screen_ref, own_ref, sum_ref, send_ref, total):
    step = pl.program_id(0)
    own = own_ref[...]
    mask = mask_row(screen_ref, step * blocks, blocks, width)
    term = lax.dot_general(own * mask, own, CONTRACT_LAST, preferred_element_type=F32)

    @pl.when(step == 0)
    def _():
        total[...] = term

    @pl.when(step > 0)
    def _():
        total[...] += term

    @pl.when(step == pl.num_programs(0) - 1)
    def _():
        half = total.shape[0] // 2
        low, high = pl.ds(0, half), pl.ds(half, half)
        for place, (rows, cols) in enumerate(((low, low), (high, low), (high, high))):
            part = total[rows, cols]
            sum_ref[pl.ds(place * half, half), :] = part
            send_ref[pl.ds(place * half, half), :] = part.astype(BF16)


def cross_pairs_kernel(
    blocks, width, screen_ref, other_screen_ref, own_ref, other_ref, sum_ref, send_ref, total
):
    step = pl.program_id(0)
    core = lax.axis_index("occ")
    mask = mask_row(screen_ref, step * blocks, blocks, width) * mask_row(
        other_screen_ref, step * blocks, blocks, width
    )
    term = lax.dot_general(
        own_ref[...] * mask, other_ref[...], CONTRACT_LAST, preferred_element_type=F32
    )

    @pl.when(step == 0)
    def _():
        total[...] = term

    @pl.when(step > 0)
    def _():
        total[...] += term

    @pl.when(step == pl.num_programs(0) - 1)
    def _():
        half = total.shape[0] // 2
        for place in range(2):
            rows = pl.ds(place * half, half)
            straight = total[rows, pl.ds(place * half, half)]
            across = total[rows, pl.ds((1 - place) * half, half)]
            part = jnp.where(core == 0, straight, across)
            sum_ref[rows, :] = part
            send_ref[rows, :] = part.astype(BF16)


def tiles(aux_dev, blocks):
    steps = 4 if blocks % 4 == 0 else 1
    return steps, aux_dev // steps, blocks // steps


def own_pairs(own, screen):
    virt, aux_dev = own.shape
    blocks = screen.shape[1]
    steps, tile, per_step = tiles(aux_dev, blocks)
    half = virt // 2
    return pl.pallas_call(
        functools.partial(own_pairs_kernel, per_step, aux_dev // blocks),
        grid=(steps,),
        in_specs=[
            pl.BlockSpec(memory_space=SMEM),
            pl.BlockSpec((virt, tile), lambda i: (0, i)),
        ],
        out_specs=[pl.BlockSpec((3 * half, half), lambda i: (0, 0))] * 2,
        out_shape=[
            jax.ShapeDtypeStruct((3 * half, half), F32),
            jax.ShapeDtypeStruct((3 * half, half), BF16),
        ],
        scratch_shapes=[pltpu.VMEM((virt, virt), F32)],
        compiler_params=pltpu.CompilerParams(vmem_limit_bytes=16 << 20),
        cost_estimate=pl.CostEstimate(
            flops=2 * virt * virt * aux_dev, bytes_accessed=2 * virt * aux_dev, transcendentals=0
        ),
        name="own_pairs",
    )(screen, own)


def cross_pairs(own, other, screen, other_screen):
    virt, aux_dev = own.shape
    blocks = screen.shape[1]
    steps, tile, per_step = tiles(aux_dev, blocks)
    half = virt // 2
    return pl.pallas_call(
        functools.partial(cross_pairs_kernel, per_step, aux_dev // blocks),
        grid=(steps,),
        in_specs=[
            pl.BlockSpec(memory_space=SMEM),
            pl.BlockSpec(memory_space=SMEM),
            pl.BlockSpec((virt, tile), lambda i: (0, i)),
            pl.BlockSpec((virt, tile), lambda i: (0, i)),
        ],
        out_specs=[pl.BlockSpec((2 * half, half), lambda i: (0, 0))] * 2,
        out_shape=[
            jax.ShapeDtypeStruct((2 * half, half), F32),
            jax.ShapeDtypeStruct((2 * half, half), BF16),
        ],
        scratch_shapes=[pltpu.VMEM((virt, virt), F32)],
        compiler_params=pltpu.CompilerParams(vmem_limit_bytes=16 << 20),
        cost_estimate=pl.CostEstimate(
            flops=2 * virt * virt * aux_dev, bytes_accessed=4 * virt * aux_dev, transcendentals=0
        ),
        name="cross_pairs",
    )(screen, other_screen, own, other)


def symmetric(packed):
    half = packed.shape[1]
    first, low, last = (packed[k * half : (k + 1) * half, :] for k in range(3))
    top = jnp.concatenate([first, low.T], axis=1)
    return jnp.concatenate([top, jnp.concatenate([low, last], axis=1)], axis=0)


def gamma_kernel(
    blocks,
    width,
    screen_ref,
    other_screen_ref,
    owner_ref,
    positions_ref,
    energy_ref,
    other_energy_ref,
    virt_ref,
    own_sum_ref,
    other_sum_ref,
    cross_sum_ref,
    other_cross_ref,
    own_ref,
    other_ref,
    gamma_ref,
    virial_ref,
    amps,
    other_amps,
):
    step = pl.program_id(0)
    core = lax.axis_index("occ")
    virt = own_ref.shape[0]
    half = virt // 2

    @pl.when(step == 0)
    def _():
        virt_row = jnp.broadcast_to(virt_ref[...].astype(F32), (virt, virt))
        virt_col = virt_row.T
        energy = energy_ref[...].astype(F32)
        other_energy = other_energy_ref[...].astype(F32)
        own_row, own_col = virt_row - energy, virt_col - energy
        other_row, other_col = virt_row - other_energy, virt_col - other_energy
        amps[:, 0:virt] = (symmetric(own_sum_ref[...]) / (own_col + own_row)).astype(BF16)
        other_amps[...] = (symmetric(other_sum_ref[...]) / (other_col + other_row)).astype(BF16)
        mine = [cross_sum_ref[pl.ds(k * half, half), :] for k in range(2)]
        theirs = [other_cross_ref[pl.ds(k * half, half), :].T for k in range(2)]
        even = core == 0
        cross = jnp.concatenate(
            [
                jnp.concatenate(
                    [jnp.where(even, mine[0], theirs[0]), jnp.where(even, theirs[1], mine[0])], axis=1
                ),
                jnp.concatenate(
                    [jnp.where(even, theirs[0], mine[1]), jnp.where(even, mine[1], theirs[1])], axis=1
                ),
            ],
            axis=0,
        )
        amps[:, virt : 2 * virt] = (cross / (own_col + other_row)).astype(BF16)

    own = own_ref[...] * mask_row(screen_ref, step * blocks, blocks, width)
    other = other_ref[...] * mask_row(other_screen_ref, step * blocks, blocks, width)
    cross_part = jnp.dot(amps[:, virt : 2 * virt], other, preferred_element_type=F32)
    gamma = (
        jnp.dot(amps[:, 0:virt], own, preferred_element_type=F32) + cross_part
    ).astype(BF16)
    gamma_ref[...] = gamma
    other_part = jnp.dot(other_amps[...], other, preferred_element_type=F32)
    weight = jnp.sum(
        (gamma.astype(F32) + cross_part) * own.astype(F32) + other_part * other.astype(F32),
        axis=0,
        keepdims=True,
    )
    for k in range(blocks):
        atom = owner_ref[0, step * blocks + k]
        where = [positions_ref[c, atom] for c in range(3)]
        part = weight[:, k * width : (k + 1) * width]
        rows = [part * (where[c] * where[d]) for c in range(3) for d in range(3)]
        virial_ref[:, k * width : (k + 1) * width] = jnp.concatenate(rows, axis=0)


def gamma_and_virial(
    own, other, screen, other_screen, owner, positions, energy, other_energy, virt_energy,
    own_sum, other_sum, cross_sum, other_cross,
):
    virt, aux_dev = own.shape
    blocks = screen.shape[1]
    steps, tile, per_step = tiles(aux_dev, blocks)
    smem = pl.BlockSpec(memory_space=SMEM)
    vmem = pl.BlockSpec(memory_space=VMEM)
    column_block = pl.BlockSpec((virt, tile), lambda i: (0, i))
    return pl.pallas_call(
        functools.partial(gamma_kernel, per_step, aux_dev // blocks),
        grid=(steps,),
        in_specs=[smem] * 4 + [vmem] * 7 + [column_block] * 2,
        out_specs=[column_block, pl.BlockSpec((9, tile), lambda i: (0, i))],
        out_shape=[
            jax.ShapeDtypeStruct((virt, aux_dev), BF16),
            jax.ShapeDtypeStruct((9, aux_dev), F32),
        ],
        scratch_shapes=[pltpu.VMEM((virt, 2 * virt), BF16), pltpu.VMEM((virt, virt), BF16)],
        compiler_params=pltpu.CompilerParams(vmem_limit_bytes=24 << 20),
        cost_estimate=pl.CostEstimate(
            flops=6 * virt * virt * aux_dev, bytes_accessed=6 * virt * aux_dev, transcendentals=0
        ),
        name="gamma_and_virial",
    )(
        screen, other_screen, owner.reshape(1, -1), positions,
        energy.reshape(1, 1), other_energy.reshape(1, 1), virt_energy.reshape(1, -1),
        own_sum, other_sum, cross_sum, other_cross, own, other,
    )


def swap(array, axis, size, bit):
    return lax.ppermute(array, axis, [(i, i ^ bit) for i in range(size)])


def sum_over_aux(total, send, n_aux, bits):
    for bit in bits:
        total = total + swap(send, "aux", n_aux, bit).astype(F32)
        send = total.astype(BF16)
    return total


def two_occ_body(n_aux, coeffs, occ_energy, virt_energy, screen, owner, positions):
    own = coeffs[0]
    other = swap(own, "occ", 2, 1)
    other_screen = swap(screen, "occ", 2, 1)
    other_energy = swap(occ_energy, "occ", 2, 1)
    bits = [1 << k for k in range(n_aux.bit_length() - 1)]
    own_sum, own_send = own_pairs(own, screen)
    cross_sum, cross_send = cross_pairs(own, other, screen, other_screen)
    own_sum = sum_over_aux(own_sum, own_send, n_aux, bits)
    cross_sum = sum_over_aux(cross_sum, cross_send, n_aux, bits)
    other_sum = swap(own_sum, "occ", 2, 1)
    other_cross = swap(cross_sum, "occ", 2, 1)
    gamma, virial = gamma_and_virial(
        own, other, screen, other_screen, owner, positions, occ_energy, other_energy, virt_energy,
        own_sum, other_sum, cross_sum, other_cross,
    )
    return gamma[None], virial


def general_body(n_aux, coeffs, occ_energy, virt_energy, screen, owner, positions):
    occ_dev, virt, aux_dev = coeffs.shape
    width = aux_dev // screen.shape[1]
    column_mask = jnp.repeat(screen[0], width).astype(BF16)
    masked = coeffs * column_mask[None, None, :]
    whole = lax.all_gather(masked, "occ", axis=0, tiled=True)
    energies = lax.all_gather(occ_energy, "occ", axis=0, tiled=True)
    all_rows = whole.reshape(-1, aux_dev)
    local = masked.reshape(-1, aux_dev)
    virt_f = virt_energy.astype(F32)
    spread_local = (virt_f[None, :] - occ_energy.astype(F32)[:, None]).reshape(-1)
    spread_all = (virt_f[None, :] - energies.astype(F32)[:, None]).reshape(-1)
    pairs = lax.dot_general(all_rows, local, CONTRACT_LAST, preferred_element_type=F32)
    if n_aux & (n_aux - 1):
        summed = lax.psum(pairs, "aux")
    else:
        bits = [1 << k for k in range(n_aux.bit_length() - 1)]
        summed = sum_over_aux(pairs, pairs.astype(BF16), n_aux, bits)
    amps = (summed / (spread_all[:, None] + spread_local[None, :])).astype(BF16)
    gamma = lax.dot_general(
        amps, all_rows, (((0,), (0,)), ((), ())), preferred_element_type=F32
    ).astype(BF16)
    partial_weight = jnp.sum(gamma.astype(F32) * local.astype(F32), axis=0)
    weight = lax.psum(partial_weight, "occ")
    where = jnp.repeat(positions[:, owner], width, axis=1)
    virial = (where[:, None, :] * where[None, :, :]).reshape(9, aux_dev) * weight[None, :]
    return gamma.reshape(occ_dev, virt, aux_dev), virial


def solution(mesh):
    placed = (P("occ", None, "aux"), P("occ"), P(), P("occ", "aux"), P("aux"), P())
    n_occ, n_aux = mesh.shape["occ"], mesh.shape["aux"]
    power_of_two = n_aux & (n_aux - 1) == 0

    def body(coeffs, *rest):
        fits = n_occ == 2 and coeffs.shape[0] == 1 and power_of_two
        chosen = two_occ_body if fits else general_body
        return chosen(n_aux, coeffs, *rest)

    return jax.shard_map(
        body,
        mesh=mesh,
        in_specs=placed,
        out_specs=(P("occ", None, "aux"), P(None, "aux")),
        check_vma=False,
    )
```

time: 159 us -> 38.1 us (0.24)
  waiting for transfers between devices: 121 us -> 8.62 us
  starting transfers between devices: 0.08 us -> 15.4 us
  between operations: 14.8 us -> 1.44 us
  matrix products: 10.6 us -> 0 us
  Pallas kernels: 0 us -> 9.89 us
  blocking collectives: 5.82 us -> 0 us
  other arithmetic: 4.57 us -> 0.34 us
    psum x1 -> x0, waiting for transfers between devices: 107 us -> none  [body(): lax.psum(lax.dot_general(all_rows, local, contract_last, preferred_elemen...]
    ppermute x0 -> x13, starting transfers between devices: none -> 15.4 us  [swap(): return lax.ppermute(array, axis, [(i, i ^ bit) for i in range(size)])]
    all_gather x1 -> x0, waiting for transfers between devices: 14.2 us -> none  [body(): lax.all_gather(masked, 'occ', axis=0, tiled=True)]
    dot_general x3 -> x0, matrix products: 10.6 us -> none  [the longest x1 5.29 us: body(): lax.dot_general(amps, all_rows, contract_first, preferred_element_type=jn...]
    pallas_call x0 -> x3, Pallas kernels: none -> 9.89 us  [the longest x1 5.38 us: gamma_and_virial(): pl.pallas_call(functools.partial(gamma_kernel, per_step, aux_dev // block...]
    ppermute x0 -> x13, waiting for transfers between devices: none -> 8.62 us  [swap(): return lax.ppermute(array, axis, [(i, i ^ bit) for i in range(size)])]
    mul x3 -> x0, other arithmetic: 3.82 us -> none  [the longest x1 3.05 us: body(): masked = coeffs * column_mask[None, None, :]]
    psum x1 -> x0, blocking collectives: 3.35 us -> none  [body(): weight = lax.psum(partial_weight, 'occ')]
  transfers between devices with their start and end apart: 2 -> 13, of which waited for: 2 -> 8; matrix products, arithmetic and copies ran while one was open for 1% -> 1% of each run, Pallas kernels for 0% -> 12%
where the time goes in v1:
time: 38.1 us; the launch traced here: 37.9 us
  starting transfers between devices  15.4 us (40%)
  Pallas kernels  9.89 us (26%)
  waiting for transfers between devices  8.62 us (23%)
  local copies, waits for them, and re-layouts  2.28 us (6%)
  between operations  1.44 us (4%)
    ppermute x13, starting transfers between devices, swap(): return lax.ppermute(array, axis, [(i, i ^ bit) for i in range(size)])  15.4 us
    ppermute x13, waiting for transfers between devices, swap(): return lax.ppermute(array, axis, [(i, i ^ bit) for i in range(size)])  8.62 us
    pallas_call x1, Pallas kernels, gamma_and_virial(): pl.pallas_call(functools.partial(gamma_kernel, per_step, aux_dev // block...  5.38 us
    pallas_call x1, Pallas kernels, cross_pairs(): pl.pallas_call(functools.partial(cross_pairs_kernel, per_step, aux_dev //...  2.31 us
    unnamed x14, local copies, waits for them, and re-layouts  2.28 us
    pallas_call x1, Pallas kernels, own_pairs(): pl.pallas_call(functools.partial(own_pairs_kernel, per_step, aux_dev // b...  2.2 us
  transfers between devices with their start and end apart: 13, of which 8 were waited for; matrix products, arithmetic and copies ran while one was open for 1% of the time, Pallas kernels for 12%

profile of v1, /device:TPU:0, one launch (start us, length us, event | category | flops | bytes accessed | tf_op | source)
XLA Modules:
  0.0 37.9 jit_solution(9588990142013208714)
XLA Ops:
  0.6 0.5 %collective-permute-start.7 = (bf16[256,4096]{1,0:T(8,128)(2,1)}, bf16[256,4096]{1,0:T(8,128)(2,1)S(1)}, u32[]{:S(2)}, u32[]{:S(2)}) collective-permute-start(bf16[256,4096]{1,0:T(8,128)(2,1)} %bitcast.6), channel_id=1, source_target_pairs={{0,16},{16,0},{1,17},{17,1},{2,18},{18,2},{3,19},{19,3},{4,20},{20... | collective-permute-start | bytes 6291464 | tf_op jit(solution)/shard_map/ppermute | solution.py:252
  1.1 0.0 copy-start
  1.1 1.6 %copy-done = bf16[1,256,4096]{2,1,0:T(8,128)(2,1)S(1)} copy-done((bf16[1,256,4096]{2,1,0:T(8,128)(2,1)S(1)}, bf16[1,256,4096]{2,1,0:T(8,128)(2,1)}, u32[]{:S(2)}) %copy-start) | copy-done | bytes 2097176
  2.7 0.0 copy-start.2
  2.7 0.7 %copy-done.2 = s32[1,32]{1,0:T(1,128)S(1)} copy-done((s32[1,32]{1,0:T(1,128)S(1)}, s32[1,32]{1,0:T(1,128)}, u32[]{:S(2)}) %copy-start.2) | copy-done | bytes 152
  3.4 2.2 %own_pairs.1 = (f32[384,128]{1,0:T(8,128)S(1)}, bf16[384,128]{1,0:T(8,128)(2,1)S(1)}) custom-call(s32[1,32]{1,0:T(1,128)S(1)} %copy-done.2, bf16[256,4096]{1,0:T(8,128)(2,1)S(1)} %bitcast.7), custom_call_target="tpu_custom_call" | custom-call | flops 536870912 | bytes 2097152 | tf_op jit(solution)/shard_map/own_pairs/pallas_call | solution.py:90
  5.6 2.6 %collective-permute-start.2 = (bf16[384,128]{1,0:T(8,128)(2,1)S(1)}, bf16[384,128]{1,0:T(8,128)(2,1)S(1)}, u32[]{:S(2)}, u32[]{:S(2)}) collective-permute-start(bf16[384,128]{1,0:T(8,128)(2,1)S(1)} %get-tuple-element.9), channel_id=1, source_target_pairs={{0,1},{1,0},{2,3},{3,2},{4,5},{5,4},{6,7},{7,6},{8,9},{9,8},{10,11... | collective-permute-start | bytes 294920 | tf_op jit(solution)/shard_map/ppermute | solution.py:252
  8.2 0.2 collective-permute-start
  8.4 0.9 %collective-permute-done.other_screen_ref = s32[1,32]{1,0:T(1,128)S(1)} collective-permute-done((s32[1,32]{1,0:T(1,128)S(1)}, s32[1,32]{1,0:T(1,128)S(1)}, u32[]{:S(2)}, u32[]{:S(2)}) %collective-permute-start) | collective-permute-done | bytes 160 | tf_op jit(solution)/shard_map/ppermute | solution.py:252
  9.3 0.0 collective-permute-done.7.other_ref
  9.3 2.3 %cross_pairs.1 = (f32[256,128]{1,0:T(8,128)S(1)}, bf16[256,128]{1,0:T(8,128)(2,1)S(1)}) custom-call(s32[1,32]{1,0:T(1,128)S(1)} %copy-done.2, s32[1,32]{1,0:T(1,128)S(1)} %collective-permute-done.other_screen_ref, bf16[256,4096]{1,0:T(8,128)(2,1)S(1)} %bitcast.8, bf16[256,4096]{1,0:T(8,128)(2,1)S(1)} %collective-permute-done.7.other_ref), custom_call_target="tpu_custom_call" | custom-call | flops 536870912 | bytes 4194304 | tf_op jit(solution)/shard_map/cross_pairs/pallas_call | solution.py:116
  11.6 0.0 copy-start.6
  11.6 0.0 copy-start.1
  11.6 0.0 copy-start.3
  11.7 0.0 copy-start.4
  11.7 0.0 copy-start.5
  11.7 0.3 collective-permute-start.8
  12.0 0.0 collective-permute-done.2
  12.0 1.9 %collective-permute-start.3 = (bf16[384,128]{1,0:T(8,128)(2,1)S(1)}, bf16[384,128]{1,0:T(8,128)(2,1)S(1)}, u32[]{:S(2)}, u32[]{:S(2)}) collective-permute-start(bf16[384,128]{1,0:T(8,128)(2,1)S(1)} %fusion), channel_id=1, source_target_pairs={{0,2},{1,3},{2,0},{3,1},{4,6},{5,7},{6,4},{7,5},{8,10},{9,11},{10,... | collective-permute-start | bytes 294920 | tf_op jit(solution)/shard_map/ppermute | solution.py:252
  13.9 2.1 %collective-permute-done.8 = bf16[256,128]{1,0:T(8,128)(2,1)S(1)} collective-permute-done((bf16[256,128]{1,0:T(8,128)(2,1)S(1)}, bf16[256,128]{1,0:T(8,128)(2,1)S(1)}, u32[]{:S(2)}, u32[]{:S(2)}) %collective-permute-start.8) | collective-permute-done | bytes 65568 | tf_op jit(solution)/shard_map/ppermute | solution.py:252
  16.0 1.6 %collective-permute-start.9 = (bf16[256,128]{1,0:T(8,128)(2,1)S(1)}, bf16[256,128]{1,0:T(8,128)(2,1)S(1)}, u32[]{:S(2)}, u32[]{:S(2)}) collective-permute-start(bf16[256,128]{1,0:T(8,128)(2,1)S(1)} %fusion.2), channel_id=1, source_target_pairs={{0,2},{1,3},{2,0},{3,1},{4,6},{5,7},{6,4},{7,5},{8,10},{9,11},{10,... | collective-permute-start | bytes 196616 | tf_op jit(solution)/shard_map/ppermute | solution.py:252
  17.6 0.0 collective-permute-done.3
  17.7 1.6 %collective-permute-start.4 = (bf16[384,128]{1,0:T(8,128)(2,1)S(1)}, bf16[384,128]{1,0:T(8,128)(2,1)S(1)}, u32[]{:S(2)}, u32[]{:S(2)}) collective-permute-start(bf16[384,128]{1,0:T(8,128)(2,1)S(1)} %fusion.5), channel_id=1, source_target_pairs={{0,4},{1,5},{2,6},{3,7},{4,0},{5,1},{6,2},{7,3},{8,12},{9,13},{10,... | collective-permute-start | bytes 294920 | tf_op jit(solution)/shard_map/ppermute | solution.py:252
  19.3 1.1 %collective-permute-done.9 = bf16[256,128]{1,0:T(8,128)(2,1)S(1)} collective-permute-done((bf16[256,128]{1,0:T(8,128)(2,1)S(1)}, bf16[256,128]{1,0:T(8,128)(2,1)S(1)}, u32[]{:S(2)}, u32[]{:S(2)}) %collective-permute-start.9) | collective-permute-done | bytes 65568 | tf_op jit(solution)/shard_map/ppermute | solution.py:252
  20.4 1.6 %collective-permute-start.10 = (bf16[256,128]{1,0:T(8,128)(2,1)S(1)}, bf16[256,128]{1,0:T(8,128)(2,1)S(1)}, u32[]{:S(2)}, u32[]{:S(2)}) collective-permute-start(bf16[256,128]{1,0:T(8,128)(2,1)S(1)} %fusion.4), channel_id=1, source_target_pairs={{0,4},{1,5},{2,6},{3,7},{4,0},{5,1},{6,2},{7,3},{8,12},{9,13},{10,... | collective-permute-start | bytes 196616 | tf_op jit(solution)/shard_map/ppermute | solution.py:252
  22.0 0.7 %collective-permute-done.4 = bf16[384,128]{1,0:T(8,128)(2,1)S(1)} collective-permute-done((bf16[384,128]{1,0:T(8,128)(2,1)S(1)}, bf16[384,128]{1,0:T(8,128)(2,1)S(1)}, u32[]{:S(2)}, u32[]{:S(2)}) %collective-permute-start.4) | collective-permute-done | bytes 98336 | tf_op jit(solution)/shard_map/ppermute | solution.py:252
  22.7 0.1 fusion.1
  22.8 2.7 %collective-permute-start.5 = (bf16[384,128]{1,0:T(8,128)(2,1)S(1)}, bf16[384,128]{1,0:T(8,128)(2,1)S(1)}, u32[]{:S(2)}, u32[]{:S(2)}) collective-permute-start(bf16[384,128]{1,0:T(8,128)(2,1)S(1)} %fusion.1), channel_id=1, source_target_pairs={{0,8},{1,9},{2,10},{3,11},{4,12},{5,13},{6,14},{7,15},{8,0},{9,1},... | collective-permute-start | bytes 294920 | tf_op jit(solution)/shard_map/ppermute | solution.py:252
  25.5 0.2 collective-permute-done.10
  25.7 1.7 %collective-permute-start.11 = (bf16[256,128]{1,0:T(8,128)(2,1)S(1)}, bf16[256,128]{1,0:T(8,128)(2,1)S(1)}, u32[]{:S(2)}, u32[]{:S(2)}) collective-permute-start(bf16[256,128]{1,0:T(8,128)(2,1)S(1)} %fusion.3), channel_id=1, source_target_pairs={{0,8},{1,9},{2,10},{3,11},{4,12},{5,13},{6,14},{7,15},{8,0},{9,1},... | collective-permute-start | bytes 196616 | tf_op jit(solution)/shard_map/ppermute | solution.py:252
  27.4 2.7 %collective-permute-done.5 = bf16[384,128]{1,0:T(8,128)(2,1)S(1)} collective-permute-done((bf16[384,128]{1,0:T(8,128)(2,1)S(1)}, bf16[384,128]{1,0:T(8,128)(2,1)S(1)}, u32[]{:S(2)}, u32[]{:S(2)}) %collective-permute-start.5) | collective-permute-done | bytes 98336 | tf_op jit(solution)/shard_map/ppermute | solution.py:252
  30.1 0.1 convert_add_fusion.own_sum_ref
  30.2 0.1 collective-permute-start.6
  30.3 0.7 %collective-permute-done.11 = bf16[256,128]{1,0:T(8,128)(2,1)S(1)} collective-permute-done((bf16[256,128]{1,0:T(8,128)(2,1)S(1)}, bf16[256,128]{1,0:T(8,128)(2,1)S(1)}, u32[]{:S(2)}, u32[]{:S(2)}) %collective-permute-start.11) | collective-permute-done | bytes 65568 | tf_op jit(solution)/shard_map/ppermute | solution.py:252
  31.0 0.1 collective-permute-start.12
  31.1 0.5 %collective-permute-start.1 = (bf16[1]{0:T(256)(128)(2,1)}, bf16[1]{0:T(256)(128)(2,1)}, u32[]{:S(2)}, u32[]{:S(2)}) collective-permute-start(bf16[1]{0:T(256)(128)(2,1)} %param.7), channel_id=1, source_target_pairs={{0,16},{16,0},{1,17},{17,1},{2,18},{18,2},{3,19},{19,3},{4,20},{20... | collective-permute-start | bytes 14 | tf_op jit(solution)/shard_map/ppermute | solution.py:252
  32.2 0.0 copy-done.6
  32.3 0.3 collective-permute-done.1
  32.5 0.0 collective-permute-done.6.other_sum_ref
  32.5 0.0 collective-permute-done.12.other_cross_ref
  32.5 0.0 copy-done.1
  32.5 0.0 copy-done.3
  32.5 0.0 copy-done.4
  32.6 0.0 copy-done.5
  32.6 5.4 %gamma_and_virial.1 = (bf16[256,4096]{1,0:T(8,128)(2,1)}, f32[9,4096]{1,0:T(8,128)}) custom-call(s32[1,32]{1,0:T(1,128)S(1)} %copy-done.3, s32[1,32]{1,0:T(1,128)S(1)} %collective-permute-done.other_screen_ref, s32[1,32]{1,0:T(1,128)S(1)} %bitcast.10, f32[3,128]{1,0:T(4,128)S(1)} %copy-done.4, bf16[1,1]{1,0:T(2,128)(2,1)} %bitcast.5.energy_ref, ...), custom_call_target="tpu_custom_call" | custom-call | flops 1610612736 | bytes 6291456 | tf_op jit(solution)/shard_map/gamma_and_virial/pallas_call | solution.py:229
  (7 shorter events, 0.2 us)
Async XLA Ops:
  0.6 8.7 %collective-permute-start.7 = (bf16[256,4096]{1,0:T(8,128)(2,1)}, bf16[256,4096]{1,0:T(8,128)(2,1)S(1)}, u32[]{:S(2)}, u32[]{:S(2)}) collective-permute-start(bf16[256,4096]{1,0:T(8,128)(2,1)} %bitcast.6), channel_id=1, source_target_pairs={{0,16},{16,0},{1,17},{17,1},{2,18},{18,2},{3,19},{19,3},{4,20},{20... | collective-permute-start | bytes 6291464 | tf_op jit(solution)/shard_map/ppermute | solution.py:252
  1.1 1.6 %copy-start = (bf16[1,256,4096]{2,1,0:T(8,128)(2,1)S(1)}, bf16[1,256,4096]{2,1,0:T(8,128)(2,1)}, u32[]{:S(2)}) copy-start(bf16[1,256,4096]{2,1,0:T(8,128)(2,1)} %param.6) | copy-start | bytes 6291460
  2.7 0.7 %copy-start.2 = (s32[1,32]{1,0:T(1,128)S(1)}, s32[1,32]{1,0:T(1,128)}, u32[]{:S(2)}) copy-start(s32[1,32]{1,0:T(1,128)} %screen_ref.5) | copy-start | bytes 388
  5.6 6.4 %collective-permute-start.2 = (bf16[384,128]{1,0:T(8,128)(2,1)S(1)}, bf16[384,128]{1,0:T(8,128)(2,1)S(1)}, u32[]{:S(2)}, u32[]{:S(2)}) collective-permute-start(bf16[384,128]{1,0:T(8,128)(2,1)S(1)} %get-tuple-element.9), channel_id=1, source_target_pairs={{0,1},{1,0},{2,3},{3,2},{4,5},{5,4},{6,7},{7,6},{8,9},{9,8},{10,11... | collective-permute-start | bytes 294920 | tf_op jit(solution)/shard_map/ppermute | solution.py:252
  8.2 1.1 %collective-permute-start = (s32[1,32]{1,0:T(1,128)S(1)}, s32[1,32]{1,0:T(1,128)S(1)}, u32[]{:S(2)}, u32[]{:S(2)}) collective-permute-start(s32[1,32]{1,0:T(1,128)S(1)} %copy-done.2), channel_id=1, source_target_pairs={{0,16},{16,0},{1,17},{17,1},{2,18},{18,2},{3,19},{19,3},{4,20},{20... | collective-permute-start | bytes 392 | tf_op jit(solution)/shard_map/ppermute | solution.py:252
  11.6 20.6 %copy-start.6 = (bf16[256]{0:T(256)(128)(2,1)S(1)}, bf16[256]{0:T(256)(128)(2,1)}, u32[]{:S(2)}) copy-start(bf16[256]{0:T(256)(128)(2,1)} %param.8) | copy-start | bytes 1540
  11.6 20.9 %copy-start.1 = (bf16[1,256,4096]{2,1,0:T(8,128)(2,1)S(1)}, bf16[1,256,4096]{2,1,0:T(8,128)(2,1)}, u32[]{:S(2)}) copy-start(bf16[1,256,4096]{2,1,0:T(8,128)(2,1)} %param.6) | copy-start | bytes 6291460
  11.6 20.9 %copy-start.3 = (s32[1,32]{1,0:T(1,128)S(1)}, s32[1,32]{1,0:T(1,128)}, u32[]{:S(2)}) copy-start(s32[1,32]{1,0:T(1,128)} %screen_ref.5) | copy-start | bytes 388
  11.7 20.9 %copy-start.4 = (f32[3,128]{1,0:T(4,128)S(1)}, f32[3,128]{1,0:T(4,128)}, u32[]{:S(2)}) copy-start(f32[3,128]{1,0:T(4,128)} %positions_ref.1) | copy-start | bytes 4612
  11.7 20.9 %copy-start.5 = (s32[32]{0:T(128)S(1)}, s32[32]{0:T(128)}, u32[]{:S(2)}) copy-start(s32[32]{0:T(128)} %param.10) | copy-start | bytes 388
  11.7 4.3 %collective-permute-start.8 = (bf16[256,128]{1,0:T(8,128)(2,1)S(1)}, bf16[256,128]{1,0:T(8,128)(2,1)S(1)}, u32[]{:S(2)}, u32[]{:S(2)}) collective-permute-start(bf16[256,128]{1,0:T(8,128)(2,1)S(1)} %get-tuple-element.11), channel_id=1, source_target_pairs={{0,1},{1,0},{2,3},{3,2},{4,5},{5,4},{6,7},{7,6},{8,9},{9,8},{10,11... | collective-permute-start | bytes 196616 | tf_op jit(solution)/shard_map/ppermute | solution.py:252
  12.0 5.6 %collective-permute-start.3 = (bf16[384,128]{1,0:T(8,128)(2,1)S(1)}, bf16[384,128]{1,0:T(8,128)(2,1)S(1)}, u32[]{:S(2)}, u32[]{:S(2)}) collective-permute-start(bf16[384,128]{1,0:T(8,128)(2,1)S(1)} %fusion), channel_id=1, source_target_pairs={{0,2},{1,3},{2,0},{3,1},{4,6},{5,7},{6,4},{7,5},{8,10},{9,11},{10,... | collective-permute-start | bytes 294920 | tf_op jit(solution)/shard_map/ppermute | solution.py:252
  16.0 4.3 %collective-permute-start.9 = (bf16[256,128]{1,0:T(8,128)(2,1)S(1)}, bf16[256,128]{1,0:T(8,128)(2,1)S(1)}, u32[]{:S(2)}, u32[]{:S(2)}) collective-permute-start(bf16[256,128]{1,0:T(8,128)(2,1)S(1)} %fusion.2), channel_id=1, source_target_pairs={{0,2},{1,3},{2,0},{3,1},{4,6},{5,7},{6,4},{7,5},{8,10},{9,11},{10,... | collective-permute-start | bytes 196616 | tf_op jit(solution)/shard_map/ppermute | solution.py:252
  17.7 5.1 %collective-permute-start.4 = (bf16[384,128]{1,0:T(8,128)(2,1)S(1)}, bf16[384,128]{1,0:T(8,128)(2,1)S(1)}, u32[]{:S(2)}, u32[]{:S(2)}) collective-permute-start(bf16[384,128]{1,0:T(8,128)(2,1)S(1)} %fusion.5), channel_id=1, source_target_pairs={{0,4},{1,5},{2,6},{3,7},{4,0},{5,1},{6,2},{7,3},{8,12},{9,13},{10,... | collective-permute-start | bytes 294920 | tf_op jit(solution)/shard_map/ppermute | solution.py:252
  20.4 5.3 %collective-permute-start.10 = (bf16[256,128]{1,0:T(8,128)(2,1)S(1)}, bf16[256,128]{1,0:T(8,128)(2,1)S(1)}, u32[]{:S(2)}, u32[]{:S(2)}) collective-permute-start(bf16[256,128]{1,0:T(8,128)(2,1)S(1)} %fusion.4), channel_id=1, source_target_pairs={{0,4},{1,5},{2,6},{3,7},{4,0},{5,1},{6,2},{7,3},{8,12},{9,13},{10,... | collective-permute-start | bytes 196616 | tf_op jit(solution)/shard_map/ppermute | solution.py:252
  22.8 7.3 %collective-permute-start.5 = (bf16[384,128]{1,0:T(8,128)(2,1)S(1)}, bf16[384,128]{1,0:T(8,128)(2,1)S(1)}, u32[]{:S(2)}, u32[]{:S(2)}) collective-permute-start(bf16[384,128]{1,0:T(8,128)(2,1)S(1)} %fusion.1), channel_id=1, source_target_pairs={{0,8},{1,9},{2,10},{3,11},{4,12},{5,13},{6,14},{7,15},{8,0},{9,1},... | collective-permute-start | bytes 294920 | tf_op jit(solution)/shard_map/ppermute | solution.py:252
  25.7 5.2 %collective-permute-start.11 = (bf16[256,128]{1,0:T(8,128)(2,1)S(1)}, bf16[256,128]{1,0:T(8,128)(2,1)S(1)}, u32[]{:S(2)}, u32[]{:S(2)}) collective-permute-start(bf16[256,128]{1,0:T(8,128)(2,1)S(1)} %fusion.3), channel_id=1, source_target_pairs={{0,8},{1,9},{2,10},{3,11},{4,12},{5,13},{6,14},{7,15},{8,0},{9,1},... | collective-permute-start | bytes 196616 | tf_op jit(solution)/shard_map/ppermute | solution.py:252
  30.2 2.3 %collective-permute-start.6 = (f32[384,128]{1,0:T(8,128)S(1)}, f32[384,128]{1,0:T(8,128)S(1)}, u32[]{:S(2)}, u32[]{:S(2)}) collective-permute-start(f32[384,128]{1,0:T(8,128)S(1)} %convert_add_fusion.own_sum_ref), channel_id=1, source_target_pairs={{0,16},{16,0},{1,17},{17,1},{2,18},{18,2},{3,19},{19,3},{4,20},{20... | collective-permute-start | bytes 589832 | tf_op jit(solution)/shard_map/ppermute | solution.py:252
  31.0 1.5 %collective-permute-start.12 = (f32[256,128]{1,0:T(8,128)S(1)}, f32[256,128]{1,0:T(8,128)S(1)}, u32[]{:S(2)}, u32[]{:S(2)}) collective-permute-start(f32[256,128]{1,0:T(8,128)S(1)} %convert_add_fusion.4.cross_sum_ref), channel_id=1, source_target_pairs={{0,16},{16,0},{1,17},{17,1},{2,18},{18,2},{3,19},{19,3},{4,20},{20... | collective-permute-start | bytes 393224 | tf_op jit(solution)/shard_map/ppermute | solution.py:252
  31.1 1.5 %collective-permute-start.1 = (bf16[1]{0:T(256)(128)(2,1)}, bf16[1]{0:T(256)(128)(2,1)}, u32[]{:S(2)}, u32[]{:S(2)}) collective-permute-start(bf16[1]{0:T(256)(128)(2,1)} %param.7), channel_id=1, source_target_pairs={{0,16},{16,0},{1,17},{17,1},{2,18},{18,2},{3,19},{19,3},{4,20},{20... | collective-permute-start | bytes 14 | tf_op jit(solution)/shard_map/ppermute | solution.py:252

commit v2 on v0

v2 whole, which is shorter than its diff:
```python
import functools

import jax
import jax.numpy as jnp
from jax import lax
from jax.experimental import pallas as pl
from jax.experimental.pallas import tpu as pltpu
from jax.sharding import PartitionSpec as P

F32 = jnp.float32
BF16 = jnp.bfloat16
CONTRACT_LAST = (((1,), (1,)), ((), ()))
SMEM = pltpu.MemorySpace.SMEM
VMEM = pltpu.MemorySpace.VMEM
PAD = 16


def mask_row(screen, first, count, width):
    values = screen.astype(F32)
    pieces = [
        jnp.broadcast_to(values[:, k : k + 1], (1, width)) for k in range(first, first + count)
    ]
    return jnp.concatenate(pieces, axis=1).astype(BF16)


def split(aux_dev, blocks, wanted):
    steps = wanted if blocks % wanted == 0 else 1
    return steps, aux_dev // steps, blocks // steps


def triangle(size):
    return (lax.broadcasted_iota(jnp.int32, (size, size), axis) for axis in (0, 1))


def own_pairs_kernel(
    blocks, width, screen_hbm, own_hbm, own_ref, sum_ref, send_ref, total, screen, own_sem, screen_sem
):
    half = total.shape[0] // 2
    screen_copy = pltpu.make_async_copy(screen_hbm, screen, screen_sem)
    own_copy = pltpu.make_async_copy(own_hbm, own_ref, own_sem)
    screen_copy.start()
    own_copy.start()
    screen_copy.wait()
    mask = mask_row(screen[...], 0, blocks, width)
    own_copy.wait()
    own = own_ref[...]
    total[...] = lax.dot_general(own * mask, own, CONTRACT_LAST, preferred_element_type=F32)
    low, high = pl.ds(0, half), pl.ds(half, half)
    row, col = triangle(half)
    first, last = total[low, low], total[high, high]
    diagonal = jnp.sum(jnp.where(row == col, last, 0.0), axis=0, keepdims=True)
    parts = (
        total[high, low],
        jnp.where(row >= col, first, last),
        jnp.broadcast_to(diagonal, (PAD, half)),
    )
    start = 0
    for part in parts:
        rows = pl.ds(start, part.shape[0])
        sum_ref[rows, :] = part
        send_ref[rows, :] = part.astype(BF16)
        start += part.shape[0]


def cross_pairs_kernel(
    blocks, width, screen_ref, other_screen_ref, own_ref, other_ref, sum_ref, send_ref, total
):
    half = total.shape[0] // 2
    core = lax.axis_index("occ")
    mask = mask_row(screen_ref[...] * other_screen_ref[...], 0, blocks, width)
    total[...] = lax.dot_general(
        own_ref[...], other_ref[...] * mask, CONTRACT_LAST, preferred_element_type=F32
    )
    for place in range(2):
        rows = pl.ds(place * half, half)
        straight = total[rows, pl.ds(place * half, half)]
        across = total[rows, pl.ds((1 - place) * half, half)]
        part = jnp.where(core == 0, straight, across)
        sum_ref[rows, :] = part
        send_ref[rows, :] = part.astype(BF16)


def in_hbm(array):
    return pltpu.with_memory_space_constraint(array, pltpu.HBM)


def own_pairs(own, screen):
    virt, aux_dev = own.shape
    blocks = screen.shape[1]
    half = virt // 2
    hbm = pl.BlockSpec(memory_space=pltpu.HBM)
    return pl.pallas_call(
        functools.partial(own_pairs_kernel, blocks, aux_dev // blocks),
        in_specs=[hbm, hbm],
        out_specs=[pl.BlockSpec(memory_space=VMEM)] * 3,
        out_shape=[
            jax.ShapeDtypeStruct((virt, aux_dev), BF16),
            jax.ShapeDtypeStruct((2 * half + PAD, half), F32),
            jax.ShapeDtypeStruct((2 * half + PAD, half), BF16),
        ],
        scratch_shapes=[
            pltpu.VMEM((virt, virt), F32),
            pltpu.VMEM((1, blocks), jnp.int32),
            pltpu.SemaphoreType.DMA,
            pltpu.SemaphoreType.DMA,
        ],
        compiler_params=pltpu.CompilerParams(vmem_limit_bytes=8 << 20),
        cost_estimate=pl.CostEstimate(
            flops=2 * virt * virt * aux_dev, bytes_accessed=2 * virt * aux_dev, transcendentals=0
        ),
        name="own_pairs",
    )(in_hbm(screen), in_hbm(own))


def cross_pairs(own, other, screen, other_screen):
    virt, aux_dev = own.shape
    blocks = other_screen.shape[1]
    half = virt // 2
    vmem = pl.BlockSpec(memory_space=VMEM)
    return pl.pallas_call(
        functools.partial(cross_pairs_kernel, blocks, aux_dev // blocks),
        in_specs=[vmem] * 4,
        out_specs=[vmem] * 2,
        out_shape=[
            jax.ShapeDtypeStruct((2 * half, half), F32),
            jax.ShapeDtypeStruct((2 * half, half), BF16),
        ],
        scratch_shapes=[pltpu.VMEM((virt, virt), F32)],
        compiler_params=pltpu.CompilerParams(vmem_limit_bytes=8 << 20),
        cost_estimate=pl.CostEstimate(
            flops=2 * virt * virt * aux_dev, bytes_accessed=4 * virt * aux_dev, transcendentals=0
        ),
        name="cross_pairs",
    )(screen, other_screen, own, other)


def symmetric(packed):
    half = packed.shape[1]
    row, col = triangle(half)
    low, both = packed[0:half, :], packed[half : 2 * half, :]
    turned = both.T
    first = jnp.where(row >= col, both, turned)
    last = jnp.where(row < col, both, turned)
    last = jnp.where(row == col, packed[2 * half : 2 * half + 1, :], last)
    top = jnp.concatenate([first, low.T], axis=1)
    return jnp.concatenate([top, jnp.concatenate([low, last], axis=1)], axis=0)


def tables_kernel(
    width, owner_ref, positions_ref, energy_ref, other_energy_ref, virt_ref,
    screen_ref, other_screen_ref, own_ref, other_ref, cross_ref, factor_ref, mask_ref,
):
    virt = own_ref.shape[0]
    virt_row = jnp.broadcast_to(virt_ref[...].astype(F32), (virt, virt))
    virt_col = virt_row.T
    energy = energy_ref[...].astype(F32)
    other_energy = other_energy_ref[...].astype(F32)
    own_row, own_col = virt_row - energy, virt_col - energy
    other_row, other_col = virt_row - other_energy, virt_col - other_energy
    own_ref[...] = 1.0 / (own_col + own_row)
    other_ref[...] = 1.0 / (other_col + other_row)
    cross_ref[...] = 1.0 / (own_col + other_row)
    blocks = owner_ref.shape[1]
    mask_ref[0:1, :] = mask_row(screen_ref[...], 0, blocks, width).astype(F32)
    mask_ref[1:2, :] = mask_row(other_screen_ref[...], 0, blocks, width).astype(F32)
    for block in range(blocks):
        where = [positions_ref[c, owner_ref[0, block]] for c in range(3)]
        rows = [
            jnp.full((1, width), where[c] * where[d], F32) for c in range(3) for d in range(3)
        ]
        factor_ref[:, block * width : (block + 1) * width] = jnp.concatenate(rows, axis=0)


def make_tables(width, owner, positions, energy, other_energy, virt_energy, screen, other_screen):
    virt, blocks = virt_energy.shape[0], owner.shape[0]
    smem = pl.BlockSpec(memory_space=SMEM)
    vmem = pl.BlockSpec(memory_space=VMEM)
    return pl.pallas_call(
        functools.partial(tables_kernel, width),
        in_specs=[smem] * 2 + [vmem] * 5,
        out_specs=[vmem] * 5,
        out_shape=[jax.ShapeDtypeStruct((virt, virt), F32)] * 3
        + [jax.ShapeDtypeStruct((rows, blocks * width), F32) for rows in (9, 2)],
        compiler_params=pltpu.CompilerParams(vmem_limit_bytes=4 << 20),
        cost_estimate=pl.CostEstimate(
            flops=16 * virt * virt, bytes_accessed=12 * virt * virt, transcendentals=0
        ),
        name="tables",
    )(
        owner.reshape(1, -1), positions,
        energy.reshape(1, 1), other_energy.reshape(1, 1), virt_energy.reshape(1, -1),
        screen, other_screen,
    )


def gamma_kernel(
    steps, own_ref, other_ref, own_inverse_ref, other_inverse_ref, cross_inverse_ref, factor_ref, mask_ref,
    own_sum_ref, other_sum_ref, cross_sum_ref, other_cross_ref,
    gamma_hbm, virial_hbm, gamma_ref, virial_ref, amps, sems, virial_sem,
):
    virt, aux_dev = own_ref.shape
    half, tile = virt // 2, aux_dev // steps
    mine = [cross_sum_ref[pl.ds(k * half, half), :] for k in range(2)]
    theirs = [other_cross_ref[pl.ds(k * half, half), :].T for k in range(2)]
    even = lax.axis_index("occ") == 0
    top = [jnp.where(even, mine[0], theirs[0]), jnp.where(even, theirs[1], mine[0])]
    bottom = [jnp.where(even, theirs[0], mine[1]), jnp.where(even, mine[1], theirs[1])]
    cross = jnp.concatenate(
        [jnp.concatenate(top, axis=1), jnp.concatenate(bottom, axis=1)], axis=0
    )
    own_amps, cross_amps, other_amps = (pl.ds(k * virt, virt) for k in range(3))
    amps[:, own_amps] = (symmetric(own_sum_ref[...]) * own_inverse_ref[...]).astype(BF16)
    amps[:, cross_amps] = (cross * cross_inverse_ref[...]).astype(BF16)
    amps[:, other_amps] = (symmetric(other_sum_ref[...]) * other_inverse_ref[...]).astype(BF16)
    copies = []
    for step in range(steps):
        columns = pl.ds(step * tile, tile)
        mask = mask_ref[:, columns].astype(BF16)
        own, other = own_ref[:, columns] * mask[0:1, :], other_ref[:, columns] * mask[1:2, :]
        cross_part = jnp.dot(amps[:, cross_amps], other, preferred_element_type=F32)
        gamma = jnp.dot(amps[:, own_amps], own, preferred_element_type=F32) + cross_part
        gamma_ref[:, columns] = gamma.astype(BF16)
        copies.append(
            pltpu.make_async_copy(
                gamma_ref.at[:, columns], gamma_hbm.at[:, columns], sems.at[step]
            )
        )
        copies[step].start()
        other_part = jnp.dot(amps[:, other_amps], other, preferred_element_type=F32)
        weight = jnp.sum(
            (gamma + cross_part) * own.astype(F32) + other_part * other.astype(F32),
            axis=0,
            keepdims=True,
        )
        virial_ref[:, columns] = factor_ref[:, columns] * weight
    copies.append(pltpu.make_async_copy(virial_ref, virial_hbm, virial_sem))
    copies[steps].start()
    for copy in copies:
        copy.wait()


def gamma_and_virial(own, other, tables, sums):
    virt, aux_dev = own.shape
    steps = 8 if aux_dev % 1024 == 0 else 1
    vmem = pl.BlockSpec(memory_space=VMEM)
    hbm = pl.BlockSpec(memory_space=pltpu.HBM)
    return pl.pallas_call(
        functools.partial(gamma_kernel, steps),
        in_specs=[vmem] * 11,
        out_specs=[hbm, hbm],
        out_shape=[
            jax.ShapeDtypeStruct((virt, aux_dev), BF16),
            jax.ShapeDtypeStruct((9, aux_dev), F32),
        ],
        scratch_shapes=[
            pltpu.VMEM((virt, aux_dev), BF16),
            pltpu.VMEM((9, aux_dev), F32),
            pltpu.VMEM((virt, 3 * virt), BF16),
            pltpu.SemaphoreType.DMA((steps,)),
            pltpu.SemaphoreType.DMA,
        ],
        compiler_params=pltpu.CompilerParams(vmem_limit_bytes=8 << 20),
        cost_estimate=pl.CostEstimate(
            flops=6 * virt * virt * aux_dev, bytes_accessed=6 * virt * aux_dev, transcendentals=0
        ),
        name="gamma_and_virial",
    )(own, other, *tables, *sums)


def swap(array, axis, size, bit):
    return lax.ppermute(array, axis, [(i, i ^ bit) for i in range(size)])


def swap_by_core(array, n_aux, bits):
    pairs = [
        (core * n_aux + i, core * n_aux + (i ^ bit))
        for core, bit in enumerate(bits)
        for i in range(n_aux)
    ]
    return lax.ppermute(array, ("occ", "aux"), pairs)


def sum_over_aux(total, send, n_aux, orders, beside=()):
    steps = list(zip(*orders))
    for step, bits in enumerate(steps):
        if step == len(steps) - 1 and beside:
            send, beside = lax.optimization_barrier((send, beside))
        total = total + swap_by_core(send, n_aux, bits).astype(F32)
        send = total.astype(BF16)
    return total, beside


def orders_of(bits):
    turned = [bits[k ^ 1] if k ^ 1 < len(bits) else bits[k] for k in range(len(bits))]
    half = len(bits) // 2
    high = bits[half:][::-1]
    return (bits, turned), (high + bits[:half], high + turned[:half])


def two_occ_body(n_aux, coeffs, occ_energy, virt_energy, screen, owner, positions):
    raw = coeffs[0]
    other = swap(raw, "occ", 2, 1)
    other_screen = swap(screen, "occ", 2, 1)
    other_energy = swap(occ_energy, "occ", 2, 1)
    cross_orders, own_orders = orders_of([1 << k for k in range(n_aux.bit_length() - 1)])
    own, own_sum, own_send = own_pairs(raw, screen)
    own_send, other_screen, other_energy = lax.optimization_barrier(
        (own_send, other_screen, other_energy)
    )
    cross_sum, cross_send = cross_pairs(own, other, screen, other_screen)
    own_sum, late = sum_over_aux(
        own_sum, own_send, n_aux, own_orders, (virt_energy, screen, other_screen, other_energy)
    )
    width = coeffs.shape[2] // screen.shape[1]
    late_virt, late_screen, late_other_screen, late_other_energy = late
    tables = make_tables(
        width, owner, positions, occ_energy, late_other_energy, late_virt, late_screen,
        late_other_screen,
    )
    own_sum, tables = lax.optimization_barrier((own_sum, tables))
    cross_sum, _ = sum_over_aux(cross_sum, cross_send, n_aux, cross_orders)
    other_sum = swap(own_sum, "occ", 2, 1)
    other_cross = swap(cross_sum, "occ", 2, 1)
    gamma, virial = gamma_and_virial(
        own, other, tables, (own_sum, other_sum, cross_sum, other_cross)
    )
    return gamma[None], virial


def general_body(n_aux, coeffs, occ_energy, virt_energy, screen, owner, positions):
    occ_dev, virt, aux_dev = coeffs.shape
    width = aux_dev // screen.shape[1]
    column_mask = jnp.repeat(screen[0], width).astype(BF16)
    masked = coeffs * column_mask[None, None, :]
    whole = lax.all_gather(masked, "occ", axis=0, tiled=True)
    energies = lax.all_gather(occ_energy, "occ", axis=0, tiled=True)
    all_rows = whole.reshape(-1, aux_dev)
    local = masked.reshape(-1, aux_dev)
    virt_f = virt_energy.astype(F32)
    spread_local = (virt_f[None, :] - occ_energy.astype(F32)[:, None]).reshape(-1)
    spread_all = (virt_f[None, :] - energies.astype(F32)[:, None]).reshape(-1)
    pairs = lax.dot_general(all_rows, local, CONTRACT_LAST, preferred_element_type=F32)
    if n_aux & (n_aux - 1):
        summed = lax.psum(pairs, "aux")
    else:
        bits = [1 << k for k in range(n_aux.bit_length() - 1)]
        summed, send = pairs, pairs.astype(BF16)
        for bit in bits:
            summed = summed + swap(send, "aux", n_aux, bit).astype(F32)
            send = summed.astype(BF16)
    amps = (summed / (spread_all[:, None] + spread_local[None, :])).astype(BF16)
    gamma = lax.dot_general(
        amps, all_rows, (((0,), (0,)), ((), ())), preferred_element_type=F32
    ).astype(BF16)
    partial_weight = jnp.sum(gamma.astype(F32) * local.astype(F32), axis=0)
    weight = lax.psum(partial_weight, "occ")
    where = jnp.repeat(positions[:, owner], width, axis=1)
    virial = (where[:, None, :] * where[None, :, :]).reshape(9, aux_dev) * weight[None, :]
    return gamma.reshape(occ_dev, virt, aux_dev), virial


def solution(mesh):
    placed = (P("occ", None, "aux"), P("occ"), P(), P("occ", "aux"), P("aux"), P())
    n_occ, n_aux = mesh.shape["occ"], mesh.shape["aux"]
    power_of_two = n_aux & (n_aux - 1) == 0

    def body(coeffs, *rest):
        fits = n_occ == 2 and coeffs.shape[0] == 1 and power_of_two
        chosen = two_occ_body if fits else general_body
        return chosen(n_aux, coeffs, *rest)

    return jax.shard_map(
        body,
        mesh=mesh,
        in_specs=placed,
        out_specs=(P("occ", None, "aux"), P(None, "aux")),
        check_vma=False,
    )
```

time: 159 us -> 35.8 us (0.23)
  waiting for transfers between devices: 121 us -> 9.92 us
  starting transfers between devices: 0.08 us -> 16.3 us
  between operations: 14.8 us -> 1.44 us
  matrix products: 10.6 us -> 0 us
  Pallas kernels: 0 us -> 7.67 us
  blocking collectives: 5.82 us -> 0 us
  other arithmetic: 4.57 us -> 0.27 us
  local copies, waits for them, and re-layouts: 1.65 us -> 0.03 us
    psum x1 -> x0, waiting for transfers between devices: 107 us -> none  [body(): lax.psum(lax.dot_general(all_rows, local, contract_last, preferred_elemen...]
    ppermute x0 -> x13, starting transfers between devices: none -> 16.3 us  [the longest x8 15.1 us: swap_by_core(): return lax.ppermute(array, ('occ', 'aux'), pairs)]
    all_gather x1 -> x0, waiting for transfers between devices: 14.2 us -> none  [body(): lax.all_gather(masked, 'occ', axis=0, tiled=True)]
    dot_general x3 -> x0, matrix products: 10.6 us -> none  [the longest x1 5.29 us: body(): lax.dot_general(amps, all_rows, contract_first, preferred_element_type=jn...]
    ppermute x0 -> x13, waiting for transfers between devices: none -> 9.92 us  [the longest x8 7.43 us: swap_by_core(): return lax.ppermute(array, ('occ', 'aux'), pairs)]
    pallas_call x0 -> x4, Pallas kernels: none -> 7.67 us  [the longest x1 3.02 us: gamma_and_virial(): pl.pallas_call(functools.partial(gamma_kernel, steps), in_specs=[vmem] *...]
    mul x3 -> x0, other arithmetic: 3.82 us -> none  [the longest x1 3.05 us: body(): masked = coeffs * column_mask[None, None, :]]
    psum x1 -> x0, blocking collectives: 3.35 us -> none  [body(): weight = lax.psum(partial_weight, 'occ')]
  transfers between devices with their start and end apart: 2 -> 13, of which waited for: 2 -> 8; matrix products, arithmetic and copies ran while one was open for 1% -> 1% of each run, Pallas kernels for 0% -> 13%
where the time goes in v2:
time: 35.8 us; the launch traced here: 35.6 us
  starting transfers between devices  16.3 us (46%)
  waiting for transfers between devices  9.92 us (28%)
  Pallas kernels  7.67 us (21%)
  between operations  1.44 us (4%)
    ppermute x8, starting transfers between devices, swap_by_core(): return lax.ppermute(array, ('occ', 'aux'), pairs)  15.1 us
    ppermute x8, waiting for transfers between devices, swap_by_core(): return lax.ppermute(array, ('occ', 'aux'), pairs)  7.43 us
    pallas_call x1, Pallas kernels, gamma_and_virial(): pl.pallas_call(functools.partial(gamma_kernel, steps), in_specs=[vmem] *...  3.02 us
    ppermute x5, waiting for transfers between devices, swap(): return lax.ppermute(array, axis, [(i, i ^ bit) for i in range(size)])  2.49 us
    pallas_call x1, Pallas kernels, own_pairs(): pl.pallas_call(functools.partial(own_pairs_kernel, blocks, aux_dev // blo...  2.38 us
    pallas_call x1, Pallas kernels, make_tables(): pl.pallas_call(functools.partial(tables_kernel, width), in_specs=[smem] *...  1.45 us
    ppermute x5, starting transfers between devices, swap(): return lax.ppermute(array, axis, [(i, i ^ bit) for i in range(size)])  1.17 us
    pallas_call x1, Pallas kernels, cross_pairs(): pl.pallas_call(functools.partial(cross_pairs_kernel, blocks, aux_dev // b...  0.82 us
  transfers between devices with their start and end apart: 13, of which 8 were waited for; matrix products, arithmetic and copies ran while one was open for 1% of the time, Pallas kernels for 13%

profile of v2, /device:TPU:0, one launch (start us, length us, event | category | flops | bytes accessed | tf_op | source)
XLA Modules:
  0.0 35.6 jit_solution(3745282650311447997)
XLA Ops:
  0.6 0.0 copy-start
  0.6 0.5 %collective-permute-start = (bf16[256,4096]{1,0:T(8,128)(2,1)}, bf16[256,4096]{1,0:T(8,128)(2,1)S(1)}, u32[]{:S(2)}, u32[]{:S(2)}) collective-permute-start(bf16[256,4096]{1,0:T(8,128)(2,1)} %bitcast.7), channel_id=1, source_target_pairs={{0,16},{16,0},{1,17},{17,1},{2,18},{18,2},{3,19},{19,3},{4,20},{20... | collective-permute-start | bytes 6291464 | tf_op jit(solution)/shard_map/ppermute | solution.py:271
  1.2 0.1 collective-permute-start.1
  1.2 0.4 %collective-permute-start.2 = (bf16[1]{0:T(256)(128)(2,1)}, bf16[1]{0:T(256)(128)(2,1)}, u32[]{:S(2)}, u32[]{:S(2)}) collective-permute-start(bf16[1]{0:T(256)(128)(2,1)} %param.7), channel_id=1, source_target_pairs={{0,16},{16,0},{1,17},{17,1},{2,18},{18,2},{3,19},{19,3},{4,20},{20... | collective-permute-start | bytes 14 | tf_op jit(solution)/shard_map/ppermute | solution.py:271
  1.7 2.4 %own_pairs.1 = (bf16[256,4096]{1,0:T(8,128)(2,1)S(1)}, f32[272,128]{1,0:T(8,128)S(1)}, bf16[272,128]{1,0:T(8,128)(2,1)S(1)}) custom-call(s32[1,32]{1,0:T(1,128)} %screen_ref.2, bf16[256,4096]{1,0:T(8,128)(2,1)} %bitcast.8), custom_call_target="tpu_custom_call" | custom-call | flops 536870912 | bytes 2097152 | tf_op jit(solution)/shard_map/own_pairs/pallas_call | solution.py:92
  4.1 1.2 %collective-permute-done.2 = bf16[1]{0:T(256)(128)(2,1)} collective-permute-done((bf16[1]{0:T(256)(128)(2,1)}, bf16[1]{0:T(256)(128)(2,1)}, u32[]{:S(2)}, u32[]{:S(2)}) %collective-permute-start.2) | collective-permute-done | bytes 34 | tf_op jit(solution)/shard_map/ppermute | solution.py:271
  5.2 0.0 collective-permute-done.1.other_screen_ref
  5.2 3.9 %collective-permute-start.3 = (bf16[272,128]{1,0:T(8,128)(2,1)S(1)}, bf16[272,128]{1,0:T(8,128)(2,1)S(1)}, u32[]{:S(2)}, u32[]{:S(2)}) collective-permute-start(bf16[272,128]{1,0:T(8,128)(2,1)S(1)} %get-tuple-element.31), channel_id=1, source_target_pairs={{0,8},{1,9},{2,10},{3,11},{4,12},{5,13},{6,14},{7,15},{8,0},{9,1},... | collective-permute-start | bytes 208904 | tf_op jit(solution)/shard_map/ppermute | solution.py:280
  9.8 0.0 collective-permute-done.other_ref
  9.8 0.0 copy-done
  9.8 0.0 copy-start.3
  9.8 0.0 copy-start.1
  9.8 0.0 copy-start.2
  9.8 0.8 %cross_pairs.1 = (f32[256,128]{1,0:T(8,128)S(1)}, bf16[256,128]{1,0:T(8,128)(2,1)S(1)}) custom-call(s32[1,32]{1,0:T(1,128)S(1)} %copy-done, s32[1,32]{1,0:T(1,128)S(1)} %collective-permute-done.1.other_screen_ref, bf16[256,4096]{1,0:T(8,128)(2,1)S(1)} %get-tuple-element.28.own_ref, bf16[256,4096]{1,0:T(8,128)(2,1)S(1)} %collective-permute-done.other_ref), custom_call_target="tpu_custom_call" | custom-call | flops 536870912 | bytes 4194304 | tf_op jit(solution)/shard_map/cross_pairs/pallas_call | solution.py:120
  10.7 1.6 %collective-permute-start.8 = (bf16[256,128]{1,0:T(8,128)(2,1)S(1)}, bf16[256,128]{1,0:T(8,128)(2,1)S(1)}, u32[]{:S(2)}, u32[]{:S(2)}) collective-permute-start(bf16[256,128]{1,0:T(8,128)(2,1)S(1)} %get-tuple-element.51), channel_id=1, source_target_pairs={{0,1},{1,0},{2,3},{3,2},{4,5},{5,4},{6,7},{7,6},{8,9},{9,8},{10,11... | collective-permute-start | bytes 196616 | tf_op jit(solution)/shard_map/ppermute | solution.py:280
  12.2 0.9 %collective-permute-done.3 = bf16[272,128]{1,0:T(8,128)(2,1)S(1)} collective-permute-done((bf16[272,128]{1,0:T(8,128)(2,1)S(1)}, bf16[272,128]{1,0:T(8,128)(2,1)S(1)}, u32[]{:S(2)}, u32[]{:S(2)}) %collective-permute-start.3) | collective-permute-done | bytes 69664 | tf_op jit(solution)/shard_map/ppermute | solution.py:280
  13.2 0.8 %collective-permute-start.4 = (bf16[272,128]{1,0:T(8,128)(2,1)S(1)}, bf16[272,128]{1,0:T(8,128)(2,1)S(1)}, u32[]{:S(2)}, u32[]{:S(2)}) collective-permute-start(bf16[272,128]{1,0:T(8,128)(2,1)S(1)} %fusion), channel_id=1, source_target_pairs={{0,4},{1,5},{2,6},{3,7},{4,0},{5,1},{6,2},{7,3},{8,12},{9,13},{10,... | collective-permute-start | bytes 208904 | tf_op jit(solution)/shard_map/ppermute | solution.py:280
  14.0 1.0 %collective-permute-done.8 = bf16[256,128]{1,0:T(8,128)(2,1)S(1)} collective-permute-done((bf16[256,128]{1,0:T(8,128)(2,1)S(1)}, bf16[256,128]{1,0:T(8,128)(2,1)S(1)}, u32[]{:S(2)}, u32[]{:S(2)}) %collective-permute-start.8) | collective-permute-done | bytes 65568 | tf_op jit(solution)/shard_map/ppermute | solution.py:280
  15.0 1.6 %collective-permute-start.9 = (bf16[256,128]{1,0:T(8,128)(2,1)S(1)}, bf16[256,128]{1,0:T(8,128)(2,1)S(1)}, u32[]{:S(2)}, u32[]{:S(2)}) collective-permute-start(bf16[256,128]{1,0:T(8,128)(2,1)S(1)} %fusion.2), channel_id=1, source_target_pairs={{0,2},{1,3},{2,0},{3,1},{4,6},{5,7},{6,4},{7,5},{8,10},{9,11},{10,... | collective-permute-start | bytes 196616 | tf_op jit(solution)/shard_map/ppermute | solution.py:280
  16.6 0.9 %collective-permute-done.4 = bf16[272,128]{1,0:T(8,128)(2,1)S(1)} collective-permute-done((bf16[272,128]{1,0:T(8,128)(2,1)S(1)}, bf16[272,128]{1,0:T(8,128)(2,1)S(1)}, u32[]{:S(2)}, u32[]{:S(2)}) %collective-permute-start.4) | collective-permute-done | bytes 69664 | tf_op jit(solution)/shard_map/ppermute | solution.py:280
  17.6 1.7 %collective-permute-start.5 = (bf16[272,128]{1,0:T(8,128)(2,1)S(1)}, bf16[272,128]{1,0:T(8,128)(2,1)S(1)}, u32[]{:S(2)}, u32[]{:S(2)}) collective-permute-start(bf16[272,128]{1,0:T(8,128)(2,1)S(1)} %fusion.5), channel_id=1, source_target_pairs={{0,1},{1,0},{2,3},{3,2},{4,5},{5,4},{6,7},{7,6},{8,9},{9,8},{10,11... | collective-permute-start | bytes 208904 | tf_op jit(solution)/shard_map/ppermute | solution.py:280
  19.2 0.3 collective-permute-done.9
  19.6 1.8 %collective-permute-start.10 = (bf16[256,128]{1,0:T(8,128)(2,1)S(1)}, bf16[256,128]{1,0:T(8,128)(2,1)S(1)}, u32[]{:S(2)}, u32[]{:S(2)}) collective-permute-start(bf16[256,128]{1,0:T(8,128)(2,1)S(1)} %fusion.4), channel_id=1, source_target_pairs={{0,4},{1,5},{2,6},{3,7},{4,0},{5,1},{6,2},{7,3},{8,12},{9,13},{10,... | collective-permute-start | bytes 196616 | tf_op jit(solution)/shard_map/ppermute | solution.py:280
  21.4 0.6 %collective-permute-done.5 = bf16[272,128]{1,0:T(8,128)(2,1)S(1)} collective-permute-done((bf16[272,128]{1,0:T(8,128)(2,1)S(1)}, bf16[272,128]{1,0:T(8,128)(2,1)S(1)}, u32[]{:S(2)}, u32[]{:S(2)}) %collective-permute-start.5) | collective-permute-done | bytes 69664 | tf_op jit(solution)/shard_map/ppermute | solution.py:280
  22.0 0.0 copy-done.3
  22.0 1.7 %collective-permute-start.6 = (bf16[272,128]{1,0:T(8,128)(2,1)S(1)}, bf16[272,128]{1,0:T(8,128)(2,1)S(1)}, u32[]{:S(2)}, u32[]{:S(2)}) collective-permute-start(bf16[272,128]{1,0:T(8,128)(2,1)S(1)} %fusion.1), channel_id=1, source_target_pairs={{0,2},{1,3},{2,0},{3,1},{4,6},{5,7},{6,4},{7,5},{8,10},{9,11},{10,... | collective-permute-start | bytes 208904 | tf_op jit(solution)/shard_map/ppermute | solution.py:280
  23.7 0.0 copy-done.1
  23.7 0.0 copy-done.2
  23.7 1.4 %tables.1 = (f32[256,256]{1,0:T(8,128)S(1)}, f32[256,256]{1,0:T(8,128)S(1)}, f32[256,256]{1,0:T(8,128)S(1)}, f32[9,4096]{1,0:T(8,128)S(1)}, f32[2,4096]{1,0:T(2,128)S(1)}) custom-call(s32[1,32]{1,0:T(1,128)S(1)} %bitcast.6, f32[3,128]{1,0:T(4,128)S(1)} %copy-done.1, bf16[1,1]{1,0:T(2,128)(2,1)} %bitcast.5.energy_ref, bf16[1,1]{1,0:T(2,128)(2,1)} %bitcast.3.other_energy_ref, ...), custom_call_target="tpu_custom_call" | custom-call | flops 1048576 | bytes 786432 | tf_op jit(solution)/shard_map/tables/pallas_call | solution.py:178
  25.2 0.0 collective-permute-done.10
  25.2 2.1 %collective-permute-start.11 = (bf16[256,128]{1,0:T(8,128)(2,1)S(1)}, bf16[256,128]{1,0:T(8,128)(2,1)S(1)}, u32[]{:S(2)}, u32[]{:S(2)}) collective-permute-start(bf16[256,128]{1,0:T(8,128)(2,1)S(1)} %fusion.3), channel_id=1, source_target_pairs={{0,8},{1,9},{2,10},{3,11},{4,12},{5,13},{6,14},{7,15},{8,0},{9,1},... | collective-permute-start | bytes 196616 | tf_op jit(solution)/shard_map/ppermute | solution.py:280
  27.4 0.0 collective-permute-done.6
  27.4 0.1 collective-permute-start.7
  27.5 3.7 %collective-permute-done.11 = bf16[256,128]{1,0:T(8,128)(2,1)S(1)} collective-permute-done((bf16[256,128]{1,0:T(8,128)(2,1)S(1)}, bf16[256,128]{1,0:T(8,128)(2,1)S(1)}, u32[]{:S(2)}, u32[]{:S(2)}) %collective-permute-start.11) | collective-permute-done | bytes 65568 | tf_op jit(solution)/shard_map/ppermute | solution.py:280
  31.2 0.1 collective-permute-start.12
  31.3 0.0 collective-permute-done.7.other_sum_ref
  31.3 1.3 %collective-permute-done.12.other_cross_ref = f32[256,128]{1,0:T(8,128)S(1)} collective-permute-done((f32[256,128]{1,0:T(8,128)S(1)}, f32[256,128]{1,0:T(8,128)S(1)}, u32[]{:S(2)}, u32[]{:S(2)}) %collective-permute-start.12) | collective-permute-done | bytes 131104 | tf_op jit(solution)/shard_map/ppermute | solution.py:271
  32.6 3.0 %gamma_and_virial.1 = (bf16[256,4096]{1,0:T(8,128)(2,1)}, f32[9,4096]{1,0:T(8,128)}) custom-call(bf16[256,4096]{1,0:T(8,128)(2,1)S(1)} %get-tuple-element.28.own_ref, bf16[256,4096]{1,0:T(8,128)(2,1)S(1)} %collective-permute-done.other_ref, f32[256,256]{1,0:T(8,128)S(1)} %get-tuple-element.44.own_inverse_ref, ...), custom_call_target="tpu_custom_call" | custom-call | flops 1610612736 | bytes 6291456 | tf_op jit(solution)/shard_map/gamma_and_virial/pallas_call | solution.py:247
  (9 shorter events, 0.3 us)
Async XLA Ops:
  0.6 9.2 %copy-start = (s32[1,32]{1,0:T(1,128)S(1)}, s32[1,32]{1,0:T(1,128)}, u32[]{:S(2)}) copy-start(s32[1,32]{1,0:T(1,128)} %screen_ref.2) | copy-start | bytes 388
  0.6 9.2 %collective-permute-start = (bf16[256,4096]{1,0:T(8,128)(2,1)}, bf16[256,4096]{1,0:T(8,128)(2,1)S(1)}, u32[]{:S(2)}, u32[]{:S(2)}) collective-permute-start(bf16[256,4096]{1,0:T(8,128)(2,1)} %bitcast.7), channel_id=1, source_target_pairs={{0,16},{16,0},{1,17},{17,1},{2,18},{18,2},{3,19},{19,3},{4,20},{20... | collective-permute-start | bytes 6291464 | tf_op jit(solution)/shard_map/ppermute | solution.py:271
  1.2 4.1 %collective-permute-start.1 = (s32[1,32]{1,0:T(1,128)}, s32[1,32]{1,0:T(1,128)S(1)}, u32[]{:S(2)}, u32[]{:S(2)}) collective-permute-start(s32[1,32]{1,0:T(1,128)} %screen_ref.2), channel_id=1, source_target_pairs={{0,16},{16,0},{1,17},{17,1},{2,18},{18,2},{3,19},{19,3},{4,20},{20... | collective-permute-start | bytes 392 | tf_op jit(solution)/shard_map/ppermute | solution.py:271
  1.2 4.0 %collective-permute-start.2 = (bf16[1]{0:T(256)(128)(2,1)}, bf16[1]{0:T(256)(128)(2,1)}, u32[]{:S(2)}, u32[]{:S(2)}) collective-permute-start(bf16[1]{0:T(256)(128)(2,1)} %param.7), channel_id=1, source_target_pairs={{0,16},{16,0},{1,17},{17,1},{2,18},{18,2},{3,19},{19,3},{4,20},{20... | collective-permute-start | bytes 14 | tf_op jit(solution)/shard_map/ppermute | solution.py:271
  5.2 7.9 %collective-permute-start.3 = (bf16[272,128]{1,0:T(8,128)(2,1)S(1)}, bf16[272,128]{1,0:T(8,128)(2,1)S(1)}, u32[]{:S(2)}, u32[]{:S(2)}) collective-permute-start(bf16[272,128]{1,0:T(8,128)(2,1)S(1)} %get-tuple-element.31), channel_id=1, source_target_pairs={{0,8},{1,9},{2,10},{3,11},{4,12},{5,13},{6,14},{7,15},{8,0},{9,1},... | collective-permute-start | bytes 208904 | tf_op jit(solution)/shard_map/ppermute | solution.py:280
  9.8 12.2 %copy-start.3 = (bf16[256]{0:T(256)(128)(2,1)S(1)}, bf16[256]{0:T(256)(128)(2,1)}, u32[]{:S(2)}) copy-start(bf16[256]{0:T(256)(128)(2,1)} %param.8) | copy-start | bytes 1540
  9.8 13.9 %copy-start.1 = (f32[3,128]{1,0:T(4,128)S(1)}, f32[3,128]{1,0:T(4,128)}, u32[]{:S(2)}) copy-start(f32[3,128]{1,0:T(4,128)} %positions_ref.1) | copy-start | bytes 4612
  9.8 13.9 %copy-start.2 = (s32[32]{0:T(128)S(1)}, s32[32]{0:T(128)}, u32[]{:S(2)}) copy-start(s32[32]{0:T(128)} %param.10) | copy-start | bytes 388
  10.7 4.3 %collective-permute-start.8 = (bf16[256,128]{1,0:T(8,128)(2,1)S(1)}, bf16[256,128]{1,0:T(8,128)(2,1)S(1)}, u32[]{:S(2)}, u32[]{:S(2)}) collective-permute-start(bf16[256,128]{1,0:T(8,128)(2,1)S(1)} %get-tuple-element.51), channel_id=1, source_target_pairs={{0,1},{1,0},{2,3},{3,2},{4,5},{5,4},{6,7},{7,6},{8,9},{9,8},{10,11... | collective-permute-start | bytes 196616 | tf_op jit(solution)/shard_map/ppermute | solution.py:280
  13.2 4.4 %collective-permute-start.4 = (bf16[272,128]{1,0:T(8,128)(2,1)S(1)}, bf16[272,128]{1,0:T(8,128)(2,1)S(1)}, u32[]{:S(2)}, u32[]{:S(2)}) collective-permute-start(bf16[272,128]{1,0:T(8,128)(2,1)S(1)} %fusion), channel_id=1, source_target_pairs={{0,4},{1,5},{2,6},{3,7},{4,0},{5,1},{6,2},{7,3},{8,12},{9,13},{10,... | collective-permute-start | bytes 208904 | tf_op jit(solution)/shard_map/ppermute | solution.py:280
  15.0 4.5 %collective-permute-start.9 = (bf16[256,128]{1,0:T(8,128)(2,1)S(1)}, bf16[256,128]{1,0:T(8,128)(2,1)S(1)}, u32[]{:S(2)}, u32[]{:S(2)}) collective-permute-start(bf16[256,128]{1,0:T(8,128)(2,1)S(1)} %fusion.2), channel_id=1, source_target_pairs={{0,2},{1,3},{2,0},{3,1},{4,6},{5,7},{6,4},{7,5},{8,10},{9,11},{10,... | collective-permute-start | bytes 196616 | tf_op jit(solution)/shard_map/ppermute | solution.py:280
  17.6 4.4 %collective-permute-start.5 = (bf16[272,128]{1,0:T(8,128)(2,1)S(1)}, bf16[272,128]{1,0:T(8,128)(2,1)S(1)}, u32[]{:S(2)}, u32[]{:S(2)}) collective-permute-start(bf16[272,128]{1,0:T(8,128)(2,1)S(1)} %fusion.5), channel_id=1, source_target_pairs={{0,1},{1,0},{2,3},{3,2},{4,5},{5,4},{6,7},{7,6},{8,9},{9,8},{10,11... | collective-permute-start | bytes 208904 | tf_op jit(solution)/shard_map/ppermute | solution.py:280
  19.6 5.6 %collective-permute-start.10 = (bf16[256,128]{1,0:T(8,128)(2,1)S(1)}, bf16[256,128]{1,0:T(8,128)(2,1)S(1)}, u32[]{:S(2)}, u32[]{:S(2)}) collective-permute-start(bf16[256,128]{1,0:T(8,128)(2,1)S(1)} %fusion.4), channel_id=1, source_target_pairs={{0,4},{1,5},{2,6},{3,7},{4,0},{5,1},{6,2},{7,3},{8,12},{9,13},{10,... | collective-permute-start | bytes 196616 | tf_op jit(solution)/shard_map/ppermute | solution.py:280
  22.0 5.4 %collective-permute-start.6 = (bf16[272,128]{1,0:T(8,128)(2,1)S(1)}, bf16[272,128]{1,0:T(8,128)(2,1)S(1)}, u32[]{:S(2)}, u32[]{:S(2)}) collective-permute-start(bf16[272,128]{1,0:T(8,128)(2,1)S(1)} %fusion.1), channel_id=1, source_target_pairs={{0,2},{1,3},{2,0},{3,1},{4,6},{5,7},{6,4},{7,5},{8,10},{9,11},{10,... | collective-permute-start | bytes 208904 | tf_op jit(solution)/shard_map/ppermute | solution.py:280
  25.2 5.9 %collective-permute-start.11 = (bf16[256,128]{1,0:T(8,128)(2,1)S(1)}, bf16[256,128]{1,0:T(8,128)(2,1)S(1)}, u32[]{:S(2)}, u32[]{:S(2)}) collective-permute-start(bf16[256,128]{1,0:T(8,128)(2,1)S(1)} %fusion.3), channel_id=1, source_target_pairs={{0,8},{1,9},{2,10},{3,11},{4,12},{5,13},{6,14},{7,15},{8,0},{9,1},... | collective-permute-start | bytes 196616 | tf_op jit(solution)/shard_map/ppermute | solution.py:280
  27.4 3.9 %collective-permute-start.7 = (f32[272,128]{1,0:T(8,128)S(1)}, f32[272,128]{1,0:T(8,128)S(1)}, u32[]{:S(2)}, u32[]{:S(2)}) collective-permute-start(f32[272,128]{1,0:T(8,128)S(1)} %convert_add_fusion.own_sum_ref), channel_id=1, source_target_pairs={{0,16},{16,0},{1,17},{17,1},{2,18},{18,2},{3,19},{19,3},{4,20},{20... | collective-permute-start | bytes 417800 | tf_op jit(solution)/shard_map/ppermute | solution.py:271
  31.2 1.4 %collective-permute-start.12 = (f32[256,128]{1,0:T(8,128)S(1)}, f32[256,128]{1,0:T(8,128)S(1)}, u32[]{:S(2)}, u32[]{:S(2)}) collective-permute-start(f32[256,128]{1,0:T(8,128)S(1)} %convert_add_fusion.4.cross_sum_ref), channel_id=1, source_target_pairs={{0,16},{16,0},{1,17},{17,1},{2,18},{18,2},{3,19},{19,3},{4,20},{20... | collective-permute-start | bytes 393224 | tf_op jit(solution)/shard_map/ppermute | solution.py:271

commit v3 on v2

v3 whole, which is shorter than its diff:
```python
import functools

import jax
import jax.numpy as jnp
from jax import lax
from jax.experimental import pallas as pl
from jax.experimental.pallas import tpu as pltpu
from jax.sharding import PartitionSpec as P

F32 = jnp.float32
BF16 = jnp.bfloat16
CONTRACT_LAST = (((1,), (1,)), ((), ()))
SMEM = pltpu.MemorySpace.SMEM
VMEM = pltpu.MemorySpace.VMEM
PAD = 16


def mask_row(screen, first, count, width):
    values = screen.astype(F32)
    pieces = [
        jnp.broadcast_to(values[:, k : k + 1], (1, width)) for k in range(first, first + count)
    ]
    return jnp.concatenate(pieces, axis=1).astype(BF16)


def split(aux_dev, blocks, wanted):
    steps = wanted if blocks % wanted == 0 else 1
    return steps, aux_dev // steps, blocks // steps


def triangle(size):
    return (lax.broadcasted_iota(jnp.int32, (size, size), axis) for axis in (0, 1))


def own_pairs_kernel(
    blocks, width, screen_hbm, owner_hbm, positions_hbm, own_hbm,
    own_ref, factor_ref, sum_ref, send_ref, total, screen, owner, positions, sems,
):
    half = total.shape[0] // 2
    moves = ((screen_hbm, screen), (own_hbm, own_ref), (owner_hbm, owner), (positions_hbm, positions))
    copies = [pltpu.make_async_copy(*move, sems.at[k]) for k, move in enumerate(moves)]
    for copy in copies:
        copy.start()
    copies[0].wait()
    mask = mask_row(screen[...], 0, blocks, width)
    copies[2].wait()
    copies[3].wait()
    for block in range(blocks):
        atom = owner[0, block]
        where = [positions[c, atom] for c in range(3)]
        rows = [
            jnp.full((1, width), where[c] * where[d], F32) for c in range(3) for d in range(3)
        ]
        factor_ref[:, block * width : (block + 1) * width] = jnp.concatenate(rows, axis=0)
    copies[1].wait()
    own = own_ref[...]
    total[...] = lax.dot_general(own * mask, own, CONTRACT_LAST, preferred_element_type=F32)
    low, high = pl.ds(0, half), pl.ds(half, half)
    row, col = triangle(half)
    first, last = total[low, low], total[high, high]
    diagonal = jnp.sum(jnp.where(row == col, last, 0.0), axis=0, keepdims=True)
    parts = (
        total[high, low],
        jnp.where(row >= col, first, last),
        jnp.broadcast_to(diagonal, (PAD, half)),
    )
    start = 0
    for part in parts:
        rows = pl.ds(start, part.shape[0])
        sum_ref[rows, :] = part
        send_ref[rows, :] = part.astype(BF16)
        start += part.shape[0]


def cross_pairs_kernel(
    blocks, width, screen_ref, other_screen_ref, own_ref, other_ref, sum_ref, send_ref, total
):
    half = total.shape[0] // 2
    core = lax.axis_index("occ")
    mask = mask_row(screen_ref[...] * other_screen_ref[...], 0, blocks, width)
    total[...] = lax.dot_general(
        own_ref[...], other_ref[...] * mask, CONTRACT_LAST, preferred_element_type=F32
    )
    for place in range(2):
        rows = pl.ds(place * half, half)
        straight = total[rows, pl.ds(place * half, half)]
        across = total[rows, pl.ds((1 - place) * half, half)]
        part = jnp.where(core == 0, straight, across)
        sum_ref[rows, :] = part
        send_ref[rows, :] = part.astype(BF16)


def in_hbm(array):
    return pltpu.with_memory_space_constraint(array, pltpu.HBM)


def own_pairs(own, screen, owner, positions):
    virt, aux_dev = own.shape
    blocks = screen.shape[1]
    half = virt // 2
    operands = (screen, owner.reshape(1, -1), positions, own)
    return pl.pallas_call(
        functools.partial(own_pairs_kernel, blocks, aux_dev // blocks),
        in_specs=[pl.BlockSpec(memory_space=pltpu.HBM)] * 4,
        out_specs=[pl.BlockSpec(memory_space=VMEM)] * 4,
        out_shape=[
            jax.ShapeDtypeStruct((virt, aux_dev), BF16),
            jax.ShapeDtypeStruct((9, aux_dev), F32),
            jax.ShapeDtypeStruct((2 * half + PAD, half), F32),
            jax.ShapeDtypeStruct((2 * half + PAD, half), BF16),
        ],
        scratch_shapes=[
            pltpu.VMEM((virt, virt), F32),
            pltpu.VMEM((1, blocks), jnp.int32),
            pltpu.SMEM((1, blocks), jnp.int32),
            pltpu.SMEM(positions.shape, F32),
            pltpu.SemaphoreType.DMA((4,)),
        ],
        compiler_params=pltpu.CompilerParams(vmem_limit_bytes=8 << 20),
        cost_estimate=pl.CostEstimate(
            flops=2 * virt * virt * aux_dev, bytes_accessed=2 * virt * aux_dev, transcendentals=0
        ),
        name="own_pairs",
    )(*[in_hbm(operand) for operand in operands])


def cross_pairs(own, other, screen, other_screen):
    virt, aux_dev = own.shape
    blocks = other_screen.shape[1]
    half = virt // 2
    vmem = pl.BlockSpec(memory_space=VMEM)
    return pl.pallas_call(
        functools.partial(cross_pairs_kernel, blocks, aux_dev // blocks),
        in_specs=[vmem] * 4,
        out_specs=[vmem] * 2,
        out_shape=[
            jax.ShapeDtypeStruct((2 * half, half), F32),
            jax.ShapeDtypeStruct((2 * half, half), BF16),
        ],
        scratch_shapes=[pltpu.VMEM((virt, virt), F32)],
        compiler_params=pltpu.CompilerParams(vmem_limit_bytes=8 << 20),
        cost_estimate=pl.CostEstimate(
            flops=2 * virt * virt * aux_dev, bytes_accessed=4 * virt * aux_dev, transcendentals=0
        ),
        name="cross_pairs",
    )(screen, other_screen, own, other)


def symmetric(packed):
    half = packed.shape[1]
    row, col = triangle(half)
    low, both = packed[0:half, :], packed[half : 2 * half, :]
    turned = both.T
    first = jnp.where(row >= col, both, turned)
    last = jnp.where(row < col, both, turned)
    last = jnp.where(row == col, packed[2 * half : 2 * half + 1, :], last)
    top = jnp.concatenate([first, low.T], axis=1)
    return jnp.concatenate([top, jnp.concatenate([low, last], axis=1)], axis=0)


def inverse_kernel(virt_ref, energy_ref, other_energy_ref, own_ref, cross_ref):
    half = own_ref.shape[1]
    energy, other_energy = energy_ref[...].astype(F32), other_energy_ref[...].astype(F32)
    rows = [
        jnp.broadcast_to(virt_ref[:, k * half : (k + 1) * half].astype(F32), (half, half))
        for k in range(2)
    ]
    cols = [r.T for r in rows]
    row, col = triangle(half)
    twice = [(cols[k] - energy) + (rows[k] - energy) for k in range(2)]
    own_ref[0:half, :] = 1.0 / ((cols[1] - energy) + (rows[0] - energy))
    own_ref[half : 2 * half, :] = 1.0 / jnp.where(row >= col, twice[0], twice[1])
    last = rows[1][0:PAD, :] - energy
    own_ref[2 * half : 2 * half + PAD, :] = 1.0 / (last + last)
    even = lax.axis_index("occ") == 0
    for k in range(2):
        across = jnp.where(even, rows[k], rows[1 - k]) - other_energy
        cross_ref[k * half : (k + 1) * half, :] = 1.0 / ((cols[k] - energy) + across)


def inverse_spreads(virt_energy, energy, other_energy):
    half = virt_energy.shape[0] // 2
    vmem = pl.BlockSpec(memory_space=VMEM)
    return pl.pallas_call(
        inverse_kernel,
        in_specs=[vmem] * 3,
        out_specs=[vmem] * 2,
        out_shape=[
            jax.ShapeDtypeStruct((2 * half + PAD, half), F32),
            jax.ShapeDtypeStruct((2 * half, half), F32),
        ],
        compiler_params=pltpu.CompilerParams(vmem_limit_bytes=4 << 20),
        cost_estimate=pl.CostEstimate(
            flops=32 * half * half, bytes_accessed=32 * half * half, transcendentals=0
        ),
        name="inverse_spreads",
    )(virt_energy.reshape(1, -1), energy.reshape(1, 1), other_energy.reshape(1, 1))


def own_gamma_kernel(steps, blocks, width, screen_ref, amps_ref, own_ref, part_ref, weight_ref, amps):
    tile, per_step = own_ref.shape[1] // steps, blocks // steps
    amps[...] = symmetric(amps_ref[...])
    for step in range(steps):
        columns = pl.ds(step * tile, tile)
        own = own_ref[:, columns] * mask_row(screen_ref[...], step * per_step, per_step, width)
        part = jnp.dot(amps[...], own, preferred_element_type=F32)
        part_ref[:, columns] = part
        weight_ref[:, columns] = jnp.sum(part * own.astype(F32), axis=0, keepdims=True)


def other_weight_kernel(steps, blocks, width, screen_ref, amps_ref, own_ref, first_ref, weight_ref, amps):
    tile, per_step = own_ref.shape[1] // steps, blocks // steps
    amps[...] = symmetric(amps_ref[...])
    for step in range(steps):
        columns = pl.ds(step * tile, tile)
        own = own_ref[:, columns] * mask_row(screen_ref[...], step * per_step, per_step, width)
        part = jnp.dot(amps[...], own, preferred_element_type=F32)
        weight_ref[:, columns] = first_ref[:, columns] + jnp.sum(
            part * own.astype(F32), axis=0, keepdims=True
        )


def gamma_kernel(
    steps, blocks, width, screen_ref, other_screen_ref, cross_ref, other_cross_ref, own_ref,
    other_ref, part_ref, weight_ref, factor_ref,
    gamma_hbm, virial_hbm, gamma_ref, virial_ref, amps, sems, virial_sem,
):
    virt, aux_dev = own_ref.shape
    half, tile, per_step = virt // 2, aux_dev // steps, blocks // steps
    mine = [cross_ref[pl.ds(k * half, half), :] for k in range(2)]
    theirs = [other_cross_ref[pl.ds(k * half, half), :].T for k in range(2)]
    even = lax.axis_index("occ") == 0
    low, high = pl.ds(0, half), pl.ds(half, half)
    amps[low, low] = jnp.where(even, mine[0], theirs[0])
    amps[low, high] = jnp.where(even, theirs[1], mine[0])
    amps[high, low] = jnp.where(even, theirs[0], mine[1])
    amps[high, high] = jnp.where(even, mine[1], theirs[1])
    copies = []
    for step in range(steps):
        columns = pl.ds(step * tile, tile)
        other = other_ref[:, columns]
        other = other * mask_row(other_screen_ref[...], step * per_step, per_step, width)
        cross = jnp.dot(amps[...], other, preferred_element_type=F32)
        gamma_ref[:, columns] = (part_ref[:, columns] + cross).astype(BF16)
        copies.append(
            pltpu.make_async_copy(
                gamma_ref.at[:, columns], gamma_hbm.at[:, columns], sems.at[step]
            )
        )
        copies[step].start()
        twice = jnp.sum(cross * own_ref[:, columns].astype(F32), axis=0, keepdims=True)
        mask = mask_row(screen_ref[...], step * per_step, per_step, width).astype(F32)
        weight = weight_ref[:, columns] + 2.0 * (twice * mask)
        virial_ref[:, columns] = factor_ref[:, columns] * weight
    copies.append(pltpu.make_async_copy(virial_ref, virial_hbm, virial_sem))
    copies[steps].start()
    for copy in copies:
        copy.wait()


def gamma_call(kernel, name, out_shape, screen, amps, own, *rest):
    virt, aux_dev = own.shape
    blocks = screen.shape[1]
    steps = 8 if blocks % 8 == 0 else 1
    vmem = pl.BlockSpec(memory_space=VMEM)
    return pl.pallas_call(
        functools.partial(kernel, steps, blocks, aux_dev // blocks),
        in_specs=[vmem] * (3 + len(rest)),
        out_specs=[vmem] * len(out_shape),
        out_shape=out_shape,
        scratch_shapes=[pltpu.VMEM((virt, virt), BF16)],
        compiler_params=pltpu.CompilerParams(vmem_limit_bytes=8 << 20),
        cost_estimate=pl.CostEstimate(
            flops=2 * virt * virt * aux_dev, bytes_accessed=6 * virt * aux_dev, transcendentals=0
        ),
        name=name,
    )(screen, amps, own, *rest)


def own_gamma(own, screen, amps):
    row = jax.ShapeDtypeStruct((1, own.shape[1]), F32)
    part = jax.ShapeDtypeStruct(own.shape, F32)
    return gamma_call(own_gamma_kernel, "own_gamma", [part, row], screen, amps, own)


def other_weight(other, screen, amps, weight):
    row = jax.ShapeDtypeStruct((1, other.shape[1]), F32)
    return gamma_call(other_weight_kernel, "other_weight", [row], screen, amps, other, weight)[0]


def gamma_and_virial(own, other, screen, other_screen, cross, other_cross, part, weight, factor):
    virt, aux_dev = own.shape
    blocks = screen.shape[1]
    steps = 8 if blocks % 8 == 0 else 1
    vmem = pl.BlockSpec(memory_space=VMEM)
    hbm = pl.BlockSpec(memory_space=pltpu.HBM)
    return pl.pallas_call(
        functools.partial(gamma_kernel, steps, blocks, aux_dev // blocks),
        in_specs=[vmem] * 9,
        out_specs=[hbm, hbm],
        out_shape=[
            jax.ShapeDtypeStruct((virt, aux_dev), BF16),
            jax.ShapeDtypeStruct((9, aux_dev), F32),
        ],
        scratch_shapes=[
            pltpu.VMEM((virt, aux_dev), BF16),
            pltpu.VMEM((9, aux_dev), F32),
            pltpu.VMEM((virt, virt), BF16),
            pltpu.SemaphoreType.DMA((steps,)),
            pltpu.SemaphoreType.DMA,
        ],
        compiler_params=pltpu.CompilerParams(vmem_limit_bytes=8 << 20),
        cost_estimate=pl.CostEstimate(
            flops=2 * virt * virt * aux_dev, bytes_accessed=8 * virt * aux_dev, transcendentals=0
        ),
        name="gamma_and_virial",
    )(screen, other_screen, cross, other_cross, own, other, part, weight, factor)


def swap(array, axis, size, bit):
    return lax.ppermute(array, axis, [(i, i ^ bit) for i in range(size)])


def swap_by_core(array, n_aux, bits):
    pairs = [
        (core * n_aux + i, core * n_aux + (i ^ bit))
        for core, bit in enumerate(bits)
        for i in range(n_aux)
    ]
    return lax.ppermute(array, ("occ", "aux"), pairs)


def one_round(total, send, n_aux, bits):
    total = total + swap_by_core(send, n_aux, bits).astype(F32)
    return total, total.astype(BF16)


def after(value, late):
    return lax.optimization_barrier((value, late))


def orders_of(bits):
    if len(bits) != 4:
        turned = bits[1:] + bits[:1]
        return (bits, turned), (bits, turned)
    x, y, z, w = bits
    return ([z, x, w, y], [w, y, z, x]), ([x, y, z, w], [y, x, w, z])


def two_occ_body(n_aux, coeffs, occ_energy, virt_energy, screen, owner, positions):
    raw = coeffs[0]
    other_screen = swap(screen, "occ", 2, 1)
    other_energy = swap(occ_energy, "occ", 2, 1)
    other = swap(raw, "occ", 2, 1)
    cross_orders, own_orders = orders_of([1 << k for k in range(n_aux.bit_length() - 1)])
    own, factor, own_sum, own_send = own_pairs(raw, screen, owner, positions)
    cross_sum, cross_send = cross_pairs(own, other, screen, other_screen)
    rounds = len(own_orders[0])
    energy = occ_energy
    for step in range(rounds):
        if step == rounds - 2:
            own_send, other_energy = after(own_send, other_energy)
            energy = swap(other_energy, "occ", 2, 1)
        if step == rounds - 1:
            own_send, late = after(own_send, (virt_energy, energy, other_energy))
            virt_energy, energy, other_energy = late
        own_sum, own_send = one_round(own_sum, own_send, n_aux, [o[step] for o in own_orders])
    own_inverse, cross_inverse = inverse_spreads(virt_energy, energy, other_energy)
    own_amps = (own_sum * own_inverse).astype(BF16)
    part, weight = own_gamma(own, screen, own_amps)
    for step in range(rounds):
        cross_sum, cross_send = one_round(
            cross_sum, cross_send, n_aux, [o[step] for o in cross_orders]
        )
    cross = (cross_sum * cross_inverse).astype(BF16)
    own_amps, part = after(own_amps, part)
    other_amps = swap(own_amps, "occ", 2, 1)
    other_cross = swap(cross, "occ", 2, 1)
    weight = other_weight(other, other_screen, other_amps, weight)
    gamma, virial = gamma_and_virial(
        own, other, screen, other_screen, cross, other_cross, part, weight, factor
    )
    return gamma[None], virial


def general_body(n_aux, coeffs, occ_energy, virt_energy, screen, owner, positions):
    occ_dev, virt, aux_dev = coeffs.shape
    width = aux_dev // screen.shape[1]
    column_mask = jnp.repeat(screen[0], width).astype(BF16)
    masked = coeffs * column_mask[None, None, :]
    whole = lax.all_gather(masked, "occ", axis=0, tiled=True)
    energies = lax.all_gather(occ_energy, "occ", axis=0, tiled=True)
    all_rows = whole.reshape(-1, aux_dev)
    local = masked.reshape(-1, aux_dev)
    virt_f = virt_energy.astype(F32)
    spread_local = (virt_f[None, :] - occ_energy.astype(F32)[:, None]).reshape(-1)
    spread_all = (virt_f[None, :] - energies.astype(F32)[:, None]).reshape(-1)
    pairs = lax.dot_general(all_rows, local, CONTRACT_LAST, preferred_element_type=F32)
    if n_aux & (n_aux - 1):
        summed = lax.psum(pairs, "aux")
    else:
        bits = [1 << k for k in range(n_aux.bit_length() - 1)]
        summed, send = pairs, pairs.astype(BF16)
        for bit in bits:
            summed = summed + swap(send, "aux", n_aux, bit).astype(F32)
            send = summed.astype(BF16)
    amps = (summed / (spread_all[:, None] + spread_local[None, :])).astype(BF16)
    gamma = lax.dot_general(
        amps, all_rows, (((0,), (0,)), ((), ())), preferred_element_type=F32
    ).astype(BF16)
    partial_weight = jnp.sum(gamma.astype(F32) * local.astype(F32), axis=0)
    weight = lax.psum(partial_weight, "occ")
    where = jnp.repeat(positions[:, owner], width, axis=1)
    virial = (where[:, None, :] * where[None, :, :]).reshape(9, aux_dev) * weight[None, :]
    return gamma.reshape(occ_dev, virt, aux_dev), virial


def solution(mesh):
    placed = (P("occ", None, "aux"), P("occ"), P(), P("occ", "aux"), P("aux"), P())
    n_occ, n_aux = mesh.shape["occ"], mesh.shape["aux"]
    power_of_two = n_aux & (n_aux - 1) == 0

    def body(coeffs, *rest):
        fits = n_occ == 2 and coeffs.shape[0] == 1 and power_of_two
        chosen = two_occ_body if fits else general_body
        return chosen(n_aux, coeffs, *rest)

    return jax.shard_map(
        body,
        mesh=mesh,
        in_specs=placed,
        out_specs=(P("occ", None, "aux"), P(None, "aux")),
        check_vma=False,
    )
```

time: 35.8 us -> 31 us (0.87)
  waiting for transfers between devices: 9.92 us -> 6.25 us
  starting transfers between devices: 16.3 us -> 14.9 us
  Pallas kernels: 7.67 us -> 8.53 us
  between operations: 1.44 us -> 0.77 us
    ppermute x8, waiting for transfers between devices: 7.43 us -> 5.31 us  [swap_by_core(): return lax.ppermute(array, ('occ', 'aux'), pairs)]
    ppermute x5 -> x6, waiting for transfers between devices: 2.49 us -> 0.94 us  [swap(): return lax.ppermute(array, axis, [(i, i ^ bit) for i in range(size)])]
    ppermute x8, starting transfers between devices: 15.1 us -> 13.7 us  [swap_by_core(): return lax.ppermute(array, ('occ', 'aux'), pairs)]
    pallas_call x2 -> x4, Pallas kernels: 4.47 us -> 5.31 us  [the longest x1 2.09 us: gamma_and_virial(): pl.pallas_call(functools.partial(gamma_kernel, steps, blocks, aux_dev //...]
    ppermute x5 -> x6, starting transfers between devices: 1.17 us -> 1.24 us  [swap(): return lax.ppermute(array, axis, [(i, i ^ bit) for i in range(size)])]
  transfers between devices with their start and end apart: 13 -> 14, of which waited for: 8 -> 8; matrix products, arithmetic and copies ran while one was open for 1% -> 1% of each run, Pallas kernels for 13% -> 21%
where the time goes in v3:
time: 31 us; the launch traced here: 30.8 us
  starting transfers between devices  14.9 us (48%)
  Pallas kernels  8.53 us (28%)
  waiting for transfers between devices  6.25 us (20%)
  between operations  0.77 us (2%)
    ppermute x8, starting transfers between devices, swap_by_core(): return lax.ppermute(array, ('occ', 'aux'), pairs)  13.7 us
    ppermute x8, waiting for transfers between devices, swap_by_core(): return lax.ppermute(array, ('occ', 'aux'), pairs)  5.31 us
    pallas_call x1, Pallas kernels, own_pairs(): pl.pallas_call(functools.partial(own_pairs_kernel, blocks, aux_dev // blo...  2.4 us
    pallas_call x1, Pallas kernels, gamma_and_virial(): pl.pallas_call(functools.partial(gamma_kernel, steps, blocks, aux_dev //...  2.09 us
    pallas_call x2, Pallas kernels, gamma_call(): pl.pallas_call(functools.partial(kernel, steps, blocks, aux_dev // blocks...  1.93 us
    pallas_call x1, Pallas kernels, inverse_spreads(): pl.pallas_call(inverse_kernel, in_specs=[vmem] * 3, out_specs=[vmem] * 2,...  1.3 us
    ppermute x6, starting transfers between devices, swap(): return lax.ppermute(array, axis, [(i, i ^ bit) for i in range(size)])  1.24 us
    ppermute x6, waiting for transfers between devices, swap(): return lax.ppermute(array, axis, [(i, i ^ bit) for i in range(size)])  0.94 us
  transfers between devices with their start and end apart: 14, of which 8 were waited for; matrix products, arithmetic and copies ran while one was open for 1% of the time, Pallas kernels for 21%

profile of v3, /device:TPU:0, one launch (start us, length us, event | category | flops | bytes accessed | tf_op | source)
XLA Modules:
  0.0 30.8 jit_solution(17134624458846422445)
XLA Ops:
  0.6 0.0 copy-start
  0.6 0.5 %collective-permute-start.1 = (bf16[256,4096]{1,0:T(8,128)(2,1)}, bf16[256,4096]{1,0:T(8,128)(2,1)S(1)}, u32[]{:S(2)}, u32[]{:S(2)}) collective-permute-start(bf16[256,4096]{1,0:T(8,128)(2,1)} %bitcast.5), channel_id=1, source_target_pairs={{0,16},{16,0},{1,17},{17,1},{2,18},{18,2},{3,19},{19,3},{4,20},{20... | collective-permute-start | bytes 6291464 | tf_op jit(solution)/shard_map/ppermute | solution.py:321
  1.2 2.4 %own_pairs.1 = (bf16[256,4096]{1,0:T(8,128)(2,1)S(1)}, f32[9,4096]{1,0:T(8,128)S(1)}, f32[272,128]{1,0:T(8,128)S(1)}, bf16[272,128]{1,0:T(8,128)(2,1)S(1)}) custom-call(s32[1,32]{1,0:T(1,128)} %screen_ref.5, s32[1,32]{1,0:T(1,128)} %bitcast.7, f32[3,128]{1,0:T(4,128)} %positions_hbm.1, bf16[256,4096]{1,0:T(8,128)(2,1)} %bitcast.6), custom_call_target="tpu_custom_call" | custom-call | flops 536870912 | bytes 2097152 | tf_op jit(solution)/shard_map/own_pairs/pallas_call | solution.py:102
  3.6 2.6 %collective-permute-start.6 = (bf16[272,128]{1,0:T(8,128)(2,1)S(1)}, bf16[272,128]{1,0:T(8,128)(2,1)S(1)}, u32[]{:S(2)}, u32[]{:S(2)}) collective-permute-start(bf16[272,128]{1,0:T(8,128)(2,1)S(1)} %get-tuple-element.26), channel_id=1, source_target_pairs={{0,1},{1,0},{2,3},{3,2},{4,5},{5,4},{6,7},{7,6},{8,9},{9,8},{10,11... | collective-permute-start | bytes 208904 | tf_op jit(solution)/shard_map/ppermute | solution.py:330
  6.1 0.0 copy-done
  6.1 0.2 collective-permute-start
  6.4 0.3 collective-permute-start.8
  6.6 0.6 %collective-permute-done.other_screen_ref.screen_ref = s32[1,32]{1,0:T(1,128)S(1)} collective-permute-done((s32[1,32]{1,0:T(1,128)S(1)}, s32[1,32]{1,0:T(1,128)S(1)}, u32[]{:S(2)}, u32[]{:S(2)}) %collective-permute-start) | collective-permute-done | bytes 160 | tf_op jit(solution)/shard_map/ppermute | solution.py:321
  7.3 0.0 collective-permute-done.1.other_ref.own_ref
  7.3 0.0 copy-start.1
  7.3 0.8 %cross_pairs.1 = (f32[256,128]{1,0:T(8,128)S(1)}, bf16[256,128]{1,0:T(8,128)(2,1)S(1)}) custom-call(s32[1,32]{1,0:T(1,128)S(1)} %copy-done, s32[1,32]{1,0:T(1,128)S(1)} %collective-permute-done.other_screen_ref.screen_ref, bf16[256,4096]{1,0:T(8,128)(2,1)S(1)} %get-tuple-element.22.own_ref, bf16[256,4096]{1,0:T(8,128)(2,1)S(1)} %collective-permute-done.1.other_ref.own_ref), custom_call_target="tpu_custom_call" | custom-call | flops 536870912 | bytes 4194304 | tf_op jit(solution)/shard_map/cross_pairs/pallas_call | solution.py:132
  8.1 1.6 %collective-permute-start.2 = (bf16[256,128]{1,0:T(8,128)(2,1)S(1)}, bf16[256,128]{1,0:T(8,128)(2,1)S(1)}, u32[]{:S(2)}, u32[]{:S(2)}) collective-permute-start(bf16[256,128]{1,0:T(8,128)(2,1)S(1)} %get-tuple-element.24), channel_id=1, source_target_pairs={{0,4},{1,5},{2,6},{3,7},{4,0},{5,1},{6,2},{7,3},{8,12},{9,13},{10,... | collective-permute-start | bytes 196616 | tf_op jit(solution)/shard_map/ppermute | solution.py:330
  9.7 0.0 collective-permute-done.6
  9.8 1.6 %collective-permute-start.7 = (bf16[272,128]{1,0:T(8,128)(2,1)S(1)}, bf16[272,128]{1,0:T(8,128)(2,1)S(1)}, u32[]{:S(2)}, u32[]{:S(2)}) collective-permute-start(bf16[272,128]{1,0:T(8,128)(2,1)S(1)} %fusion), channel_id=1, source_target_pairs={{0,2},{1,3},{2,0},{3,1},{4,6},{5,7},{6,4},{7,5},{8,10},{9,11},{10,... | collective-permute-start | bytes 208904 | tf_op jit(solution)/shard_map/ppermute | solution.py:330
  11.3 1.8 %collective-permute-done.2 = bf16[256,128]{1,0:T(8,128)(2,1)S(1)} collective-permute-done((bf16[256,128]{1,0:T(8,128)(2,1)S(1)}, bf16[256,128]{1,0:T(8,128)(2,1)S(1)}, u32[]{:S(2)}, u32[]{:S(2)}) %collective-permute-start.2) | collective-permute-done | bytes 65568 | tf_op jit(solution)/shard_map/ppermute | solution.py:330
  13.1 1.5 %collective-permute-start.3 = (bf16[256,128]{1,0:T(8,128)(2,1)S(1)}, bf16[256,128]{1,0:T(8,128)(2,1)S(1)}, u32[]{:S(2)}, u32[]{:S(2)}) collective-permute-start(bf16[256,128]{1,0:T(8,128)(2,1)S(1)} %fusion.2), channel_id=1, source_target_pairs={{0,1},{1,0},{2,3},{3,2},{4,5},{5,4},{6,7},{7,6},{8,9},{9,8},{10,11... | collective-permute-start | bytes 196616 | tf_op jit(solution)/shard_map/ppermute | solution.py:330
  14.6 0.0 collective-permute-done.7
  14.7 0.0 collective-permute-done.8
  14.7 0.1 collective-permute-start.10
  14.8 1.3 %collective-permute-start.9 = (bf16[272,128]{1,0:T(8,128)(2,1)S(1)}, bf16[272,128]{1,0:T(8,128)(2,1)S(1)}, u32[]{:S(2)}, u32[]{:S(2)}) collective-permute-start(bf16[272,128]{1,0:T(8,128)(2,1)S(1)} %fusion.5), channel_id=1, source_target_pairs={{0,4},{1,5},{2,6},{3,7},{4,0},{5,1},{6,2},{7,3},{8,12},{9,13},{10,... | collective-permute-start | bytes 208904 | tf_op jit(solution)/shard_map/ppermute | solution.py:330
  16.1 1.4 %collective-permute-done.3 = bf16[256,128]{1,0:T(8,128)(2,1)S(1)} collective-permute-done((bf16[256,128]{1,0:T(8,128)(2,1)S(1)}, bf16[256,128]{1,0:T(8,128)(2,1)S(1)}, u32[]{:S(2)}, u32[]{:S(2)}) %collective-permute-start.3) | collective-permute-done | bytes 65568 | tf_op jit(solution)/shard_map/ppermute | solution.py:330
  17.5 2.0 %collective-permute-start.4 = (bf16[256,128]{1,0:T(8,128)(2,1)S(1)}, bf16[256,128]{1,0:T(8,128)(2,1)S(1)}, u32[]{:S(2)}, u32[]{:S(2)}) collective-permute-start(bf16[256,128]{1,0:T(8,128)(2,1)S(1)} %fusion.4), channel_id=1, source_target_pairs={{0,8},{1,9},{2,10},{3,11},{4,12},{5,13},{6,14},{7,15},{8,0},{9,1},... | collective-permute-start | bytes 196616 | tf_op jit(solution)/shard_map/ppermute | solution.py:330
  19.5 0.4 %collective-permute-done.9 = bf16[272,128]{1,0:T(8,128)(2,1)S(1)} collective-permute-done((bf16[272,128]{1,0:T(8,128)(2,1)S(1)}, bf16[272,128]{1,0:T(8,128)(2,1)S(1)}, u32[]{:S(2)}, u32[]{:S(2)}) %collective-permute-start.9) | collective-permute-done | bytes 69664 | tf_op jit(solution)/shard_map/ppermute | solution.py:330
  19.9 0.0 collective-permute-done.10
  20.0 0.0 copy-done.1
  20.0 1.6 %collective-permute-start.12 = (bf16[272,128]{1,0:T(8,128)(2,1)S(1)}, bf16[272,128]{1,0:T(8,128)(2,1)S(1)}, u32[]{:S(2)}, u32[]{:S(2)}) collective-permute-start(bf16[272,128]{1,0:T(8,128)(2,1)S(1)} %fusion.1), channel_id=1, source_target_pairs={{0,8},{1,9},{2,10},{3,11},{4,12},{5,13},{6,14},{7,15},{8,0},{9,1},... | collective-permute-start | bytes 208904 | tf_op jit(solution)/shard_map/ppermute | solution.py:330
  21.6 1.3 %inverse_spreads.1 = (f32[272,128]{1,0:T(8,128)S(1)}, f32[256,128]{1,0:T(8,128)S(1)}) custom-call(bf16[1,256]{1,0:T(2,128)(2,1)S(1)} %reshape.17.virt_ref, bf16[1,1]{1,0:T(2,128)(2,1)} %bitcast.2.energy_ref, bf16[1,1]{1,0:T(2,128)(2,1)} %bitcast.3.other_energy_ref), custom_call_target="tpu_custom_call" | custom-call | flops 524288 | bytes 524288 | tf_op jit(solution)/shard_map/inverse_spreads/pallas_call | solution.py:184
  22.9 0.0 collective-permute-done.4
  23.0 1.5 %collective-permute-start.5 = (bf16[256,128]{1,0:T(8,128)(2,1)S(1)}, bf16[256,128]{1,0:T(8,128)(2,1)S(1)}, u32[]{:S(2)}, u32[]{:S(2)}) collective-permute-start(bf16[256,128]{1,0:T(8,128)(2,1)S(1)} %fusion.3), channel_id=1, source_target_pairs={{0,2},{1,3},{2,0},{3,1},{4,6},{5,7},{6,4},{7,5},{8,10},{9,11},{10,... | collective-permute-start | bytes 196616 | tf_op jit(solution)/shard_map/ppermute | solution.py:330
  24.5 0.8 %collective-permute-done.12 = bf16[272,128]{1,0:T(8,128)(2,1)S(1)} collective-permute-done((bf16[272,128]{1,0:T(8,128)(2,1)S(1)}, bf16[272,128]{1,0:T(8,128)(2,1)S(1)}, u32[]{:S(2)}, u32[]{:S(2)}) %collective-permute-start.12) | collective-permute-done | bytes 69664 | tf_op jit(solution)/shard_map/ppermute | solution.py:330
  25.3 0.1 multiply_convert_fusion.amps_ref
  25.3 1.0 %own_gamma.1 = (f32[256,4096]{1,0:T(8,128)S(1)}, f32[1,4096]{1,0:T(1,128)S(1)}) custom-call(s32[1,32]{1,0:T(1,128)S(1)} %copy-done, bf16[272,128]{1,0:T(8,128)(2,1)S(1)} %multiply_convert_fusion.amps_ref, bf16[256,4096]{1,0:T(8,128)(2,1)S(1)} %get-tuple-element.22.own_ref), custom_call_target="tpu_custom_call" | custom-call | flops 536870912 | bytes 6291456 | tf_op jit(solution)/shard_map/own_gamma/pallas_call | solution.py:266
  26.3 0.1 collective-permute-start.13
  26.4 0.9 %collective-permute-done.5 = bf16[256,128]{1,0:T(8,128)(2,1)S(1)} collective-permute-done((bf16[256,128]{1,0:T(8,128)(2,1)S(1)}, bf16[256,128]{1,0:T(8,128)(2,1)S(1)}, u32[]{:S(2)}, u32[]{:S(2)}) %collective-permute-start.5) | collective-permute-done | bytes 65568 | tf_op jit(solution)/shard_map/ppermute | solution.py:330
  27.3 0.1 multiply_convert_fusion.1.cross_ref
  27.4 0.1 collective-permute-start.11
  27.5 0.2 collective-permute-done.13.amps_ref
  27.7 0.9 %other_weight.1.weight_ref = f32[1,4096]{1,0:T(1,128)S(1)} custom-call(s32[1,32]{1,0:T(1,128)S(1)} %collective-permute-done.other_screen_ref.screen_ref, bf16[272,128]{1,0:T(8,128)(2,1)S(1)} %collective-permute-done.13.amps_ref, bf16[256,4096]{1,0:T(8,128)(2,1)S(1)} %collective-permute-done.1.other_ref.own_ref, f32[1,4096]{1,0:T(1,128)S(1)} %get-tuple-element.38.first_ref), custom_call_target="tpu_custom_call" | custom-call | flops 536870912 | bytes 6291456 | tf_op jit(solution)/shard_map/other_weight/pallas_call | solution.py:266
  28.6 0.1 collective-permute-done.11.other_cross_ref
  28.7 2.1 %gamma_and_virial.1 = (bf16[256,4096]{1,0:T(8,128)(2,1)}, f32[9,4096]{1,0:T(8,128)}) custom-call(s32[1,32]{1,0:T(1,128)S(1)} %copy-done, s32[1,32]{1,0:T(1,128)S(1)} %collective-permute-done.other_screen_ref.screen_ref, bf16[256,128]{1,0:T(8,128)(2,1)S(1)} %multiply_convert_fusion.1.cross_ref, bf16[256,128]{1,0:T(8,128)(2,1)S(1)} %collective-permute-done.11.other_cross_ref, ...), custom_call_target="tpu_custom_call" | custom-call | flops 536870912 | bytes 8388608 | tf_op jit(solution)/shard_map/gamma_and_virial/pallas_call | solution.py:297
  (7 shorter events, 0.2 us)
Async XLA Ops:
  0.6 5.5 %copy-start = (s32[1,32]{1,0:T(1,128)S(1)}, s32[1,32]{1,0:T(1,128)}, u32[]{:S(2)}) copy-start(s32[1,32]{1,0:T(1,128)} %screen_ref.5) | copy-start | bytes 388
  0.6 6.6 %collective-permute-start.1 = (bf16[256,4096]{1,0:T(8,128)(2,1)}, bf16[256,4096]{1,0:T(8,128)(2,1)S(1)}, u32[]{:S(2)}, u32[]{:S(2)}) collective-permute-start(bf16[256,4096]{1,0:T(8,128)(2,1)} %bitcast.5), channel_id=1, source_target_pairs={{0,16},{16,0},{1,17},{17,1},{2,18},{18,2},{3,19},{19,3},{4,20},{20... | collective-permute-start | bytes 6291464 | tf_op jit(solution)/shard_map/ppermute | solution.py:321
  3.6 6.2 %collective-permute-start.6 = (bf16[272,128]{1,0:T(8,128)(2,1)S(1)}, bf16[272,128]{1,0:T(8,128)(2,1)S(1)}, u32[]{:S(2)}, u32[]{:S(2)}) collective-permute-start(bf16[272,128]{1,0:T(8,128)(2,1)S(1)} %get-tuple-element.26), channel_id=1, source_target_pairs={{0,1},{1,0},{2,3},{3,2},{4,5},{5,4},{6,7},{7,6},{8,9},{9,8},{10,11... | collective-permute-start | bytes 208904 | tf_op jit(solution)/shard_map/ppermute | solution.py:330
  6.1 1.1 %collective-permute-start = (s32[1,32]{1,0:T(1,128)S(1)}, s32[1,32]{1,0:T(1,128)S(1)}, u32[]{:S(2)}, u32[]{:S(2)}) collective-permute-start(s32[1,32]{1,0:T(1,128)S(1)} %copy-done), channel_id=1, source_target_pairs={{0,16},{16,0},{1,17},{17,1},{2,18},{18,2},{3,19},{19,3},{4,20},{20... | collective-permute-start | bytes 392 | tf_op jit(solution)/shard_map/ppermute | solution.py:321
  6.4 8.3 %collective-permute-start.8 = (bf16[1]{0:T(256)(128)(2,1)}, bf16[1]{0:T(256)(128)(2,1)}, u32[]{:S(2)}, u32[]{:S(2)}) collective-permute-start(bf16[1]{0:T(256)(128)(2,1)} %param.7), channel_id=1, source_target_pairs={{0,16},{16,0},{1,17},{17,1},{2,18},{18,2},{3,19},{19,3},{4,20},{20... | collective-permute-start | bytes 14 | tf_op jit(solution)/shard_map/ppermute | solution.py:321
  7.3 12.7 %copy-start.1 = (bf16[256]{0:T(256)(128)(2,1)S(1)}, bf16[256]{0:T(256)(128)(2,1)}, u32[]{:S(2)}) copy-start(bf16[256]{0:T(256)(128)(2,1)} %param.8) | copy-start | bytes 1540
  8.1 5.0 %collective-permute-start.2 = (bf16[256,128]{1,0:T(8,128)(2,1)S(1)}, bf16[256,128]{1,0:T(8,128)(2,1)S(1)}, u32[]{:S(2)}, u32[]{:S(2)}) collective-permute-start(bf16[256,128]{1,0:T(8,128)(2,1)S(1)} %get-tuple-element.24), channel_id=1, source_target_pairs={{0,4},{1,5},{2,6},{3,7},{4,0},{5,1},{6,2},{7,3},{8,12},{9,13},{10,... | collective-permute-start | bytes 196616 | tf_op jit(solution)/shard_map/ppermute | solution.py:330
  9.8 4.9 %collective-permute-start.7 = (bf16[272,128]{1,0:T(8,128)(2,1)S(1)}, bf16[272,128]{1,0:T(8,128)(2,1)S(1)}, u32[]{:S(2)}, u32[]{:S(2)}) collective-permute-start(bf16[272,128]{1,0:T(8,128)(2,1)S(1)} %fusion), channel_id=1, source_target_pairs={{0,2},{1,3},{2,0},{3,1},{4,6},{5,7},{6,4},{7,5},{8,10},{9,11},{10,... | collective-permute-start | bytes 208904 | tf_op jit(solution)/shard_map/ppermute | solution.py:330
  13.1 4.3 %collective-permute-start.3 = (bf16[256,128]{1,0:T(8,128)(2,1)S(1)}, bf16[256,128]{1,0:T(8,128)(2,1)S(1)}, u32[]{:S(2)}, u32[]{:S(2)}) collective-permute-start(bf16[256,128]{1,0:T(8,128)(2,1)S(1)} %fusion.2), channel_id=1, source_target_pairs={{0,1},{1,0},{2,3},{3,2},{4,5},{5,4},{6,7},{7,6},{8,9},{9,8},{10,11... | collective-permute-start | bytes 196616 | tf_op jit(solution)/shard_map/ppermute | solution.py:330
  14.7 5.3 %collective-permute-start.10 = (bf16[1]{0:T(256)(128)(2,1)}, bf16[1]{0:T(256)(128)(2,1)}, u32[]{:S(2)}, u32[]{:S(2)}) collective-permute-start(bf16[1]{0:T(256)(128)(2,1)} %collective-permute-done.8), channel_id=1, source_target_pairs={{0,16},{16,0},{1,17},{17,1},{2,18},{18,2},{3,19},{19,3},{4,20},{20... | collective-permute-start | bytes 14 | tf_op jit(solution)/shard_map/ppermute | solution.py:321
  14.8 5.1 %collective-permute-start.9 = (bf16[272,128]{1,0:T(8,128)(2,1)S(1)}, bf16[272,128]{1,0:T(8,128)(2,1)S(1)}, u32[]{:S(2)}, u32[]{:S(2)}) collective-permute-start(bf16[272,128]{1,0:T(8,128)(2,1)S(1)} %fusion.5), channel_id=1, source_target_pairs={{0,4},{1,5},{2,6},{3,7},{4,0},{5,1},{6,2},{7,3},{8,12},{9,13},{10,... | collective-permute-start | bytes 208904 | tf_op jit(solution)/shard_map/ppermute | solution.py:330
  17.5 5.4 %collective-permute-start.4 = (bf16[256,128]{1,0:T(8,128)(2,1)S(1)}, bf16[256,128]{1,0:T(8,128)(2,1)S(1)}, u32[]{:S(2)}, u32[]{:S(2)}) collective-permute-start(bf16[256,128]{1,0:T(8,128)(2,1)S(1)} %fusion.4), channel_id=1, source_target_pairs={{0,8},{1,9},{2,10},{3,11},{4,12},{5,13},{6,14},{7,15},{8,0},{9,1},... | collective-permute-start | bytes 196616 | tf_op jit(solution)/shard_map/ppermute | solution.py:330
  20.0 5.3 %collective-permute-start.12 = (bf16[272,128]{1,0:T(8,128)(2,1)S(1)}, bf16[272,128]{1,0:T(8,128)(2,1)S(1)}, u32[]{:S(2)}, u32[]{:S(2)}) collective-permute-start(bf16[272,128]{1,0:T(8,128)(2,1)S(1)} %fusion.1), channel_id=1, source_target_pairs={{0,8},{1,9},{2,10},{3,11},{4,12},{5,13},{6,14},{7,15},{8,0},{9,1},... | collective-permute-start | bytes 208904 | tf_op jit(solution)/shard_map/ppermute | solution.py:330
  23.0 4.3 %collective-permute-start.5 = (bf16[256,128]{1,0:T(8,128)(2,1)S(1)}, bf16[256,128]{1,0:T(8,128)(2,1)S(1)}, u32[]{:S(2)}, u32[]{:S(2)}) collective-permute-start(bf16[256,128]{1,0:T(8,128)(2,1)S(1)} %fusion.3), channel_id=1, source_target_pairs={{0,2},{1,3},{2,0},{3,1},{4,6},{5,7},{6,4},{7,5},{8,10},{9,11},{10,... | collective-permute-start | bytes 196616 | tf_op jit(solution)/shard_map/ppermute | solution.py:330
  26.3 1.3 %collective-permute-start.13 = (bf16[272,128]{1,0:T(8,128)(2,1)S(1)}, bf16[272,128]{1,0:T(8,128)(2,1)S(1)}, u32[]{:S(2)}, u32[]{:S(2)}) collective-permute-start(bf16[272,128]{1,0:T(8,128)(2,1)S(1)} %multiply_convert_fusion.amps_ref), channel_id=1, source_target_pairs={{0,16},{16,0},{1,17},{17,1},{2,18},{18,2},{3,19},{19,3},{4,20},{20... | collective-permute-start | bytes 208904 | tf_op jit(solution)/shard_map/ppermute | solution.py:321
  27.4 1.3 %collective-permute-start.11 = (bf16[256,128]{1,0:T(8,128)(2,1)S(1)}, bf16[256,128]{1,0:T(8,128)(2,1)S(1)}, u32[]{:S(2)}, u32[]{:S(2)}) collective-permute-start(bf16[256,128]{1,0:T(8,128)(2,1)S(1)} %multiply_convert_fusion.1.cross_ref), channel_id=1, source_target_pairs={{0,16},{16,0},{1,17},{17,1},{2,18},{18,2},{3,19},{19,3},{4,20},{20... | collective-permute-start | bytes 196616 | tf_op jit(solution)/shard_map/ppermute | solution.py:321

commit v4 on v3

--- a/solution.py
+++ b/solution.py
@@ -12,6 +12,7 @@
 CONTRACT_LAST = (((1,), (1,)), ((), ()))
 SMEM = pltpu.MemorySpace.SMEM
 VMEM = pltpu.MemorySpace.VMEM
+LANES = 128
 PAD = 16
 
 
@@ -140,7 +141,7 @@
         scratch_shapes=[pltpu.VMEM((virt, virt), F32)],
         compiler_params=pltpu.CompilerParams(vmem_limit_bytes=8 << 20),
         cost_estimate=pl.CostEstimate(
-            flops=2 * virt * virt * aux_dev, bytes_accessed=4 * virt * aux_dev, transcendentals=0
+            flops=8 * virt * virt * aux_dev, bytes_accessed=16 * virt * aux_dev, transcendentals=0
         ),
         name="cross_pairs",
     )(screen, other_screen, own, other)
@@ -160,7 +161,9 @@
 
 def inverse_kernel(virt_ref, energy_ref, other_energy_ref, own_ref, cross_ref):
     half = own_ref.shape[1]
-    energy, other_energy = energy_ref[...].astype(F32), other_energy_ref[...].astype(F32)
+    energy, other_energy = (
+        ref[...].astype(F32)[0:1, 0:1] for ref in (energy_ref, other_energy_ref)
+    )
     rows = [
         jnp.broadcast_to(virt_ref[:, k * half : (k + 1) * half].astype(F32), (half, half))
         for k in range(2)
@@ -194,39 +197,44 @@
             flops=32 * half * half, bytes_accessed=32 * half * half, transcendentals=0
         ),
         name="inverse_spreads",
-    )(virt_energy.reshape(1, -1), energy.reshape(1, 1), other_energy.reshape(1, 1))
-
-
-def own_gamma_kernel(steps, blocks, width, screen_ref, amps_ref, own_ref, part_ref, weight_ref, amps):
+    )(virt_energy.reshape(1, -1), energy.reshape(1, -1), other_energy.reshape(1, -1))
+
+
+def own_gamma_kernel(
+    steps, blocks, width, screen_ref, amps_ref, own_ref, masked_ref, part_ref, weight_ref, amps
+):
     tile, per_step = own_ref.shape[1] // steps, blocks // steps
     amps[...] = symmetric(amps_ref[...])
     for step in range(steps):
         columns = pl.ds(step * tile, tile)
         own = own_ref[:, columns] * mask_row(screen_ref[...], step * per_step, per_step, width)
         part = jnp.dot(amps[...], own, preferred_element_type=F32)
+        masked_ref[:, columns] = own
         part_ref[:, columns] = part
         weight_ref[:, columns] = jnp.sum(part * own.astype(F32), axis=0, keepdims=True)
 
 
-def other_weight_kernel(steps, blocks, width, screen_ref, amps_ref, own_ref, first_ref, weight_ref, amps):
+def other_weight_kernel(
+    steps, blocks, width, screen_ref, amps_ref, own_ref, first_ref, masked_ref, weight_ref, amps
+):
     tile, per_step = own_ref.shape[1] // steps, blocks // steps
     amps[...] = symmetric(amps_ref[...])
     for step in range(steps):
         columns = pl.ds(step * tile, tile)
         own = own_ref[:, columns] * mask_row(screen_ref[...], step * per_step, per_step, width)
         part = jnp.dot(amps[...], own, preferred_element_type=F32)
+        masked_ref[:, columns] = own
         weight_ref[:, columns] = first_ref[:, columns] + jnp.sum(
             part * own.astype(F32), axis=0, keepdims=True
         )
 
 
 def gamma_kernel(
-    steps, blocks, width, screen_ref, other_screen_ref, cross_ref, other_cross_ref, own_ref,
-    other_ref, part_ref, weight_ref, factor_ref,
+    steps, cross_ref, other_cross_ref, own_ref, other_ref, part_ref, weight_ref, factor_ref,
     gamma_hbm, virial_hbm, gamma_ref, virial_ref, amps, sems, virial_sem,
 ):
     virt, aux_dev = own_ref.shape
-    half, tile, per_step = virt // 2, aux_dev // steps, blocks // steps
+    half, tile = virt // 2, aux_dev // steps
     mine = [cross_ref[pl.ds(k * half, half), :] for k in range(2)]
     theirs = [other_cross_ref[pl.ds(k * half, half), :].T for k in range(2)]
     even = lax.axis_index("occ") == 0
@@ -238,9 +246,7 @@
     copies = []
     for step in range(steps):
         columns = pl.ds(step * tile, tile)
-        other = other_ref[:, columns]
-        other = other * mask_row(other_screen_ref[...], step * per_step, per_step, width)
-        cross = jnp.dot(amps[...], other, preferred_element_type=F32)
+        cross = jnp.dot(amps[...], other_ref[:, columns], preferred_element_type=F32)
         gamma_ref[:, columns] = (part_ref[:, columns] + cross).astype(BF16)
         copies.append(
             pltpu.make_async_copy(
@@ -249,9 +255,7 @@
         )
         copies[step].start()
         twice = jnp.sum(cross * own_ref[:, columns].astype(F32), axis=0, keepdims=True)
-        mask = mask_row(screen_ref[...], step * per_step, per_step, width).astype(F32)
-        weight = weight_ref[:, columns] + 2.0 * (twice * mask)
-        virial_ref[:, columns] = factor_ref[:, columns] * weight
+        virial_ref[:, columns] = factor_ref[:, columns] * (weight_ref[:, columns] + 2.0 * twice)
     copies.append(pltpu.make_async_copy(virial_ref, virial_hbm, virial_sem))
     copies[steps].start()
     for copy in copies:
@@ -280,23 +284,26 @@
 def own_gamma(own, screen, amps):
     row = jax.ShapeDtypeStruct((1, own.shape[1]), F32)
     part = jax.ShapeDtypeStruct(own.shape, F32)
-    return gamma_call(own_gamma_kernel, "own_gamma", [part, row], screen, amps, own)
+    masked = jax.ShapeDtypeStruct(own.shape, BF16)
+    return gamma_call(own_gamma_kernel, "own_gamma", [masked, part, row], screen, amps, own)
 
 
 def other_weight(other, screen, amps, weight):
     row = jax.ShapeDtypeStruct((1, other.shape[1]), F32)
-    return gamma_call(other_weight_kernel, "other_weight", [row], screen, amps, other, weight)[0]
-
-
-def gamma_and_virial(own, other, screen, other_screen, cross, other_cross, part, weight, factor):
+    masked = jax.ShapeDtypeStruct(other.shape, BF16)
+    return gamma_call(
+        other_weight_kernel, "other_weight", [masked, row], screen, amps, other, weight
+    )
+
+
+def gamma_and_virial(own, other, cross, other_cross, part, weight, factor):
     virt, aux_dev = own.shape
-    blocks = screen.shape[1]
-    steps = 8 if blocks % 8 == 0 else 1
+    steps = 8 if aux_dev % 1024 == 0 else 1
     vmem = pl.BlockSpec(memory_space=VMEM)
     hbm = pl.BlockSpec(memory_space=pltpu.HBM)
     return pl.pallas_call(
-        functools.partial(gamma_kernel, steps, blocks, aux_dev // blocks),
-        in_specs=[vmem] * 9,
+        functools.partial(gamma_kernel, steps),
+        in_specs=[vmem] * 7,
         out_specs=[hbm, hbm],
         out_shape=[
             jax.ShapeDtypeStruct((virt, aux_dev), BF16),
@@ -314,7 +321,7 @@
             flops=2 * virt * virt * aux_dev, bytes_accessed=8 * virt * aux_dev, transcendentals=0
         ),
         name="gamma_and_virial",
-    )(screen, other_screen, cross, other_cross, own, other, part, weight, factor)
+    )(cross, other_cross, own, other, part, weight, factor)
 
 
 def swap(array, axis, size, bit):
@@ -344,42 +351,40 @@
         turned = bits[1:] + bits[:1]
         return (bits, turned), (bits, turned)
     x, y, z, w = bits
-    return ([z, x, w, y], [w, y, z, x]), ([x, y, z, w], [y, x, w, z])
+    return ([x, y, z, w], [y, x, w, z]), ([x, w, z, y], [y, z, w, x])
 
 
 def two_occ_body(n_aux, coeffs, occ_energy, virt_energy, screen, owner, positions):
     raw = coeffs[0]
     other_screen = swap(screen, "occ", 2, 1)
-    other_energy = swap(occ_energy, "occ", 2, 1)
     other = swap(raw, "occ", 2, 1)
     cross_orders, own_orders = orders_of([1 << k for k in range(n_aux.bit_length() - 1)])
     own, factor, own_sum, own_send = own_pairs(raw, screen, owner, positions)
     cross_sum, cross_send = cross_pairs(own, other, screen, other_screen)
     rounds = len(own_orders[0])
-    energy = occ_energy
+    energy = jnp.pad(occ_energy, (0, LANES - 1))
+    cross_send, energy = after(cross_send, energy)
+    other_energy = swap(energy, "occ", 2, 1)
+    inverses = inverse_spreads(virt_energy, energy, other_energy)
+    first_cross = cross_send
     for step in range(rounds):
-        if step == rounds - 2:
-            own_send, other_energy = after(own_send, other_energy)
-            energy = swap(other_energy, "occ", 2, 1)
-        if step == rounds - 1:
-            own_send, late = after(own_send, (virt_energy, energy, other_energy))
-            virt_energy, energy, other_energy = late
+        if step == 1:
+            own_send, _ = after(own_send, first_cross)
+        if step == rounds // 2:
+            cross_send, inverses = after(cross_send, inverses)
         own_sum, own_send = one_round(own_sum, own_send, n_aux, [o[step] for o in own_orders])
-    own_inverse, cross_inverse = inverse_spreads(virt_energy, energy, other_energy)
-    own_amps = (own_sum * own_inverse).astype(BF16)
-    part, weight = own_gamma(own, screen, own_amps)
-    for step in range(rounds):
         cross_sum, cross_send = one_round(
             cross_sum, cross_send, n_aux, [o[step] for o in cross_orders]
         )
+    own_inverse, cross_inverse = inverses
+    own_amps = (own_sum * own_inverse).astype(BF16)
+    own, part, weight = own_gamma(own, screen, own_amps)
     cross = (cross_sum * cross_inverse).astype(BF16)
-    own_amps, part = after(own_amps, part)
+    cross, part = after(cross, part)
     other_amps = swap(own_amps, "occ", 2, 1)
     other_cross = swap(cross, "occ", 2, 1)
-    weight = other_weight(other, other_screen, other_amps, weight)
-    gamma, virial = gamma_and_virial(
-        own, other, screen, other_screen, cross, other_cross, part, weight, factor
-    )
+    other, weight = other_weight(other, other_screen, other_amps, weight)
+    gamma, virial = gamma_and_virial(own, other, cross, other_cross, part, weight, factor)
     return gamma[None], virial
 
 
@@ -421,7 +426,8 @@
     power_of_two = n_aux & (n_aux - 1) == 0
 
     def body(coeffs, *rest):
-        fits = n_occ == 2 and coeffs.shape[0] == 1 and power_of_two
+        even_halves = coeffs.shape[1] % (2 * LANES) == 0
+        fits = n_occ == 2 and coeffs.shape[0] == 1 and power_of_two and even_halves
         chosen = two_occ_body if fits else general_body
         return chosen(n_aux, coeffs, *rest)
 

time: 31 us -> 30.2 us (0.974)
  waiting for transfers between devices: 6.25 us -> 3.28 us
  starting transfers between devices: 14.9 us -> 17.8 us
  Pallas kernels: 8.53 us -> 7.18 us
  between operations: 0.77 us -> 1.46 us
    ppermute x8, starting transfers between devices: 13.7 us -> 17 us  [swap_by_core(): return lax.ppermute(array, ('occ', 'aux'), pairs)]
    ppermute x8, waiting for transfers between devices: 5.31 us -> 3.02 us  [swap_by_core(): return lax.ppermute(array, ('occ', 'aux'), pairs)]
    pallas_call x1, Pallas kernels: 1.3 us -> 0.12 us  [inverse_spreads(): pl.pallas_call(inverse_kernel, in_specs=[vmem] * 3, out_specs=[vmem] * 2,...]
    ppermute x6 -> x5, waiting for transfers between devices: 0.94 us -> 0.26 us  [swap(): return lax.ppermute(array, axis, [(i, i ^ bit) for i in range(size)])]
    ppermute x6 -> x5, starting transfers between devices: 1.24 us -> 0.81 us  [swap(): return lax.ppermute(array, axis, [(i, i ^ bit) for i in range(size)])]
  transfers between devices with their start and end apart: 14 -> 13, of which waited for: 8 -> 6; matrix products, arithmetic and copies ran while one was open for 1% -> 1% of each run, Pallas kernels for 21% -> 17%
where the time goes in v4:
time: 30.2 us; the launch traced here: 30.1 us
  starting transfers between devices  17.8 us (59%)
  Pallas kernels  7.18 us (24%)
  waiting for transfers between devices  3.28 us (11%)
  between operations  1.46 us (5%)
    ppermute x8, starting transfers between devices, swap_by_core(): return lax.ppermute(array, ('occ', 'aux'), pairs)  17 us
    ppermute x8, waiting for transfers between devices, swap_by_core(): return lax.ppermute(array, ('occ', 'aux'), pairs)  3.02 us
    pallas_call x1, Pallas kernels, own_pairs(): pl.pallas_call(functools.partial(own_pairs_kernel, blocks, aux_dev // blo...  2.4 us
    pallas_call x2, Pallas kernels, gamma_call(): pl.pallas_call(functools.partial(kernel, steps, blocks, aux_dev // blocks...  1.93 us
    pallas_call x1, Pallas kernels, gamma_and_virial(): pl.pallas_call(functools.partial(gamma_kernel, steps), in_specs=[vmem] *...  1.92 us
    pallas_call x1, Pallas kernels, cross_pairs(): pl.pallas_call(functools.partial(cross_pairs_kernel, blocks, aux_dev // b...  0.82 us
    ppermute x5, starting transfers between devices, swap(): return lax.ppermute(array, axis, [(i, i ^ bit) for i in range(size)])  0.81 us
  transfers between devices with their start and end apart: 13, of which 6 were waited for; matrix products, arithmetic and copies ran while one was open for 1% of the time, Pallas kernels for 17%

profile of v4, /device:TPU:0, one launch (start us, length us, event | category | flops | bytes accessed | tf_op | source)
XLA Modules:
  0.0 30.1 jit_solution(9907895396737167133)
XLA Ops:
  0.6 0.0 copy-start
  0.6 0.0 copy-start.1
  0.7 0.5 %collective-permute-start.1 = (bf16[256,4096]{1,0:T(8,128)(2,1)}, bf16[256,4096]{1,0:T(8,128)(2,1)S(1)}, u32[]{:S(2)}, u32[]{:S(2)}) collective-permute-start(bf16[256,4096]{1,0:T(8,128)(2,1)} %bitcast.7), channel_id=1, source_target_pairs={{0,16},{16,0},{1,17},{17,1},{2,18},{18,2},{3,19},{19,3},{4,20},{20... | collective-permute-start | bytes 6291464 | tf_op jit(solution)/shard_map/ppermute | solution.py:328
  1.2 0.1 collective-permute-start
  1.2 2.4 %own_pairs.1 = (bf16[256,4096]{1,0:T(8,128)(2,1)S(1)}, f32[9,4096]{1,0:T(8,128)S(1)}, f32[272,128]{1,0:T(8,128)S(1)}, bf16[272,128]{1,0:T(8,128)(2,1)S(1)}) custom-call(s32[1,32]{1,0:T(1,128)} %screen_ref.3, s32[1,32]{1,0:T(1,128)} %bitcast.9, f32[3,128]{1,0:T(4,128)} %positions_hbm.1, bf16[256,4096]{1,0:T(8,128)(2,1)} %bitcast.8), custom_call_target="tpu_custom_call" | custom-call | flops 536870912 | bytes 2097152 | tf_op jit(solution)/shard_map/own_pairs/pallas_call | solution.py:103
  3.7 3.0 %collective-permute-start.7 = (bf16[272,128]{1,0:T(8,128)(2,1)S(1)}, bf16[272,128]{1,0:T(8,128)(2,1)S(1)}, u32[]{:S(2)}, u32[]{:S(2)}) collective-permute-start(bf16[272,128]{1,0:T(8,128)(2,1)S(1)} %get-tuple-element.35), channel_id=1, source_target_pairs={{0,1},{1,0},{2,3},{3,2},{4,5},{5,4},{6,7},{7,6},{8,9},{9,8},{10,11... | collective-permute-start | bytes 208904 | tf_op jit(solution)/shard_map/ppermute | solution.py:337
  7.3 0.0 copy-done.1
  7.3 0.0 collective-permute-done.other_screen_ref.screen_ref
  7.3 0.0 collective-permute-done.1.other_ref.own_ref
  7.3 0.0 copy-done
  7.4 0.8 %cross_pairs.1 = (f32[256,128]{1,0:T(8,128)S(1)}, bf16[256,128]{1,0:T(8,128)(2,1)S(1)}) custom-call(s32[1,32]{1,0:T(1,128)S(1)} %copy-done, s32[1,32]{1,0:T(1,128)S(1)} %collective-permute-done.other_screen_ref.screen_ref, bf16[256,4096]{1,0:T(8,128)(2,1)S(1)} %get-tuple-element.25.own_ref, bf16[256,4096]{1,0:T(8,128)(2,1)S(1)} %collective-permute-done.1.other_ref.own_ref), custom_call_target="tpu_custom_call" | custom-call | flops 2147483648 | bytes 16777216 | tf_op jit(solution)/shard_map/cross_pairs/pallas_call | solution.py:133
  8.2 0.1 collective-permute-start.4
  8.3 1.3 %collective-permute-start.2 = (bf16[256,128]{1,0:T(8,128)(2,1)S(1)}, bf16[256,128]{1,0:T(8,128)(2,1)S(1)}, u32[]{:S(2)}, u32[]{:S(2)}) collective-permute-start(bf16[256,128]{1,0:T(8,128)(2,1)S(1)} %get-tuple-element.28), channel_id=1, source_target_pairs={{0,1},{1,0},{2,3},{3,2},{4,5},{5,4},{6,7},{7,6},{8,9},{9,8},{10,11... | collective-permute-start | bytes 196616 | tf_op jit(solution)/shard_map/ppermute | solution.py:337
  9.6 0.0 collective-permute-done.7
  9.6 2.7 %collective-permute-start.8 = (bf16[272,128]{1,0:T(8,128)(2,1)S(1)}, bf16[272,128]{1,0:T(8,128)(2,1)S(1)}, u32[]{:S(2)}, u32[]{:S(2)}) collective-permute-start(bf16[272,128]{1,0:T(8,128)(2,1)S(1)} %fusion), channel_id=1, source_target_pairs={{0,8},{1,9},{2,10},{3,11},{4,12},{5,13},{6,14},{7,15},{8,0},{9,1},... | collective-permute-start | bytes 208904 | tf_op jit(solution)/shard_map/ppermute | solution.py:337
  12.2 0.0 collective-permute-done.4
  12.2 0.1 inverse_spreads.1
  12.4 0.2 collective-permute-done.2
  12.6 1.6 %collective-permute-start.3 = (bf16[256,128]{1,0:T(8,128)(2,1)S(1)}, bf16[256,128]{1,0:T(8,128)(2,1)S(1)}, u32[]{:S(2)}, u32[]{:S(2)}) collective-permute-start(bf16[256,128]{1,0:T(8,128)(2,1)S(1)} %fusion.2), channel_id=1, source_target_pairs={{0,2},{1,3},{2,0},{3,1},{4,6},{5,7},{6,4},{7,5},{8,10},{9,11},{10,... | collective-permute-start | bytes 196616 | tf_op jit(solution)/shard_map/ppermute | solution.py:337
  14.2 0.7 %collective-permute-done.8 = bf16[272,128]{1,0:T(8,128)(2,1)S(1)} collective-permute-done((bf16[272,128]{1,0:T(8,128)(2,1)S(1)}, bf16[272,128]{1,0:T(8,128)(2,1)S(1)}, u32[]{:S(2)}, u32[]{:S(2)}) %collective-permute-start.8) | collective-permute-done | bytes 69664 | tf_op jit(solution)/shard_map/ppermute | solution.py:337
  14.9 2.0 %collective-permute-start.9 = (bf16[272,128]{1,0:T(8,128)(2,1)S(1)}, bf16[272,128]{1,0:T(8,128)(2,1)S(1)}, u32[]{:S(2)}, u32[]{:S(2)}) collective-permute-start(bf16[272,128]{1,0:T(8,128)(2,1)S(1)} %fusion.5), channel_id=1, source_target_pairs={{0,4},{1,5},{2,6},{3,7},{4,0},{5,1},{6,2},{7,3},{8,12},{9,13},{10,... | collective-permute-start | bytes 208904 | tf_op jit(solution)/shard_map/ppermute | solution.py:337
  16.9 0.1 collective-permute-done.3
  17.0 1.6 %collective-permute-start.5 = (bf16[256,128]{1,0:T(8,128)(2,1)S(1)}, bf16[256,128]{1,0:T(8,128)(2,1)S(1)}, u32[]{:S(2)}, u32[]{:S(2)}) collective-permute-start(bf16[256,128]{1,0:T(8,128)(2,1)S(1)} %fusion.4), channel_id=1, source_target_pairs={{0,4},{1,5},{2,6},{3,7},{4,0},{5,1},{6,2},{7,3},{8,12},{9,13},{10,... | collective-permute-start | bytes 196616 | tf_op jit(solution)/shard_map/ppermute | solution.py:337
  18.6 0.7 %collective-permute-done.9 = bf16[272,128]{1,0:T(8,128)(2,1)S(1)} collective-permute-done((bf16[272,128]{1,0:T(8,128)(2,1)S(1)}, bf16[272,128]{1,0:T(8,128)(2,1)S(1)}, u32[]{:S(2)}, u32[]{:S(2)}) %collective-permute-start.9) | collective-permute-done | bytes 69664 | tf_op jit(solution)/shard_map/ppermute | solution.py:337
  19.3 2.2 %collective-permute-start.10 = (bf16[272,128]{1,0:T(8,128)(2,1)S(1)}, bf16[272,128]{1,0:T(8,128)(2,1)S(1)}, u32[]{:S(2)}, u32[]{:S(2)}) collective-permute-start(bf16[272,128]{1,0:T(8,128)(2,1)S(1)} %fusion.1), channel_id=1, source_target_pairs={{0,2},{1,3},{2,0},{3,1},{4,6},{5,7},{6,4},{7,5},{8,10},{9,11},{10,... | collective-permute-start | bytes 208904 | tf_op jit(solution)/shard_map/ppermute | solution.py:337
  21.5 0.0 collective-permute-done.5
  21.5 2.7 %collective-permute-start.6 = (bf16[256,128]{1,0:T(8,128)(2,1)S(1)}, bf16[256,128]{1,0:T(8,128)(2,1)S(1)}, u32[]{:S(2)}, u32[]{:S(2)}) collective-permute-start(bf16[256,128]{1,0:T(8,128)(2,1)S(1)} %fusion.3), channel_id=1, source_target_pairs={{0,8},{1,9},{2,10},{3,11},{4,12},{5,13},{6,14},{7,15},{8,0},{9,1},... | collective-permute-start | bytes 196616 | tf_op jit(solution)/shard_map/ppermute | solution.py:337
  24.2 0.0 collective-permute-done.10
  24.2 0.1 multiply_convert_fusion.amps_ref
  24.3 0.1 collective-permute-start.12
  24.4 1.0 %own_gamma.1 = (bf16[256,4096]{1,0:T(8,128)(2,1)S(1)}, f32[256,4096]{1,0:T(8,128)S(1)}, f32[1,4096]{1,0:T(1,128)S(1)}) custom-call(s32[1,32]{1,0:T(1,128)S(1)} %copy-done, bf16[272,128]{1,0:T(8,128)(2,1)S(1)} %multiply_convert_fusion.amps_ref, bf16[256,4096]{1,0:T(8,128)(2,1)S(1)} %get-tuple-element.25.own_ref), custom_call_target="tpu_custom_call" | custom-call | flops 536870912 | bytes 6291456 | tf_op jit(solution)/shard_map/own_gamma/pallas_call | solution.py:270
  25.4 1.4 %collective-permute-done.6 = bf16[256,128]{1,0:T(8,128)(2,1)S(1)} collective-permute-done((bf16[256,128]{1,0:T(8,128)(2,1)S(1)}, bf16[256,128]{1,0:T(8,128)(2,1)S(1)}, u32[]{:S(2)}, u32[]{:S(2)}) %collective-permute-start.6) | collective-permute-done | bytes 65568 | tf_op jit(solution)/shard_map/ppermute | solution.py:337
  26.8 0.1 multiply_convert_fusion.1.cross_ref
  26.8 0.1 collective-permute-start.11
  26.9 0.0 collective-permute-done.12.amps_ref
  26.9 1.0 %other_weight.1 = (bf16[256,4096]{1,0:T(8,128)(2,1)S(1)}, f32[1,4096]{1,0:T(1,128)S(1)}) custom-call(s32[1,32]{1,0:T(1,128)S(1)} %collective-permute-done.other_screen_ref.screen_ref, bf16[272,128]{1,0:T(8,128)(2,1)S(1)} %collective-permute-done.12.amps_ref, bf16[256,4096]{1,0:T(8,128)(2,1)S(1)} %collective-permute-done.1.other_ref.own_ref, ...), custom_call_target="tpu_custom_call" | custom-call | flops 536870912 | bytes 6291456 | tf_op jit(solution)/shard_map/other_weight/pallas_call | solution.py:270
  27.9 0.2 collective-permute-done.11.other_cross_ref
  28.1 1.9 %gamma_and_virial.1 = (bf16[256,4096]{1,0:T(8,128)(2,1)}, f32[9,4096]{1,0:T(8,128)}) custom-call(bf16[256,128]{1,0:T(8,128)(2,1)S(1)} %multiply_convert_fusion.1.cross_ref, bf16[256,128]{1,0:T(8,128)(2,1)S(1)} %collective-permute-done.11.other_cross_ref, bf16[256,4096]{1,0:T(8,128)(2,1)S(1)} %get-tuple-element.40.own_ref, ...), custom_call_target="tpu_custom_call" | custom-call | flops 536870912 | bytes 8388608 | tf_op jit(solution)/shard_map/gamma_and_virial/pallas_call | solution.py:304
  (8 shorter events, 0.2 us)
Async XLA Ops:
  0.6 6.7 %copy-start = (s32[1,32]{1,0:T(1,128)S(1)}, s32[1,32]{1,0:T(1,128)}, u32[]{:S(2)}) copy-start(s32[1,32]{1,0:T(1,128)} %screen_ref.3) | copy-start | bytes 388
  0.6 6.7 %copy-start.1 = (bf16[256]{0:T(256)(128)(2,1)S(1)}, bf16[256]{0:T(256)(128)(2,1)}, u32[]{:S(2)}) copy-start(bf16[256]{0:T(256)(128)(2,1)} %param.8) | copy-start | bytes 1540
  0.7 6.7 %collective-permute-start.1 = (bf16[256,4096]{1,0:T(8,128)(2,1)}, bf16[256,4096]{1,0:T(8,128)(2,1)S(1)}, u32[]{:S(2)}, u32[]{:S(2)}) collective-permute-start(bf16[256,4096]{1,0:T(8,128)(2,1)} %bitcast.7), channel_id=1, source_target_pairs={{0,16},{16,0},{1,17},{17,1},{2,18},{18,2},{3,19},{19,3},{4,20},{20... | collective-permute-start | bytes 6291464 | tf_op jit(solution)/shard_map/ppermute | solution.py:328
  1.2 6.2 %collective-permute-start = (s32[1,32]{1,0:T(1,128)}, s32[1,32]{1,0:T(1,128)S(1)}, u32[]{:S(2)}, u32[]{:S(2)}) collective-permute-start(s32[1,32]{1,0:T(1,128)} %screen_ref.3), channel_id=1, source_target_pairs={{0,16},{16,0},{1,17},{17,1},{2,18},{18,2},{3,19},{19,3},{4,20},{20... | collective-permute-start | bytes 392 | tf_op jit(solution)/shard_map/ppermute | solution.py:328
  3.7 5.9 %collective-permute-start.7 = (bf16[272,128]{1,0:T(8,128)(2,1)S(1)}, bf16[272,128]{1,0:T(8,128)(2,1)S(1)}, u32[]{:S(2)}, u32[]{:S(2)}) collective-permute-start(bf16[272,128]{1,0:T(8,128)(2,1)S(1)} %get-tuple-element.35), channel_id=1, source_target_pairs={{0,1},{1,0},{2,3},{3,2},{4,5},{5,4},{6,7},{7,6},{8,9},{9,8},{10,11... | collective-permute-start | bytes 208904 | tf_op jit(solution)/shard_map/ppermute | solution.py:337
  8.2 4.1 %collective-permute-start.4 = (bf16[128]{0:T(256)(128)(2,1)S(1)}, bf16[128]{0:T(256)(128)(2,1)S(1)}, u32[]{:S(2)}, u32[]{:S(2)}) collective-permute-start(bf16[128]{0:T(256)(128)(2,1)S(1)} %pad.4), channel_id=1, source_target_pairs={{0,16},{16,0},{1,17},{17,1},{2,18},{18,2},{3,19},{19,3},{4,20},{20... | collective-permute-start | bytes 776 | tf_op jit(solution)/shard_map/ppermute | solution.py:328
  8.3 4.3 %collective-permute-start.2 = (bf16[256,128]{1,0:T(8,128)(2,1)S(1)}, bf16[256,128]{1,0:T(8,128)(2,1)S(1)}, u32[]{:S(2)}, u32[]{:S(2)}) collective-permute-start(bf16[256,128]{1,0:T(8,128)(2,1)S(1)} %get-tuple-element.28), channel_id=1, source_target_pairs={{0,1},{1,0},{2,3},{3,2},{4,5},{5,4},{6,7},{7,6},{8,9},{9,8},{10,11... | collective-permute-start | bytes 196616 | tf_op jit(solution)/shard_map/ppermute | solution.py:337
  9.6 5.3 %collective-permute-start.8 = (bf16[272,128]{1,0:T(8,128)(2,1)S(1)}, bf16[272,128]{1,0:T(8,128)(2,1)S(1)}, u32[]{:S(2)}, u32[]{:S(2)}) collective-permute-start(bf16[272,128]{1,0:T(8,128)(2,1)S(1)} %fusion), channel_id=1, source_target_pairs={{0,8},{1,9},{2,10},{3,11},{4,12},{5,13},{6,14},{7,15},{8,0},{9,1},... | collective-permute-start | bytes 208904 | tf_op jit(solution)/shard_map/ppermute | solution.py:337
  12.6 4.3 %collective-permute-start.3 = (bf16[256,128]{1,0:T(8,128)(2,1)S(1)}, bf16[256,128]{1,0:T(8,128)(2,1)S(1)}, u32[]{:S(2)}, u32[]{:S(2)}) collective-permute-start(bf16[256,128]{1,0:T(8,128)(2,1)S(1)} %fusion.2), channel_id=1, source_target_pairs={{0,2},{1,3},{2,0},{3,1},{4,6},{5,7},{6,4},{7,5},{8,10},{9,11},{10,... | collective-permute-start | bytes 196616 | tf_op jit(solution)/shard_map/ppermute | solution.py:337
  14.9 4.4 %collective-permute-start.9 = (bf16[272,128]{1,0:T(8,128)(2,1)S(1)}, bf16[272,128]{1,0:T(8,128)(2,1)S(1)}, u32[]{:S(2)}, u32[]{:S(2)}) collective-permute-start(bf16[272,128]{1,0:T(8,128)(2,1)S(1)} %fusion.5), channel_id=1, source_target_pairs={{0,4},{1,5},{2,6},{3,7},{4,0},{5,1},{6,2},{7,3},{8,12},{9,13},{10,... | collective-permute-start | bytes 208904 | tf_op jit(solution)/shard_map/ppermute | solution.py:337
  17.0 4.5 %collective-permute-start.5 = (bf16[256,128]{1,0:T(8,128)(2,1)S(1)}, bf16[256,128]{1,0:T(8,128)(2,1)S(1)}, u32[]{:S(2)}, u32[]{:S(2)}) collective-permute-start(bf16[256,128]{1,0:T(8,128)(2,1)S(1)} %fusion.4), channel_id=1, source_target_pairs={{0,4},{1,5},{2,6},{3,7},{4,0},{5,1},{6,2},{7,3},{8,12},{9,13},{10,... | collective-permute-start | bytes 196616 | tf_op jit(solution)/shard_map/ppermute | solution.py:337
  19.3 4.9 %collective-permute-start.10 = (bf16[272,128]{1,0:T(8,128)(2,1)S(1)}, bf16[272,128]{1,0:T(8,128)(2,1)S(1)}, u32[]{:S(2)}, u32[]{:S(2)}) collective-permute-start(bf16[272,128]{1,0:T(8,128)(2,1)S(1)} %fusion.1), channel_id=1, source_target_pairs={{0,2},{1,3},{2,0},{3,1},{4,6},{5,7},{6,4},{7,5},{8,10},{9,11},{10,... | collective-permute-start | bytes 208904 | tf_op jit(solution)/shard_map/ppermute | solution.py:337
  21.5 5.2 %collective-permute-start.6 = (bf16[256,128]{1,0:T(8,128)(2,1)S(1)}, bf16[256,128]{1,0:T(8,128)(2,1)S(1)}, u32[]{:S(2)}, u32[]{:S(2)}) collective-permute-start(bf16[256,128]{1,0:T(8,128)(2,1)S(1)} %fusion.3), channel_id=1, source_target_pairs={{0,8},{1,9},{2,10},{3,11},{4,12},{5,13},{6,14},{7,15},{8,0},{9,1},... | collective-permute-start | bytes 196616 | tf_op jit(solution)/shard_map/ppermute | solution.py:337
  24.3 2.6 %collective-permute-start.12 = (bf16[272,128]{1,0:T(8,128)(2,1)S(1)}, bf16[272,128]{1,0:T(8,128)(2,1)S(1)}, u32[]{:S(2)}, u32[]{:S(2)}) collective-permute-start(bf16[272,128]{1,0:T(8,128)(2,1)S(1)} %multiply_convert_fusion.amps_ref), channel_id=1, source_target_pairs={{0,16},{16,0},{1,17},{17,1},{2,18},{18,2},{3,19},{19,3},{4,20},{20... | collective-permute-start | bytes 208904 | tf_op jit(solution)/shard_map/ppermute | solution.py:328
  26.8 1.3 %collective-permute-start.11 = (bf16[256,128]{1,0:T(8,128)(2,1)S(1)}, bf16[256,128]{1,0:T(8,128)(2,1)S(1)}, u32[]{:S(2)}, u32[]{:S(2)}) collective-permute-start(bf16[256,128]{1,0:T(8,128)(2,1)S(1)} %multiply_convert_fusion.1.cross_ref), channel_id=1, source_target_pairs={{0,16},{16,0},{1,17},{17,1},{2,18},{18,2},{3,19},{19,3},{4,20},{20... | collective-permute-start | bytes 196616 | tf_op jit(solution)/shard_map/ppermute | solution.py:328

commit v5 on v4

--- a/solution.py
+++ b/solution.py
@@ -351,26 +351,28 @@
         turned = bits[1:] + bits[:1]
         return (bits, turned), (bits, turned)
     x, y, z, w = bits
-    return ([x, y, z, w], [y, x, w, z]), ([x, w, z, y], [y, z, w, x])
+    return ([z, y, x, w], [z, x, w, y]), ([x, y, z, w], [y, z, x, w])
 
 
 def two_occ_body(n_aux, coeffs, occ_energy, virt_energy, screen, owner, positions):
     raw = coeffs[0]
     other_screen = swap(screen, "occ", 2, 1)
+    other_one = swap(occ_energy, "occ", 2, 1)
     other = swap(raw, "occ", 2, 1)
     cross_orders, own_orders = orders_of([1 << k for k in range(n_aux.bit_length() - 1)])
     own, factor, own_sum, own_send = own_pairs(raw, screen, owner, positions)
     cross_sum, cross_send = cross_pairs(own, other, screen, other_screen)
     rounds = len(own_orders[0])
-    energy = jnp.pad(occ_energy, (0, LANES - 1))
-    cross_send, energy = after(cross_send, energy)
-    other_energy = swap(energy, "occ", 2, 1)
-    inverses = inverse_spreads(virt_energy, energy, other_energy)
     first_cross = cross_send
+    _, other_one = after(first_cross, other_one)
+    other_energy = jnp.pad(other_one, (0, LANES - 1))
     for step in range(rounds):
         if step == 1:
             own_send, _ = after(own_send, first_cross)
-        if step == rounds // 2:
+            cross_send, other_energy = after(cross_send, other_energy)
+            energy = swap(other_energy, "occ", 2, 1)
+            inverses = inverse_spreads(virt_energy, energy, other_energy)
+        if step == max(rounds // 2, 1):
             cross_send, inverses = after(cross_send, inverses)
         own_sum, own_send = one_round(own_sum, own_send, n_aux, [o[step] for o in own_orders])
         cross_sum, cross_send = one_round(
@@ -427,7 +429,7 @@
 
     def body(coeffs, *rest):
         even_halves = coeffs.shape[1] % (2 * LANES) == 0
-        fits = n_occ == 2 and coeffs.shape[0] == 1 and power_of_two and even_halves
+        fits = n_occ == 2 and coeffs.shape[0] == 1 and power_of_two and n_aux > 2 and even_halves
         chosen = two_occ_body if fits else general_body
         return chosen(n_aux, coeffs, *rest)
 

time: 30.2 us -> 29.9 us (0.990)
  between operations: 1.46 us -> 0.79 us
  local copies, waits for them, and re-layouts: 0.02 us -> 0.64 us
    ppermute x8, starting transfers between devices: 17 us -> 15.9 us  [swap_by_core(): return lax.ppermute(array, ('occ', 'aux'), pairs)]
    ppermute x5 -> x6, starting transfers between devices: 0.81 us -> 1.64 us  [swap(): return lax.ppermute(array, axis, [(i, i ^ bit) for i in range(size)])]
    pad x1, local copies, waits for them, and re-layouts: 0.01 us -> 0.63 us  [two_occ_body(): other_energy = jnp.pad(other_one, (0, LANES - 1))]
  transfers between devices with their start and end apart: 13 -> 14, of which waited for: 6 -> 5; matrix products, arithmetic and copies ran while one was open for 1% -> 3% of each run, Pallas kernels for 17% -> 18%
where the time goes in v5:
time: 29.9 us; the launch traced here: 29.7 us
  starting transfers between devices  17.5 us (59%)
  Pallas kernels  7.16 us (24%)
  waiting for transfers between devices  3.34 us (11%)
  between operations  0.79 us (3%)
  local copies, waits for them, and re-layouts  0.64 us (2%)
  other arithmetic  0.3 us (1%)
    ppermute x8, starting transfers between devices, swap_by_core(): return lax.ppermute(array, ('occ', 'aux'), pairs)  15.9 us
    ppermute x8, waiting for transfers between devices, swap_by_core(): return lax.ppermute(array, ('occ', 'aux'), pairs)  3.32 us
    pallas_call x1, Pallas kernels, own_pairs(): pl.pallas_call(functools.partial(own_pairs_kernel, blocks, aux_dev // blo...  2.4 us
    pallas_call x2, Pallas kernels, gamma_call(): pl.pallas_call(functools.partial(kernel, steps, blocks, aux_dev // blocks...  1.93 us
    pallas_call x1, Pallas kernels, gamma_and_virial(): pl.pallas_call(functools.partial(gamma_kernel, steps), in_specs=[vmem] *...  1.9 us
    ppermute x6, starting transfers between devices, swap(): return lax.ppermute(array, axis, [(i, i ^ bit) for i in range(size)])  1.64 us
    pallas_call x1, Pallas kernels, cross_pairs(): pl.pallas_call(functools.partial(cross_pairs_kernel, blocks, aux_dev // b...  0.82 us
    pad x1, local copies, waits for them, and re-layouts, two_occ_body(): other_energy = jnp.pad(other_one, (0, LANES - 1))  0.63 us
  transfers between devices with their start and end apart: 14, of which 5 were waited for; matrix products, arithmetic and copies ran while one was open for 3% of the time, Pallas kernels for 18%

profile of v5, /device:TPU:0, one launch (start us, length us, event | category | flops | bytes accessed | tf_op | source)
XLA Modules:
  0.0 29.7 jit_solution(15267948348707251053)
XLA Ops:
  0.6 0.0 copy-start
  0.6 0.5 %collective-permute-start.1 = (bf16[256,4096]{1,0:T(8,128)(2,1)}, bf16[256,4096]{1,0:T(8,128)(2,1)S(1)}, u32[]{:S(2)}, u32[]{:S(2)}) collective-permute-start(bf16[256,4096]{1,0:T(8,128)(2,1)} %bitcast.7), channel_id=1, source_target_pairs={{0,16},{16,0},{1,17},{17,1},{2,18},{18,2},{3,19},{19,3},{4,20},{20... | collective-permute-start | bytes 6291464 | tf_op jit(solution)/shard_map/ppermute | solution.py:328
  1.2 0.1 collective-permute-start
  1.2 0.4 %collective-permute-start.3 = (bf16[1]{0:T(256)(128)(2,1)}, bf16[1]{0:T(256)(128)(2,1)}, u32[]{:S(2)}, u32[]{:S(2)}) collective-permute-start(bf16[1]{0:T(256)(128)(2,1)} %param.7), channel_id=1, source_target_pairs={{0,16},{16,0},{1,17},{17,1},{2,18},{18,2},{3,19},{19,3},{4,20},{20... | collective-permute-start | bytes 14 | tf_op jit(solution)/shard_map/ppermute | solution.py:328
  1.7 2.4 %own_pairs.1 = (bf16[256,4096]{1,0:T(8,128)(2,1)S(1)}, f32[9,4096]{1,0:T(8,128)S(1)}, f32[272,128]{1,0:T(8,128)S(1)}, bf16[272,128]{1,0:T(8,128)(2,1)S(1)}) custom-call(s32[1,32]{1,0:T(1,128)} %screen_ref.3, s32[1,32]{1,0:T(1,128)} %bitcast.9, f32[3,128]{1,0:T(4,128)} %positions_hbm.1, bf16[256,4096]{1,0:T(8,128)(2,1)} %bitcast.8), custom_call_target="tpu_custom_call" | custom-call | flops 536870912 | bytes 2097152 | tf_op jit(solution)/shard_map/own_pairs/pallas_call | solution.py:103
  4.1 2.6 %collective-permute-start.8 = (bf16[272,128]{1,0:T(8,128)(2,1)S(1)}, bf16[272,128]{1,0:T(8,128)(2,1)S(1)}, u32[]{:S(2)}, u32[]{:S(2)}) collective-permute-start(bf16[272,128]{1,0:T(8,128)(2,1)S(1)} %get-tuple-element.37), channel_id=1, source_target_pairs={{0,1},{1,0},{2,3},{3,2},{4,5},{5,4},{6,7},{7,6},{8,9},{9,8},{10,11... | collective-permute-start | bytes 208904 | tf_op jit(solution)/shard_map/ppermute | solution.py:337
  6.7 0.0 collective-permute-done.other_screen_ref.screen_ref
  6.7 0.0 collective-permute-done.1.other_ref.own_ref
  6.7 0.0 copy-done
  6.7 0.0 copy-start.1
  6.7 0.8 %cross_pairs.1 = (f32[256,128]{1,0:T(8,128)S(1)}, bf16[256,128]{1,0:T(8,128)(2,1)S(1)}) custom-call(s32[1,32]{1,0:T(1,128)S(1)} %copy-done, s32[1,32]{1,0:T(1,128)S(1)} %collective-permute-done.other_screen_ref.screen_ref, bf16[256,4096]{1,0:T(8,128)(2,1)S(1)} %get-tuple-element.26.own_ref, bf16[256,4096]{1,0:T(8,128)(2,1)S(1)} %collective-permute-done.1.other_ref.own_ref), custom_call_target="tpu_custom_call" | custom-call | flops 2147483648 | bytes 16777216 | tf_op jit(solution)/shard_map/cross_pairs/pallas_call | solution.py:133
  7.6 1.6 %collective-permute-start.2 = (bf16[256,128]{1,0:T(8,128)(2,1)S(1)}, bf16[256,128]{1,0:T(8,128)(2,1)S(1)}, u32[]{:S(2)}, u32[]{:S(2)}) collective-permute-start(bf16[256,128]{1,0:T(8,128)(2,1)S(1)} %get-tuple-element.28), channel_id=1, source_target_pairs={{0,4},{1,5},{2,6},{3,7},{4,0},{5,1},{6,2},{7,3},{8,12},{9,13},{10,... | collective-permute-start | bytes 196616 | tf_op jit(solution)/shard_map/ppermute | solution.py:337
  9.2 0.0 collective-permute-done.8
  9.2 0.0 collective-permute-done.3
  9.2 1.9 %collective-permute-start.9 = (bf16[272,128]{1,0:T(8,128)(2,1)S(1)}, bf16[272,128]{1,0:T(8,128)(2,1)S(1)}, u32[]{:S(2)}, u32[]{:S(2)}) collective-permute-start(bf16[272,128]{1,0:T(8,128)(2,1)S(1)} %fusion), channel_id=1, source_target_pairs={{0,2},{1,3},{2,0},{3,1},{4,6},{5,7},{6,4},{7,5},{8,10},{9,11},{10,... | collective-permute-start | bytes 208904 | tf_op jit(solution)/shard_map/ppermute | solution.py:337
  11.1 0.6 %pad.4 = bf16[128]{0:T(256)(128)(2,1)S(1)} pad(bf16[1]{0:T(256)(128)(2,1)} %collective-permute-done.3, bf16[]{:T(256)} %constant.2.clone.1), padding=0_127 | pad | bytes 260 | tf_op jit(solution)/shard_map/jit(_pad)/pad | solution.py:368
  11.8 0.3 collective-permute-done.2
  12.1 0.1 collective-permute-start.5
  12.1 0.0 copy-done.1
  12.2 1.6 %collective-permute-start.4 = (bf16[256,128]{1,0:T(8,128)(2,1)S(1)}, bf16[256,128]{1,0:T(8,128)(2,1)S(1)}, u32[]{:S(2)}, u32[]{:S(2)}) collective-permute-start(bf16[256,128]{1,0:T(8,128)(2,1)S(1)} %fusion.2), channel_id=1, source_target_pairs={{0,2},{1,3},{2,0},{3,1},{4,6},{5,7},{6,4},{7,5},{8,10},{9,11},{10,... | collective-permute-start | bytes 196616 | tf_op jit(solution)/shard_map/ppermute | solution.py:337
  13.8 0.0 collective-permute-done.5
  13.8 0.1 inverse_spreads.1
  13.9 0.0 collective-permute-done.9
  13.9 1.7 %collective-permute-start.10 = (bf16[272,128]{1,0:T(8,128)(2,1)S(1)}, bf16[272,128]{1,0:T(8,128)(2,1)S(1)}, u32[]{:S(2)}, u32[]{:S(2)}) collective-permute-start(bf16[272,128]{1,0:T(8,128)(2,1)S(1)} %fusion.5), channel_id=1, source_target_pairs={{0,4},{1,5},{2,6},{3,7},{4,0},{5,1},{6,2},{7,3},{8,12},{9,13},{10,... | collective-permute-start | bytes 208904 | tf_op jit(solution)/shard_map/ppermute | solution.py:337
  15.6 0.9 %collective-permute-done.4 = bf16[256,128]{1,0:T(8,128)(2,1)S(1)} collective-permute-done((bf16[256,128]{1,0:T(8,128)(2,1)S(1)}, bf16[256,128]{1,0:T(8,128)(2,1)S(1)}, u32[]{:S(2)}, u32[]{:S(2)}) %collective-permute-start.4) | collective-permute-done | bytes 65568 | tf_op jit(solution)/shard_map/ppermute | solution.py:337
  16.5 1.3 %collective-permute-start.6 = (bf16[256,128]{1,0:T(8,128)(2,1)S(1)}, bf16[256,128]{1,0:T(8,128)(2,1)S(1)}, u32[]{:S(2)}, u32[]{:S(2)}) collective-permute-start(bf16[256,128]{1,0:T(8,128)(2,1)S(1)} %fusion.4), channel_id=1, source_target_pairs={{0,1},{1,0},{2,3},{3,2},{4,5},{5,4},{6,7},{7,6},{8,9},{9,8},{10,11... | collective-permute-start | bytes 196616 | tf_op jit(solution)/shard_map/ppermute | solution.py:337
  17.8 0.5 %collective-permute-done.10 = bf16[272,128]{1,0:T(8,128)(2,1)S(1)} collective-permute-done((bf16[272,128]{1,0:T(8,128)(2,1)S(1)}, bf16[272,128]{1,0:T(8,128)(2,1)S(1)}, u32[]{:S(2)}, u32[]{:S(2)}) %collective-permute-start.10) | collective-permute-done | bytes 69664 | tf_op jit(solution)/shard_map/ppermute | solution.py:337
  18.3 2.7 %collective-permute-start.11 = (bf16[272,128]{1,0:T(8,128)(2,1)S(1)}, bf16[272,128]{1,0:T(8,128)(2,1)S(1)}, u32[]{:S(2)}, u32[]{:S(2)}) collective-permute-start(bf16[272,128]{1,0:T(8,128)(2,1)S(1)} %fusion.1), channel_id=1, source_target_pairs={{0,8},{1,9},{2,10},{3,11},{4,12},{5,13},{6,14},{7,15},{8,0},{9,1},... | collective-permute-start | bytes 208904 | tf_op jit(solution)/shard_map/ppermute | solution.py:337
  21.0 0.0 collective-permute-done.6
  21.1 2.4 %collective-permute-start.7 = (bf16[256,128]{1,0:T(8,128)(2,1)S(1)}, bf16[256,128]{1,0:T(8,128)(2,1)S(1)}, u32[]{:S(2)}, u32[]{:S(2)}) collective-permute-start(bf16[256,128]{1,0:T(8,128)(2,1)S(1)} %fusion.3), channel_id=1, source_target_pairs={{0,8},{1,9},{2,10},{3,11},{4,12},{5,13},{6,14},{7,15},{8,0},{9,1},... | collective-permute-start | bytes 196616 | tf_op jit(solution)/shard_map/ppermute | solution.py:337
  23.5 1.6 %collective-permute-done.11 = bf16[272,128]{1,0:T(8,128)(2,1)S(1)} collective-permute-done((bf16[272,128]{1,0:T(8,128)(2,1)S(1)}, bf16[272,128]{1,0:T(8,128)(2,1)S(1)}, u32[]{:S(2)}, u32[]{:S(2)}) %collective-permute-start.11) | collective-permute-done | bytes 69664 | tf_op jit(solution)/shard_map/ppermute | solution.py:337
  25.1 0.1 multiply_convert_fusion.amps_ref
  25.2 0.1 collective-permute-start.13
  25.3 1.0 %own_gamma.1 = (bf16[256,4096]{1,0:T(8,128)(2,1)S(1)}, f32[256,4096]{1,0:T(8,128)S(1)}, f32[1,4096]{1,0:T(1,128)S(1)}) custom-call(s32[1,32]{1,0:T(1,128)S(1)} %copy-done, bf16[272,128]{1,0:T(8,128)(2,1)S(1)} %multiply_convert_fusion.amps_ref, bf16[256,4096]{1,0:T(8,128)(2,1)S(1)} %get-tuple-element.26.own_ref), custom_call_target="tpu_custom_call" | custom-call | flops 536870912 | bytes 6291456 | tf_op jit(solution)/shard_map/own_gamma/pallas_call | solution.py:270
  26.2 0.1 collective-permute-done.7
  26.3 0.1 multiply_convert_fusion.1.cross_ref
  26.4 0.5 %collective-permute-start.12 = (bf16[256,128]{1,0:T(8,128)(2,1)S(1)}, bf16[256,128]{1,0:T(8,128)(2,1)S(1)}, u32[]{:S(2)}, u32[]{:S(2)}) collective-permute-start(bf16[256,128]{1,0:T(8,128)(2,1)S(1)} %multiply_convert_fusion.1.cross_ref), channel_id=1, source_target_pairs={{0,16},{16,0},{1,17},{17,1},{2,18},{18,2},{3,19},{19,3},{4,20},{20... | collective-permute-start | bytes 196616 | tf_op jit(solution)/shard_map/ppermute | solution.py:328
  26.8 0.0 collective-permute-done.13.amps_ref
  26.8 1.0 %other_weight.1 = (bf16[256,4096]{1,0:T(8,128)(2,1)S(1)}, f32[1,4096]{1,0:T(1,128)S(1)}) custom-call(s32[1,32]{1,0:T(1,128)S(1)} %collective-permute-done.other_screen_ref.screen_ref, bf16[272,128]{1,0:T(8,128)(2,1)S(1)} %collective-permute-done.13.amps_ref, bf16[256,4096]{1,0:T(8,128)(2,1)S(1)} %collective-permute-done.1.other_ref.own_ref, ...), custom_call_target="tpu_custom_call" | custom-call | flops 536870912 | bytes 6291456 | tf_op jit(solution)/shard_map/other_weight/pallas_call | solution.py:270
  27.8 0.0 collective-permute-done.12.other_cross_ref
  27.8 1.9 %gamma_and_virial.1 = (bf16[256,4096]{1,0:T(8,128)(2,1)}, f32[9,4096]{1,0:T(8,128)}) custom-call(bf16[256,128]{1,0:T(8,128)(2,1)S(1)} %multiply_convert_fusion.1.cross_ref, bf16[256,128]{1,0:T(8,128)(2,1)S(1)} %collective-permute-done.12.other_cross_ref, bf16[256,4096]{1,0:T(8,128)(2,1)S(1)} %get-tuple-element.42.own_ref, ...), custom_call_target="tpu_custom_call" | custom-call | flops 536870912 | bytes 8388608 | tf_op jit(solution)/shard_map/gamma_and_virial/pallas_call | solution.py:304
  (7 shorter events, 0.2 us)
Async XLA Ops:
  0.6 6.1 %copy-start = (s32[1,32]{1,0:T(1,128)S(1)}, s32[1,32]{1,0:T(1,128)}, u32[]{:S(2)}) copy-start(s32[1,32]{1,0:T(1,128)} %screen_ref.3) | copy-start | bytes 388
  0.6 6.1 %collective-permute-start.1 = (bf16[256,4096]{1,0:T(8,128)(2,1)}, bf16[256,4096]{1,0:T(8,128)(2,1)S(1)}, u32[]{:S(2)}, u32[]{:S(2)}) collective-permute-start(bf16[256,4096]{1,0:T(8,128)(2,1)} %bitcast.7), channel_id=1, source_target_pairs={{0,16},{16,0},{1,17},{17,1},{2,18},{18,2},{3,19},{19,3},{4,20},{20... | collective-permute-start | bytes 6291464 | tf_op jit(solution)/shard_map/ppermute | solution.py:328
  1.2 5.5 %collective-permute-start = (s32[1,32]{1,0:T(1,128)}, s32[1,32]{1,0:T(1,128)S(1)}, u32[]{:S(2)}, u32[]{:S(2)}) collective-permute-start(s32[1,32]{1,0:T(1,128)} %screen_ref.3), channel_id=1, source_target_pairs={{0,16},{16,0},{1,17},{17,1},{2,18},{18,2},{3,19},{19,3},{4,20},{20... | collective-permute-start | bytes 392 | tf_op jit(solution)/shard_map/ppermute | solution.py:328
  1.2 8.0 %collective-permute-start.3 = (bf16[1]{0:T(256)(128)(2,1)}, bf16[1]{0:T(256)(128)(2,1)}, u32[]{:S(2)}, u32[]{:S(2)}) collective-permute-start(bf16[1]{0:T(256)(128)(2,1)} %param.7), channel_id=1, source_target_pairs={{0,16},{16,0},{1,17},{17,1},{2,18},{18,2},{3,19},{19,3},{4,20},{20... | collective-permute-start | bytes 14 | tf_op jit(solution)/shard_map/ppermute | solution.py:328
  4.1 5.1 %collective-permute-start.8 = (bf16[272,128]{1,0:T(8,128)(2,1)S(1)}, bf16[272,128]{1,0:T(8,128)(2,1)S(1)}, u32[]{:S(2)}, u32[]{:S(2)}) collective-permute-start(bf16[272,128]{1,0:T(8,128)(2,1)S(1)} %get-tuple-element.37), channel_id=1, source_target_pairs={{0,1},{1,0},{2,3},{3,2},{4,5},{5,4},{6,7},{7,6},{8,9},{9,8},{10,11... | collective-permute-start | bytes 208904 | tf_op jit(solution)/shard_map/ppermute | solution.py:337
  6.7 5.4 %copy-start.1 = (bf16[256]{0:T(256)(128)(2,1)S(1)}, bf16[256]{0:T(256)(128)(2,1)}, u32[]{:S(2)}) copy-start(bf16[256]{0:T(256)(128)(2,1)} %param.8) | copy-start | bytes 1540
  7.6 4.5 %collective-permute-start.2 = (bf16[256,128]{1,0:T(8,128)(2,1)S(1)}, bf16[256,128]{1,0:T(8,128)(2,1)S(1)}, u32[]{:S(2)}, u32[]{:S(2)}) collective-permute-start(bf16[256,128]{1,0:T(8,128)(2,1)S(1)} %get-tuple-element.28), channel_id=1, source_target_pairs={{0,4},{1,5},{2,6},{3,7},{4,0},{5,1},{6,2},{7,3},{8,12},{9,13},{10,... | collective-permute-start | bytes 196616 | tf_op jit(solution)/shard_map/ppermute | solution.py:337
  9.2 4.7 %collective-permute-start.9 = (bf16[272,128]{1,0:T(8,128)(2,1)S(1)}, bf16[272,128]{1,0:T(8,128)(2,1)S(1)}, u32[]{:S(2)}, u32[]{:S(2)}) collective-permute-start(bf16[272,128]{1,0:T(8,128)(2,1)S(1)} %fusion), channel_id=1, source_target_pairs={{0,2},{1,3},{2,0},{3,1},{4,6},{5,7},{6,4},{7,5},{8,10},{9,11},{10,... | collective-permute-start | bytes 208904 | tf_op jit(solution)/shard_map/ppermute | solution.py:337
  12.1 1.7 %collective-permute-start.5 = (bf16[128]{0:T(256)(128)(2,1)S(1)}, bf16[128]{0:T(256)(128)(2,1)S(1)}, u32[]{:S(2)}, u32[]{:S(2)}) collective-permute-start(bf16[128]{0:T(256)(128)(2,1)S(1)} %pad.4), channel_id=1, source_target_pairs={{0,16},{16,0},{1,17},{17,1},{2,18},{18,2},{3,19},{19,3},{4,20},{20... | collective-permute-start | bytes 776 | tf_op jit(solution)/shard_map/ppermute | solution.py:328
  12.2 4.3 %collective-permute-start.4 = (bf16[256,128]{1,0:T(8,128)(2,1)S(1)}, bf16[256,128]{1,0:T(8,128)(2,1)S(1)}, u32[]{:S(2)}, u32[]{:S(2)}) collective-permute-start(bf16[256,128]{1,0:T(8,128)(2,1)S(1)} %fusion.2), channel_id=1, source_target_pairs={{0,2},{1,3},{2,0},{3,1},{4,6},{5,7},{6,4},{7,5},{8,10},{9,11},{10,... | collective-permute-start | bytes 196616 | tf_op jit(solution)/shard_map/ppermute | solution.py:337
  13.9 4.4 %collective-permute-start.10 = (bf16[272,128]{1,0:T(8,128)(2,1)S(1)}, bf16[272,128]{1,0:T(8,128)(2,1)S(1)}, u32[]{:S(2)}, u32[]{:S(2)}) collective-permute-start(bf16[272,128]{1,0:T(8,128)(2,1)S(1)} %fusion.5), channel_id=1, source_target_pairs={{0,4},{1,5},{2,6},{3,7},{4,0},{5,1},{6,2},{7,3},{8,12},{9,13},{10,... | collective-permute-start | bytes 208904 | tf_op jit(solution)/shard_map/ppermute | solution.py:337
  16.5 4.5 %collective-permute-start.6 = (bf16[256,128]{1,0:T(8,128)(2,1)S(1)}, bf16[256,128]{1,0:T(8,128)(2,1)S(1)}, u32[]{:S(2)}, u32[]{:S(2)}) collective-permute-start(bf16[256,128]{1,0:T(8,128)(2,1)S(1)} %fusion.4), channel_id=1, source_target_pairs={{0,1},{1,0},{2,3},{3,2},{4,5},{5,4},{6,7},{7,6},{8,9},{9,8},{10,11... | collective-permute-start | bytes 196616 | tf_op jit(solution)/shard_map/ppermute | solution.py:337
  18.3 6.8 %collective-permute-start.11 = (bf16[272,128]{1,0:T(8,128)(2,1)S(1)}, bf16[272,128]{1,0:T(8,128)(2,1)S(1)}, u32[]{:S(2)}, u32[]{:S(2)}) collective-permute-start(bf16[272,128]{1,0:T(8,128)(2,1)S(1)} %fusion.1), channel_id=1, source_target_pairs={{0,8},{1,9},{2,10},{3,11},{4,12},{5,13},{6,14},{7,15},{8,0},{9,1},... | collective-permute-start | bytes 208904 | tf_op jit(solution)/shard_map/ppermute | solution.py:337
  21.1 5.2 %collective-permute-start.7 = (bf16[256,128]{1,0:T(8,128)(2,1)S(1)}, bf16[256,128]{1,0:T(8,128)(2,1)S(1)}, u32[]{:S(2)}, u32[]{:S(2)}) collective-permute-start(bf16[256,128]{1,0:T(8,128)(2,1)S(1)} %fusion.3), channel_id=1, source_target_pairs={{0,8},{1,9},{2,10},{3,11},{4,12},{5,13},{6,14},{7,15},{8,0},{9,1},... | collective-permute-start | bytes 196616 | tf_op jit(solution)/shard_map/ppermute | solution.py:337
  25.2 1.7 %collective-permute-start.13 = (bf16[272,128]{1,0:T(8,128)(2,1)S(1)}, bf16[272,128]{1,0:T(8,128)(2,1)S(1)}, u32[]{:S(2)}, u32[]{:S(2)}) collective-permute-start(bf16[272,128]{1,0:T(8,128)(2,1)S(1)} %multiply_convert_fusion.amps_ref), channel_id=1, source_target_pairs={{0,16},{16,0},{1,17},{17,1},{2,18},{18,2},{3,19},{19,3},{4,20},{20... | collective-permute-start | bytes 208904 | tf_op jit(solution)/shard_map/ppermute | solution.py:328
  26.4 1.5 %collective-permute-start.12 = (bf16[256,128]{1,0:T(8,128)(2,1)S(1)}, bf16[256,128]{1,0:T(8,128)(2,1)S(1)}, u32[]{:S(2)}, u32[]{:S(2)}) collective-permute-start(bf16[256,128]{1,0:T(8,128)(2,1)S(1)} %multiply_convert_fusion.1.cross_ref), channel_id=1, source_target_pairs={{0,16},{16,0},{1,17},{17,1},{2,18},{18,2},{3,19},{19,3},{4,20},{20... | collective-permute-start | bytes 196616 | tf_op jit(solution)/shard_map/ppermute | solution.py:328

commit v6 on v5

--- a/solution.py
+++ b/solution.py
@@ -254,6 +254,9 @@
             )
         )
         copies[step].start()
+    for step in range(steps):
+        columns = pl.ds(step * tile, tile)
+        cross = jnp.dot(amps[...], other_ref[:, columns], preferred_element_type=F32)
         twice = jnp.sum(cross * own_ref[:, columns].astype(F32), axis=0, keepdims=True)
         virial_ref[:, columns] = factor_ref[:, columns] * (weight_ref[:, columns] + 2.0 * twice)
     copies.append(pltpu.make_async_copy(virial_ref, virial_hbm, virial_sem))

time: 29.9 us -> 30.2 us (1.010)
  Pallas kernels: 7.16 us -> 7.49 us
    pallas_call x1, Pallas kernels: 1.9 us -> 2.23 us  [gamma_and_virial(): pl.pallas_call(functools.partial(gamma_kernel, steps), in_specs=[vmem] *...]
  transfers between devices with their start and end apart: 14 -> 14, of which waited for: 5 -> 5; matrix products, arithmetic and copies ran while one was open for 3% -> 3% of each run, Pallas kernels for 18% -> 17%
where the time goes in v6:
time: 30.2 us; the launch traced here: 30.1 us
  starting transfers between devices  17.5 us (58%)
  Pallas kernels  7.49 us (25%)
  waiting for transfers between devices  3.34 us (11%)
  between operations  0.79 us (3%)
  local copies, waits for them, and re-layouts  0.64 us (2%)
    ppermute x8, starting transfers between devices, swap_by_core(): return lax.ppermute(array, ('occ', 'aux'), pairs)  15.9 us
    ppermute x8, waiting for transfers between devices, swap_by_core(): return lax.ppermute(array, ('occ', 'aux'), pairs)  3.32 us
    pallas_call x1, Pallas kernels, own_pairs(): pl.pallas_call(functools.partial(own_pairs_kernel, blocks, aux_dev // blo...  2.4 us
    pallas_call x1, Pallas kernels, gamma_and_virial(): pl.pallas_call(functools.partial(gamma_kernel, steps), in_specs=[vmem] *...  2.23 us
    pallas_call x2, Pallas kernels, gamma_call(): pl.pallas_call(functools.partial(kernel, steps, blocks, aux_dev // blocks...  1.93 us
    ppermute x6, starting transfers between devices, swap(): return lax.ppermute(array, axis, [(i, i ^ bit) for i in range(size)])  1.64 us
    pallas_call x1, Pallas kernels, cross_pairs(): pl.pallas_call(functools.partial(cross_pairs_kernel, blocks, aux_dev // b...  0.82 us
    pad x1, local copies, waits for them, and re-layouts, two_occ_body(): other_energy = jnp.pad(other_one, (0, LANES - 1))  0.63 us
  transfers between devices with their start and end apart: 14, of which 5 were waited for; matrix products, arithmetic and copies ran while one was open for 3% of the time, Pallas kernels for 17%

profile of v6, /device:TPU:0, one launch (start us, length us, event | category | flops | bytes accessed | tf_op | source)
XLA Modules:
  0.0 30.1 jit_solution(8066231036448540755)
XLA Ops:
  0.6 0.0 copy-start
  0.6 0.5 %collective-permute-start.1 = (bf16[256,4096]{1,0:T(8,128)(2,1)}, bf16[256,4096]{1,0:T(8,128)(2,1)S(1)}, u32[]{:S(2)}, u32[]{:S(2)}) collective-permute-start(bf16[256,4096]{1,0:T(8,128)(2,1)} %bitcast.7), channel_id=1, source_target_pairs={{0,16},{16,0},{1,17},{17,1},{2,18},{18,2},{3,19},{19,3},{4,20},{20... | collective-permute-start | bytes 6291464 | tf_op jit(solution)/shard_map/ppermute | solution.py:331
  1.2 0.1 collective-permute-start
  1.2 0.4 %collective-permute-start.3 = (bf16[1]{0:T(256)(128)(2,1)}, bf16[1]{0:T(256)(128)(2,1)}, u32[]{:S(2)}, u32[]{:S(2)}) collective-permute-start(bf16[1]{0:T(256)(128)(2,1)} %param.7), channel_id=1, source_target_pairs={{0,16},{16,0},{1,17},{17,1},{2,18},{18,2},{3,19},{19,3},{4,20},{20... | collective-permute-start | bytes 14 | tf_op jit(solution)/shard_map/ppermute | solution.py:331
  1.7 2.4 %own_pairs.1 = (bf16[256,4096]{1,0:T(8,128)(2,1)S(1)}, f32[9,4096]{1,0:T(8,128)S(1)}, f32[272,128]{1,0:T(8,128)S(1)}, bf16[272,128]{1,0:T(8,128)(2,1)S(1)}) custom-call(s32[1,32]{1,0:T(1,128)} %screen_ref.3, s32[1,32]{1,0:T(1,128)} %bitcast.9, f32[3,128]{1,0:T(4,128)} %positions_hbm.1, bf16[256,4096]{1,0:T(8,128)(2,1)} %bitcast.8), custom_call_target="tpu_custom_call" | custom-call | flops 536870912 | bytes 2097152 | tf_op jit(solution)/shard_map/own_pairs/pallas_call | solution.py:103
  4.1 2.6 %collective-permute-start.8 = (bf16[272,128]{1,0:T(8,128)(2,1)S(1)}, bf16[272,128]{1,0:T(8,128)(2,1)S(1)}, u32[]{:S(2)}, u32[]{:S(2)}) collective-permute-start(bf16[272,128]{1,0:T(8,128)(2,1)S(1)} %get-tuple-element.37), channel_id=1, source_target_pairs={{0,1},{1,0},{2,3},{3,2},{4,5},{5,4},{6,7},{7,6},{8,9},{9,8},{10,11... | collective-permute-start | bytes 208904 | tf_op jit(solution)/shard_map/ppermute | solution.py:340
  6.7 0.0 collective-permute-done.other_screen_ref.screen_ref
  6.7 0.0 collective-permute-done.1.other_ref.own_ref
  6.7 0.0 copy-done
  6.7 0.0 copy-start.1
  6.7 0.8 %cross_pairs.1 = (f32[256,128]{1,0:T(8,128)S(1)}, bf16[256,128]{1,0:T(8,128)(2,1)S(1)}) custom-call(s32[1,32]{1,0:T(1,128)S(1)} %copy-done, s32[1,32]{1,0:T(1,128)S(1)} %collective-permute-done.other_screen_ref.screen_ref, bf16[256,4096]{1,0:T(8,128)(2,1)S(1)} %get-tuple-element.26.own_ref, bf16[256,4096]{1,0:T(8,128)(2,1)S(1)} %collective-permute-done.1.other_ref.own_ref), custom_call_target="tpu_custom_call" | custom-call | flops 2147483648 | bytes 16777216 | tf_op jit(solution)/shard_map/cross_pairs/pallas_call | solution.py:133
  7.6 1.6 %collective-permute-start.2 = (bf16[256,128]{1,0:T(8,128)(2,1)S(1)}, bf16[256,128]{1,0:T(8,128)(2,1)S(1)}, u32[]{:S(2)}, u32[]{:S(2)}) collective-permute-start(bf16[256,128]{1,0:T(8,128)(2,1)S(1)} %get-tuple-element.28), channel_id=1, source_target_pairs={{0,4},{1,5},{2,6},{3,7},{4,0},{5,1},{6,2},{7,3},{8,12},{9,13},{10,... | collective-permute-start | bytes 196616 | tf_op jit(solution)/shard_map/ppermute | solution.py:340
  9.2 0.0 collective-permute-done.8
  9.2 0.0 collective-permute-done.3
  9.2 1.9 %collective-permute-start.9 = (bf16[272,128]{1,0:T(8,128)(2,1)S(1)}, bf16[272,128]{1,0:T(8,128)(2,1)S(1)}, u32[]{:S(2)}, u32[]{:S(2)}) collective-permute-start(bf16[272,128]{1,0:T(8,128)(2,1)S(1)} %fusion), channel_id=1, source_target_pairs={{0,2},{1,3},{2,0},{3,1},{4,6},{5,7},{6,4},{7,5},{8,10},{9,11},{10,... | collective-permute-start | bytes 208904 | tf_op jit(solution)/shard_map/ppermute | solution.py:340
  11.1 0.6 %pad.4 = bf16[128]{0:T(256)(128)(2,1)S(1)} pad(bf16[1]{0:T(256)(128)(2,1)} %collective-permute-done.3, bf16[]{:T(256)} %constant.2.clone.1), padding=0_127 | pad | bytes 260 | tf_op jit(solution)/shard_map/jit(_pad)/pad | solution.py:371
  11.8 0.3 collective-permute-done.2
  12.1 0.1 collective-permute-start.5
  12.1 0.0 copy-done.1
  12.2 1.6 %collective-permute-start.4 = (bf16[256,128]{1,0:T(8,128)(2,1)S(1)}, bf16[256,128]{1,0:T(8,128)(2,1)S(1)}, u32[]{:S(2)}, u32[]{:S(2)}) collective-permute-start(bf16[256,128]{1,0:T(8,128)(2,1)S(1)} %fusion.2), channel_id=1, source_target_pairs={{0,2},{1,3},{2,0},{3,1},{4,6},{5,7},{6,4},{7,5},{8,10},{9,11},{10,... | collective-permute-start | bytes 196616 | tf_op jit(solution)/shard_map/ppermute | solution.py:340
  13.8 0.0 collective-permute-done.5
  13.8 0.1 inverse_spreads.1
  13.9 0.0 collective-permute-done.9
  13.9 1.7 %collective-permute-start.10 = (bf16[272,128]{1,0:T(8,128)(2,1)S(1)}, bf16[272,128]{1,0:T(8,128)(2,1)S(1)}, u32[]{:S(2)}, u32[]{:S(2)}) collective-permute-start(bf16[272,128]{1,0:T(8,128)(2,1)S(1)} %fusion.5), channel_id=1, source_target_pairs={{0,4},{1,5},{2,6},{3,7},{4,0},{5,1},{6,2},{7,3},{8,12},{9,13},{10,... | collective-permute-start | bytes 208904 | tf_op jit(solution)/shard_map/ppermute | solution.py:340
  15.6 0.9 %collective-permute-done.4 = bf16[256,128]{1,0:T(8,128)(2,1)S(1)} collective-permute-done((bf16[256,128]{1,0:T(8,128)(2,1)S(1)}, bf16[256,128]{1,0:T(8,128)(2,1)S(1)}, u32[]{:S(2)}, u32[]{:S(2)}) %collective-permute-start.4) | collective-permute-done | bytes 65568 | tf_op jit(solution)/shard_map/ppermute | solution.py:340
  16.5 1.3 %collective-permute-start.6 = (bf16[256,128]{1,0:T(8,128)(2,1)S(1)}, bf16[256,128]{1,0:T(8,128)(2,1)S(1)}, u32[]{:S(2)}, u32[]{:S(2)}) collective-permute-start(bf16[256,128]{1,0:T(8,128)(2,1)S(1)} %fusion.4), channel_id=1, source_target_pairs={{0,1},{1,0},{2,3},{3,2},{4,5},{5,4},{6,7},{7,6},{8,9},{9,8},{10,11... | collective-permute-start | bytes 196616 | tf_op jit(solution)/shard_map/ppermute | solution.py:340
  17.8 0.5 %collective-permute-done.10 = bf16[272,128]{1,0:T(8,128)(2,1)S(1)} collective-permute-done((bf16[272,128]{1,0:T(8,128)(2,1)S(1)}, bf16[272,128]{1,0:T(8,128)(2,1)S(1)}, u32[]{:S(2)}, u32[]{:S(2)}) %collective-permute-start.10) | collective-permute-done | bytes 69664 | tf_op jit(solution)/shard_map/ppermute | solution.py:340
  18.3 2.7 %collective-permute-start.11 = (bf16[272,128]{1,0:T(8,128)(2,1)S(1)}, bf16[272,128]{1,0:T(8,128)(2,1)S(1)}, u32[]{:S(2)}, u32[]{:S(2)}) collective-permute-start(bf16[272,128]{1,0:T(8,128)(2,1)S(1)} %fusion.1), channel_id=1, source_target_pairs={{0,8},{1,9},{2,10},{3,11},{4,12},{5,13},{6,14},{7,15},{8,0},{9,1},... | collective-permute-start | bytes 208904 | tf_op jit(solution)/shard_map/ppermute | solution.py:340
  21.0 0.0 collective-permute-done.6
  21.1 2.4 %collective-permute-start.7 = (bf16[256,128]{1,0:T(8,128)(2,1)S(1)}, bf16[256,128]{1,0:T(8,128)(2,1)S(1)}, u32[]{:S(2)}, u32[]{:S(2)}) collective-permute-start(bf16[256,128]{1,0:T(8,128)(2,1)S(1)} %fusion.3), channel_id=1, source_target_pairs={{0,8},{1,9},{2,10},{3,11},{4,12},{5,13},{6,14},{7,15},{8,0},{9,1},... | collective-permute-start | bytes 196616 | tf_op jit(solution)/shard_map/ppermute | solution.py:340
  23.5 1.6 %collective-permute-done.11 = bf16[272,128]{1,0:T(8,128)(2,1)S(1)} collective-permute-done((bf16[272,128]{1,0:T(8,128)(2,1)S(1)}, bf16[272,128]{1,0:T(8,128)(2,1)S(1)}, u32[]{:S(2)}, u32[]{:S(2)}) %collective-permute-start.11) | collective-permute-done | bytes 69664 | tf_op jit(solution)/shard_map/ppermute | solution.py:340
  25.1 0.1 multiply_convert_fusion.amps_ref
  25.2 0.1 collective-permute-start.13
  25.3 1.0 %own_gamma.1 = (bf16[256,4096]{1,0:T(8,128)(2,1)S(1)}, f32[256,4096]{1,0:T(8,128)S(1)}, f32[1,4096]{1,0:T(1,128)S(1)}) custom-call(s32[1,32]{1,0:T(1,128)S(1)} %copy-done, bf16[272,128]{1,0:T(8,128)(2,1)S(1)} %multiply_convert_fusion.amps_ref, bf16[256,4096]{1,0:T(8,128)(2,1)S(1)} %get-tuple-element.26.own_ref), custom_call_target="tpu_custom_call" | custom-call | flops 536870912 | bytes 6291456 | tf_op jit(solution)/shard_map/own_gamma/pallas_call | solution.py:273
  26.2 0.1 collective-permute-done.7
  26.3 0.1 multiply_convert_fusion.1.cross_ref
  26.4 0.5 %collective-permute-start.12 = (bf16[256,128]{1,0:T(8,128)(2,1)S(1)}, bf16[256,128]{1,0:T(8,128)(2,1)S(1)}, u32[]{:S(2)}, u32[]{:S(2)}) collective-permute-start(bf16[256,128]{1,0:T(8,128)(2,1)S(1)} %multiply_convert_fusion.1.cross_ref), channel_id=1, source_target_pairs={{0,16},{16,0},{1,17},{17,1},{2,18},{18,2},{3,19},{19,3},{4,20},{20... | collective-permute-start | bytes 196616 | tf_op jit(solution)/shard_map/ppermute | solution.py:331
  26.8 0.0 collective-permute-done.13.amps_ref
  26.8 1.0 %other_weight.1 = (bf16[256,4096]{1,0:T(8,128)(2,1)S(1)}, f32[1,4096]{1,0:T(1,128)S(1)}) custom-call(s32[1,32]{1,0:T(1,128)S(1)} %collective-permute-done.other_screen_ref.screen_ref, bf16[272,128]{1,0:T(8,128)(2,1)S(1)} %collective-permute-done.13.amps_ref, bf16[256,4096]{1,0:T(8,128)(2,1)S(1)} %collective-permute-done.1.other_ref.own_ref, ...), custom_call_target="tpu_custom_call" | custom-call | flops 536870912 | bytes 6291456 | tf_op jit(solution)/shard_map/other_weight/pallas_call | solution.py:273
  27.8 0.0 collective-permute-done.12.other_cross_ref
  27.8 2.2 %gamma_and_virial.1 = (bf16[256,4096]{1,0:T(8,128)(2,1)}, f32[9,4096]{1,0:T(8,128)}) custom-call(bf16[256,128]{1,0:T(8,128)(2,1)S(1)} %multiply_convert_fusion.1.cross_ref, bf16[256,128]{1,0:T(8,128)(2,1)S(1)} %collective-permute-done.12.other_cross_ref, bf16[256,4096]{1,0:T(8,128)(2,1)S(1)} %get-tuple-element.42.own_ref, ...), custom_call_target="tpu_custom_call" | custom-call | flops 536870912 | bytes 8388608 | tf_op jit(solution)/shard_map/gamma_and_virial/pallas_call | solution.py:307
  (7 shorter events, 0.2 us)
Async XLA Ops:
  0.6 6.1 %copy-start = (s32[1,32]{1,0:T(1,128)S(1)}, s32[1,32]{1,0:T(1,128)}, u32[]{:S(2)}) copy-start(s32[1,32]{1,0:T(1,128)} %screen_ref.3) | copy-start | bytes 388
  0.6 6.1 %collective-permute-start.1 = (bf16[256,4096]{1,0:T(8,128)(2,1)}, bf16[256,4096]{1,0:T(8,128)(2,1)S(1)}, u32[]{:S(2)}, u32[]{:S(2)}) collective-permute-start(bf16[256,4096]{1,0:T(8,128)(2,1)} %bitcast.7), channel_id=1, source_target_pairs={{0,16},{16,0},{1,17},{17,1},{2,18},{18,2},{3,19},{19,3},{4,20},{20... | collective-permute-start | bytes 6291464 | tf_op jit(solution)/shard_map/ppermute | solution.py:331
  1.2 5.5 %collective-permute-start = (s32[1,32]{1,0:T(1,128)}, s32[1,32]{1,0:T(1,128)S(1)}, u32[]{:S(2)}, u32[]{:S(2)}) collective-permute-start(s32[1,32]{1,0:T(1,128)} %screen_ref.3), channel_id=1, source_target_pairs={{0,16},{16,0},{1,17},{17,1},{2,18},{18,2},{3,19},{19,3},{4,20},{20... | collective-permute-start | bytes 392 | tf_op jit(solution)/shard_map/ppermute | solution.py:331
  1.2 8.0 %collective-permute-start.3 = (bf16[1]{0:T(256)(128)(2,1)}, bf16[1]{0:T(256)(128)(2,1)}, u32[]{:S(2)}, u32[]{:S(2)}) collective-permute-start(bf16[1]{0:T(256)(128)(2,1)} %param.7), channel_id=1, source_target_pairs={{0,16},{16,0},{1,17},{17,1},{2,18},{18,2},{3,19},{19,3},{4,20},{20... | collective-permute-start | bytes 14 | tf_op jit(solution)/shard_map/ppermute | solution.py:331
  4.1 5.1 %collective-permute-start.8 = (bf16[272,128]{1,0:T(8,128)(2,1)S(1)}, bf16[272,128]{1,0:T(8,128)(2,1)S(1)}, u32[]{:S(2)}, u32[]{:S(2)}) collective-permute-start(bf16[272,128]{1,0:T(8,128)(2,1)S(1)} %get-tuple-element.37), channel_id=1, source_target_pairs={{0,1},{1,0},{2,3},{3,2},{4,5},{5,4},{6,7},{7,6},{8,9},{9,8},{10,11... | collective-permute-start | bytes 208904 | tf_op jit(solution)/shard_map/ppermute | solution.py:340
  6.7 5.4 %copy-start.1 = (bf16[256]{0:T(256)(128)(2,1)S(1)}, bf16[256]{0:T(256)(128)(2,1)}, u32[]{:S(2)}) copy-start(bf16[256]{0:T(256)(128)(2,1)} %param.8) | copy-start | bytes 1540
  7.6 4.5 %collective-permute-start.2 = (bf16[256,128]{1,0:T(8,128)(2,1)S(1)}, bf16[256,128]{1,0:T(8,128)(2,1)S(1)}, u32[]{:S(2)}, u32[]{:S(2)}) collective-permute-start(bf16[256,128]{1,0:T(8,128)(2,1)S(1)} %get-tuple-element.28), channel_id=1, source_target_pairs={{0,4},{1,5},{2,6},{3,7},{4,0},{5,1},{6,2},{7,3},{8,12},{9,13},{10,... | collective-permute-start | bytes 196616 | tf_op jit(solution)/shard_map/ppermute | solution.py:340
  9.2 4.7 %collective-permute-start.9 = (bf16[272,128]{1,0:T(8,128)(2,1)S(1)}, bf16[272,128]{1,0:T(8,128)(2,1)S(1)}, u32[]{:S(2)}, u32[]{:S(2)}) collective-permute-start(bf16[272,128]{1,0:T(8,128)(2,1)S(1)} %fusion), channel_id=1, source_target_pairs={{0,2},{1,3},{2,0},{3,1},{4,6},{5,7},{6,4},{7,5},{8,10},{9,11},{10,... | collective-permute-start | bytes 208904 | tf_op jit(solution)/shard_map/ppermute | solution.py:340
  12.1 1.7 %collective-permute-start.5 = (bf16[128]{0:T(256)(128)(2,1)S(1)}, bf16[128]{0:T(256)(128)(2,1)S(1)}, u32[]{:S(2)}, u32[]{:S(2)}) collective-permute-start(bf16[128]{0:T(256)(128)(2,1)S(1)} %pad.4), channel_id=1, source_target_pairs={{0,16},{16,0},{1,17},{17,1},{2,18},{18,2},{3,19},{19,3},{4,20},{20... | collective-permute-start | bytes 776 | tf_op jit(solution)/shard_map/ppermute | solution.py:331
  12.2 4.3 %collective-permute-start.4 = (bf16[256,128]{1,0:T(8,128)(2,1)S(1)}, bf16[256,128]{1,0:T(8,128)(2,1)S(1)}, u32[]{:S(2)}, u32[]{:S(2)}) collective-permute-start(bf16[256,128]{1,0:T(8,128)(2,1)S(1)} %fusion.2), channel_id=1, source_target_pairs={{0,2},{1,3},{2,0},{3,1},{4,6},{5,7},{6,4},{7,5},{8,10},{9,11},{10,... | collective-permute-start | bytes 196616 | tf_op jit(solution)/shard_map/ppermute | solution.py:340
  13.9 4.4 %collective-permute-start.10 = (bf16[272,128]{1,0:T(8,128)(2,1)S(1)}, bf16[272,128]{1,0:T(8,128)(2,1)S(1)}, u32[]{:S(2)}, u32[]{:S(2)}) collective-permute-start(bf16[272,128]{1,0:T(8,128)(2,1)S(1)} %fusion.5), channel_id=1, source_target_pairs={{0,4},{1,5},{2,6},{3,7},{4,0},{5,1},{6,2},{7,3},{8,12},{9,13},{10,... | collective-permute-start | bytes 208904 | tf_op jit(solution)/shard_map/ppermute | solution.py:340
  16.5 4.5 %collective-permute-start.6 = (bf16[256,128]{1,0:T(8,128)(2,1)S(1)}, bf16[256,128]{1,0:T(8,128)(2,1)S(1)}, u32[]{:S(2)}, u32[]{:S(2)}) collective-permute-start(bf16[256,128]{1,0:T(8,128)(2,1)S(1)} %fusion.4), channel_id=1, source_target_pairs={{0,1},{1,0},{2,3},{3,2},{4,5},{5,4},{6,7},{7,6},{8,9},{9,8},{10,11... | collective-permute-start | bytes 196616 | tf_op jit(solution)/shard_map/ppermute | solution.py:340
  18.3 6.8 %collective-permute-start.11 = (bf16[272,128]{1,0:T(8,128)(2,1)S(1)}, bf16[272,128]{1,0:T(8,128)(2,1)S(1)}, u32[]{:S(2)}, u32[]{:S(2)}) collective-permute-start(bf16[272,128]{1,0:T(8,128)(2,1)S(1)} %fusion.1), channel_id=1, source_target_pairs={{0,8},{1,9},{2,10},{3,11},{4,12},{5,13},{6,14},{7,15},{8,0},{9,1},... | collective-permute-start | bytes 208904 | tf_op jit(solution)/shard_map/ppermute | solution.py:340
  21.1 5.2 %collective-permute-start.7 = (bf16[256,128]{1,0:T(8,128)(2,1)S(1)}, bf16[256,128]{1,0:T(8,128)(2,1)S(1)}, u32[]{:S(2)}, u32[]{:S(2)}) collective-permute-start(bf16[256,128]{1,0:T(8,128)(2,1)S(1)} %fusion.3), channel_id=1, source_target_pairs={{0,8},{1,9},{2,10},{3,11},{4,12},{5,13},{6,14},{7,15},{8,0},{9,1},... | collective-permute-start | bytes 196616 | tf_op jit(solution)/shard_map/ppermute | solution.py:340
  25.2 1.7 %collective-permute-start.13 = (bf16[272,128]{1,0:T(8,128)(2,1)S(1)}, bf16[272,128]{1,0:T(8,128)(2,1)S(1)}, u32[]{:S(2)}, u32[]{:S(2)}) collective-permute-start(bf16[272,128]{1,0:T(8,128)(2,1)S(1)} %multiply_convert_fusion.amps_ref), channel_id=1, source_target_pairs={{0,16},{16,0},{1,17},{17,1},{2,18},{18,2},{3,19},{19,3},{4,20},{20... | collective-permute-start | bytes 208904 | tf_op jit(solution)/shard_map/ppermute | solution.py:331
  26.4 1.5 %collective-permute-start.12 = (bf16[256,128]{1,0:T(8,128)(2,1)S(1)}, bf16[256,128]{1,0:T(8,128)(2,1)S(1)}, u32[]{:S(2)}, u32[]{:S(2)}) collective-permute-start(bf16[256,128]{1,0:T(8,128)(2,1)S(1)} %multiply_convert_fusion.1.cross_ref), channel_id=1, source_target_pairs={{0,16},{16,0},{1,17},{17,1},{2,18},{18,2},{3,19},{19,3},{4,20},{20... | collective-permute-start | bytes 196616 | tf_op jit(solution)/shard_map/ppermute | solution.py:331

commit v7 on v5

--- a/solution.py
+++ b/solution.py
@@ -351,7 +351,7 @@
         turned = bits[1:] + bits[:1]
         return (bits, turned), (bits, turned)
     x, y, z, w = bits
-    return ([z, y, x, w], [z, x, w, y]), ([x, y, z, w], [y, z, x, w])
+    return ([x, y, z, w], [z, x, w, y]), ([x, y, z, w], [w, z, x, y])
 
 
 def two_occ_body(n_aux, coeffs, occ_energy, virt_energy, screen, owner, positions):

time: 29.9 us -> 30.2 us (1.010)
  starting transfers between devices: 17.5 us -> 18 us
    ppermute x8, starting transfers between devices: 15.9 us -> 16.7 us  [swap_by_core(): return lax.ppermute(array, ('occ', 'aux'), pairs)]
    ppermute x8, waiting for transfers between devices: 3.32 us -> 2.85 us  [swap_by_core(): return lax.ppermute(array, ('occ', 'aux'), pairs)]
  transfers between devices with their start and end apart: 14 -> 14, of which waited for: 5 -> 6; matrix products, arithmetic and copies ran while one was open for 3% -> 3% of each run, Pallas kernels for 18% -> 18%
where the time goes in v7:
time: 30.2 us; the launch traced here: 30 us
  starting transfers between devices  18 us (60%)
  Pallas kernels  7.17 us (24%)
  waiting for transfers between devices  3.12 us (10%)
  between operations  0.77 us (3%)
  local copies, waits for them, and re-layouts  0.64 us (2%)
    ppermute x8, starting transfers between devices, swap_by_core(): return lax.ppermute(array, ('occ', 'aux'), pairs)  16.7 us
    ppermute x8, waiting for transfers between devices, swap_by_core(): return lax.ppermute(array, ('occ', 'aux'), pairs)  2.85 us
    pallas_call x1, Pallas kernels, own_pairs(): pl.pallas_call(functools.partial(own_pairs_kernel, blocks, aux_dev // blo...  2.4 us
    pallas_call x2, Pallas kernels, gamma_call(): pl.pallas_call(functools.partial(kernel, steps, blocks, aux_dev // blocks...  1.93 us
    pallas_call x1, Pallas kernels, gamma_and_virial(): pl.pallas_call(functools.partial(gamma_kernel, steps), in_specs=[vmem] *...  1.91 us
    ppermute x6, starting transfers between devices, swap(): return lax.ppermute(array, axis, [(i, i ^ bit) for i in range(size)])  1.35 us
    pallas_call x1, Pallas kernels, cross_pairs(): pl.pallas_call(functools.partial(cross_pairs_kernel, blocks, aux_dev // b...  0.82 us
    pad x1, local copies, waits for them, and re-layouts, two_occ_body(): other_energy = jnp.pad(other_one, (0, LANES - 1))  0.63 us
  transfers between devices with their start and end apart: 14, of which 6 were waited for; matrix products, arithmetic and copies ran while one was open for 3% of the time, Pallas kernels for 18%

profile of v7, /device:TPU:0, one launch (start us, length us, event | category | flops | bytes accessed | tf_op | source)
XLA Modules:
  0.0 30.0 jit_solution(14797584437128478602)
XLA Ops:
  0.6 0.0 copy-start
  0.6 0.5 %collective-permute-start.1 = (bf16[256,4096]{1,0:T(8,128)(2,1)}, bf16[256,4096]{1,0:T(8,128)(2,1)S(1)}, u32[]{:S(2)}, u32[]{:S(2)}) collective-permute-start(bf16[256,4096]{1,0:T(8,128)(2,1)} %bitcast.7), channel_id=1, source_target_pairs={{0,16},{16,0},{1,17},{17,1},{2,18},{18,2},{3,19},{19,3},{4,20},{20... | collective-permute-start | bytes 6291464 | tf_op jit(solution)/shard_map/ppermute | solution.py:328
  1.2 0.1 collective-permute-start
  1.2 0.4 %collective-permute-start.3 = (bf16[1]{0:T(256)(128)(2,1)}, bf16[1]{0:T(256)(128)(2,1)}, u32[]{:S(2)}, u32[]{:S(2)}) collective-permute-start(bf16[1]{0:T(256)(128)(2,1)} %param.7), channel_id=1, source_target_pairs={{0,16},{16,0},{1,17},{17,1},{2,18},{18,2},{3,19},{19,3},{4,20},{20... | collective-permute-start | bytes 14 | tf_op jit(solution)/shard_map/ppermute | solution.py:328
  1.7 2.4 %own_pairs.1 = (bf16[256,4096]{1,0:T(8,128)(2,1)S(1)}, f32[9,4096]{1,0:T(8,128)S(1)}, f32[272,128]{1,0:T(8,128)S(1)}, bf16[272,128]{1,0:T(8,128)(2,1)S(1)}) custom-call(s32[1,32]{1,0:T(1,128)} %screen_ref.3, s32[1,32]{1,0:T(1,128)} %bitcast.9, f32[3,128]{1,0:T(4,128)} %positions_hbm.1, bf16[256,4096]{1,0:T(8,128)(2,1)} %bitcast.8), custom_call_target="tpu_custom_call" | custom-call | flops 536870912 | bytes 2097152 | tf_op jit(solution)/shard_map/own_pairs/pallas_call | solution.py:103
  4.1 2.6 %collective-permute-start.8 = (bf16[272,128]{1,0:T(8,128)(2,1)S(1)}, bf16[272,128]{1,0:T(8,128)(2,1)S(1)}, u32[]{:S(2)}, u32[]{:S(2)}) collective-permute-start(bf16[272,128]{1,0:T(8,128)(2,1)S(1)} %get-tuple-element.37), channel_id=1, source_target_pairs={{0,1},{1,0},{2,3},{3,2},{4,5},{5,4},{6,7},{7,6},{8,9},{9,8},{10,11... | collective-permute-start | bytes 208904 | tf_op jit(solution)/shard_map/ppermute | solution.py:337
  6.7 0.0 collective-permute-done.other_screen_ref.screen_ref
  6.7 0.0 collective-permute-done.1.other_ref.own_ref
  6.7 0.0 copy-done
  6.7 0.0 copy-start.1
  6.7 0.8 %cross_pairs.1 = (f32[256,128]{1,0:T(8,128)S(1)}, bf16[256,128]{1,0:T(8,128)(2,1)S(1)}) custom-call(s32[1,32]{1,0:T(1,128)S(1)} %copy-done, s32[1,32]{1,0:T(1,128)S(1)} %collective-permute-done.other_screen_ref.screen_ref, bf16[256,4096]{1,0:T(8,128)(2,1)S(1)} %get-tuple-element.26.own_ref, bf16[256,4096]{1,0:T(8,128)(2,1)S(1)} %collective-permute-done.1.other_ref.own_ref), custom_call_target="tpu_custom_call" | custom-call | flops 2147483648 | bytes 16777216 | tf_op jit(solution)/shard_map/cross_pairs/pallas_call | solution.py:133
  7.6 1.4 %collective-permute-start.2 = (bf16[256,128]{1,0:T(8,128)(2,1)S(1)}, bf16[256,128]{1,0:T(8,128)(2,1)S(1)}, u32[]{:S(2)}, u32[]{:S(2)}) collective-permute-start(bf16[256,128]{1,0:T(8,128)(2,1)S(1)} %get-tuple-element.28), channel_id=1, source_target_pairs={{0,1},{1,0},{2,3},{3,2},{4,5},{5,4},{6,7},{7,6},{8,9},{9,8},{10,11... | collective-permute-start | bytes 196616 | tf_op jit(solution)/shard_map/ppermute | solution.py:337
  8.9 0.1 collective-permute-done.8
  9.0 0.0 collective-permute-done.3
  9.0 2.1 %collective-permute-start.9 = (bf16[272,128]{1,0:T(8,128)(2,1)S(1)}, bf16[272,128]{1,0:T(8,128)(2,1)S(1)}, u32[]{:S(2)}, u32[]{:S(2)}) collective-permute-start(bf16[272,128]{1,0:T(8,128)(2,1)S(1)} %fusion), channel_id=1, source_target_pairs={{0,2},{1,3},{2,0},{3,1},{4,6},{5,7},{6,4},{7,5},{8,10},{9,11},{10,... | collective-permute-start | bytes 208904 | tf_op jit(solution)/shard_map/ppermute | solution.py:337
  11.1 0.6 %pad.4 = bf16[128]{0:T(256)(128)(2,1)S(1)} pad(bf16[1]{0:T(256)(128)(2,1)} %collective-permute-done.3, bf16[]{:T(256)} %constant.2.clone.1), padding=0_127 | pad | bytes 260 | tf_op jit(solution)/shard_map/jit(_pad)/pad | solution.py:368
  11.8 0.1 collective-permute-done.2
  11.9 0.2 collective-permute-start.5
  12.1 0.0 copy-done.1
  12.1 1.5 %collective-permute-start.4 = (bf16[256,128]{1,0:T(8,128)(2,1)S(1)}, bf16[256,128]{1,0:T(8,128)(2,1)S(1)}, u32[]{:S(2)}, u32[]{:S(2)}) collective-permute-start(bf16[256,128]{1,0:T(8,128)(2,1)S(1)} %fusion.2), channel_id=1, source_target_pairs={{0,2},{1,3},{2,0},{3,1},{4,6},{5,7},{6,4},{7,5},{8,10},{9,11},{10,... | collective-permute-start | bytes 196616 | tf_op jit(solution)/shard_map/ppermute | solution.py:337
  13.6 0.0 collective-permute-done.5
  13.6 0.1 inverse_spreads.1
  13.7 0.0 collective-permute-done.9
  13.8 1.8 %collective-permute-start.10 = (bf16[272,128]{1,0:T(8,128)(2,1)S(1)}, bf16[272,128]{1,0:T(8,128)(2,1)S(1)}, u32[]{:S(2)}, u32[]{:S(2)}) collective-permute-start(bf16[272,128]{1,0:T(8,128)(2,1)S(1)} %fusion.5), channel_id=1, source_target_pairs={{0,4},{1,5},{2,6},{3,7},{4,0},{5,1},{6,2},{7,3},{8,12},{9,13},{10,... | collective-permute-start | bytes 208904 | tf_op jit(solution)/shard_map/ppermute | solution.py:337
  15.6 0.8 %collective-permute-done.4 = bf16[256,128]{1,0:T(8,128)(2,1)S(1)} collective-permute-done((bf16[256,128]{1,0:T(8,128)(2,1)S(1)}, bf16[256,128]{1,0:T(8,128)(2,1)S(1)}, u32[]{:S(2)}, u32[]{:S(2)}) %collective-permute-start.4) | collective-permute-done | bytes 65568 | tf_op jit(solution)/shard_map/ppermute | solution.py:337
  16.4 1.6 %collective-permute-start.6 = (bf16[256,128]{1,0:T(8,128)(2,1)S(1)}, bf16[256,128]{1,0:T(8,128)(2,1)S(1)}, u32[]{:S(2)}, u32[]{:S(2)}) collective-permute-start(bf16[256,128]{1,0:T(8,128)(2,1)S(1)} %fusion.4), channel_id=1, source_target_pairs={{0,4},{1,5},{2,6},{3,7},{4,0},{5,1},{6,2},{7,3},{8,12},{9,13},{10,... | collective-permute-start | bytes 196616 | tf_op jit(solution)/shard_map/ppermute | solution.py:337
  18.0 0.1 collective-permute-done.10
  18.2 3.2 %collective-permute-start.11 = (bf16[272,128]{1,0:T(8,128)(2,1)S(1)}, bf16[272,128]{1,0:T(8,128)(2,1)S(1)}, u32[]{:S(2)}, u32[]{:S(2)}) collective-permute-start(bf16[272,128]{1,0:T(8,128)(2,1)S(1)} %fusion.1), channel_id=1, source_target_pairs={{0,8},{1,9},{2,10},{3,11},{4,12},{5,13},{6,14},{7,15},{8,0},{9,1},... | collective-permute-start | bytes 208904 | tf_op jit(solution)/shard_map/ppermute | solution.py:337
  21.4 0.0 collective-permute-done.6
  21.5 2.4 %collective-permute-start.7 = (bf16[256,128]{1,0:T(8,128)(2,1)S(1)}, bf16[256,128]{1,0:T(8,128)(2,1)S(1)}, u32[]{:S(2)}, u32[]{:S(2)}) collective-permute-start(bf16[256,128]{1,0:T(8,128)(2,1)S(1)} %fusion.3), channel_id=1, source_target_pairs={{0,8},{1,9},{2,10},{3,11},{4,12},{5,13},{6,14},{7,15},{8,0},{9,1},... | collective-permute-start | bytes 196616 | tf_op jit(solution)/shard_map/ppermute | solution.py:337
  23.8 0.0 collective-permute-done.11
  23.8 0.1 multiply_convert_fusion.amps_ref
  23.9 0.1 collective-permute-start.13
  24.0 1.0 %own_gamma.1 = (bf16[256,4096]{1,0:T(8,128)(2,1)S(1)}, f32[256,4096]{1,0:T(8,128)S(1)}, f32[1,4096]{1,0:T(1,128)S(1)}) custom-call(s32[1,32]{1,0:T(1,128)S(1)} %copy-done, bf16[272,128]{1,0:T(8,128)(2,1)S(1)} %multiply_convert_fusion.amps_ref, bf16[256,4096]{1,0:T(8,128)(2,1)S(1)} %get-tuple-element.26.own_ref), custom_call_target="tpu_custom_call" | custom-call | flops 536870912 | bytes 6291456 | tf_op jit(solution)/shard_map/own_gamma/pallas_call | solution.py:270
  24.9 1.8 %collective-permute-done.7 = bf16[256,128]{1,0:T(8,128)(2,1)S(1)} collective-permute-done((bf16[256,128]{1,0:T(8,128)(2,1)S(1)}, bf16[256,128]{1,0:T(8,128)(2,1)S(1)}, u32[]{:S(2)}, u32[]{:S(2)}) %collective-permute-start.7) | collective-permute-done | bytes 65568 | tf_op jit(solution)/shard_map/ppermute | solution.py:337
  26.7 0.1 multiply_convert_fusion.1.cross_ref
  26.8 0.1 collective-permute-start.12
  26.9 0.0 collective-permute-done.13.amps_ref
  26.9 1.0 %other_weight.1 = (bf16[256,4096]{1,0:T(8,128)(2,1)S(1)}, f32[1,4096]{1,0:T(1,128)S(1)}) custom-call(s32[1,32]{1,0:T(1,128)S(1)} %collective-permute-done.other_screen_ref.screen_ref, bf16[272,128]{1,0:T(8,128)(2,1)S(1)} %collective-permute-done.13.amps_ref, bf16[256,4096]{1,0:T(8,128)(2,1)S(1)} %collective-permute-done.1.other_ref.own_ref, ...), custom_call_target="tpu_custom_call" | custom-call | flops 536870912 | bytes 6291456 | tf_op jit(solution)/shard_map/other_weight/pallas_call | solution.py:270
  27.8 0.2 collective-permute-done.12.other_cross_ref
  28.1 1.9 %gamma_and_virial.1 = (bf16[256,4096]{1,0:T(8,128)(2,1)}, f32[9,4096]{1,0:T(8,128)}) custom-call(bf16[256,128]{1,0:T(8,128)(2,1)S(1)} %multiply_convert_fusion.1.cross_ref, bf16[256,128]{1,0:T(8,128)(2,1)S(1)} %collective-permute-done.12.other_cross_ref, bf16[256,4096]{1,0:T(8,128)(2,1)S(1)} %get-tuple-element.42.own_ref, ...), custom_call_target="tpu_custom_call" | custom-call | flops 536870912 | bytes 8388608 | tf_op jit(solution)/shard_map/gamma_and_virial/pallas_call | solution.py:304
  (7 shorter events, 0.2 us)
Async XLA Ops:
  0.6 6.1 %copy-start = (s32[1,32]{1,0:T(1,128)S(1)}, s32[1,32]{1,0:T(1,128)}, u32[]{:S(2)}) copy-start(s32[1,32]{1,0:T(1,128)} %screen_ref.3) | copy-start | bytes 388
  0.6 6.1 %collective-permute-start.1 = (bf16[256,4096]{1,0:T(8,128)(2,1)}, bf16[256,4096]{1,0:T(8,128)(2,1)S(1)}, u32[]{:S(2)}, u32[]{:S(2)}) collective-permute-start(bf16[256,4096]{1,0:T(8,128)(2,1)} %bitcast.7), channel_id=1, source_target_pairs={{0,16},{16,0},{1,17},{17,1},{2,18},{18,2},{3,19},{19,3},{4,20},{20... | collective-permute-start | bytes 6291464 | tf_op jit(solution)/shard_map/ppermute | solution.py:328
  1.2 5.5 %collective-permute-start = (s32[1,32]{1,0:T(1,128)}, s32[1,32]{1,0:T(1,128)S(1)}, u32[]{:S(2)}, u32[]{:S(2)}) collective-permute-start(s32[1,32]{1,0:T(1,128)} %screen_ref.3), channel_id=1, source_target_pairs={{0,16},{16,0},{1,17},{17,1},{2,18},{18,2},{3,19},{19,3},{4,20},{20... | collective-permute-start | bytes 392 | tf_op jit(solution)/shard_map/ppermute | solution.py:328
  1.2 7.8 %collective-permute-start.3 = (bf16[1]{0:T(256)(128)(2,1)}, bf16[1]{0:T(256)(128)(2,1)}, u32[]{:S(2)}, u32[]{:S(2)}) collective-permute-start(bf16[1]{0:T(256)(128)(2,1)} %param.7), channel_id=1, source_target_pairs={{0,16},{16,0},{1,17},{17,1},{2,18},{18,2},{3,19},{19,3},{4,20},{20... | collective-permute-start | bytes 14 | tf_op jit(solution)/shard_map/ppermute | solution.py:328
  4.1 4.9 %collective-permute-start.8 = (bf16[272,128]{1,0:T(8,128)(2,1)S(1)}, bf16[272,128]{1,0:T(8,128)(2,1)S(1)}, u32[]{:S(2)}, u32[]{:S(2)}) collective-permute-start(bf16[272,128]{1,0:T(8,128)(2,1)S(1)} %get-tuple-element.37), channel_id=1, source_target_pairs={{0,1},{1,0},{2,3},{3,2},{4,5},{5,4},{6,7},{7,6},{8,9},{9,8},{10,11... | collective-permute-start | bytes 208904 | tf_op jit(solution)/shard_map/ppermute | solution.py:337
  6.7 5.4 %copy-start.1 = (bf16[256]{0:T(256)(128)(2,1)S(1)}, bf16[256]{0:T(256)(128)(2,1)}, u32[]{:S(2)}) copy-start(bf16[256]{0:T(256)(128)(2,1)} %param.8) | copy-start | bytes 1540
  7.6 4.3 %collective-permute-start.2 = (bf16[256,128]{1,0:T(8,128)(2,1)S(1)}, bf16[256,128]{1,0:T(8,128)(2,1)S(1)}, u32[]{:S(2)}, u32[]{:S(2)}) collective-permute-start(bf16[256,128]{1,0:T(8,128)(2,1)S(1)} %get-tuple-element.28), channel_id=1, source_target_pairs={{0,1},{1,0},{2,3},{3,2},{4,5},{5,4},{6,7},{7,6},{8,9},{9,8},{10,11... | collective-permute-start | bytes 196616 | tf_op jit(solution)/shard_map/ppermute | solution.py:337
  9.0 4.7 %collective-permute-start.9 = (bf16[272,128]{1,0:T(8,128)(2,1)S(1)}, bf16[272,128]{1,0:T(8,128)(2,1)S(1)}, u32[]{:S(2)}, u32[]{:S(2)}) collective-permute-start(bf16[272,128]{1,0:T(8,128)(2,1)S(1)} %fusion), channel_id=1, source_target_pairs={{0,2},{1,3},{2,0},{3,1},{4,6},{5,7},{6,4},{7,5},{8,10},{9,11},{10,... | collective-permute-start | bytes 208904 | tf_op jit(solution)/shard_map/ppermute | solution.py:337
  11.9 1.7 %collective-permute-start.5 = (bf16[128]{0:T(256)(128)(2,1)S(1)}, bf16[128]{0:T(256)(128)(2,1)S(1)}, u32[]{:S(2)}, u32[]{:S(2)}) collective-permute-start(bf16[128]{0:T(256)(128)(2,1)S(1)} %pad.4), channel_id=1, source_target_pairs={{0,16},{16,0},{1,17},{17,1},{2,18},{18,2},{3,19},{19,3},{4,20},{20... | collective-permute-start | bytes 776 | tf_op jit(solution)/shard_map/ppermute | solution.py:328
  12.1 4.3 %collective-permute-start.4 = (bf16[256,128]{1,0:T(8,128)(2,1)S(1)}, bf16[256,128]{1,0:T(8,128)(2,1)S(1)}, u32[]{:S(2)}, u32[]{:S(2)}) collective-permute-start(bf16[256,128]{1,0:T(8,128)(2,1)S(1)} %fusion.2), channel_id=1, source_target_pairs={{0,2},{1,3},{2,0},{3,1},{4,6},{5,7},{6,4},{7,5},{8,10},{9,11},{10,... | collective-permute-start | bytes 196616 | tf_op jit(solution)/shard_map/ppermute | solution.py:337
  13.8 4.4 %collective-permute-start.10 = (bf16[272,128]{1,0:T(8,128)(2,1)S(1)}, bf16[272,128]{1,0:T(8,128)(2,1)S(1)}, u32[]{:S(2)}, u32[]{:S(2)}) collective-permute-start(bf16[272,128]{1,0:T(8,128)(2,1)S(1)} %fusion.5), channel_id=1, source_target_pairs={{0,4},{1,5},{2,6},{3,7},{4,0},{5,1},{6,2},{7,3},{8,12},{9,13},{10,... | collective-permute-start | bytes 208904 | tf_op jit(solution)/shard_map/ppermute | solution.py:337
  16.4 5.0 %collective-permute-start.6 = (bf16[256,128]{1,0:T(8,128)(2,1)S(1)}, bf16[256,128]{1,0:T(8,128)(2,1)S(1)}, u32[]{:S(2)}, u32[]{:S(2)}) collective-permute-start(bf16[256,128]{1,0:T(8,128)(2,1)S(1)} %fusion.4), channel_id=1, source_target_pairs={{0,4},{1,5},{2,6},{3,7},{4,0},{5,1},{6,2},{7,3},{8,12},{9,13},{10,... | collective-permute-start | bytes 196616 | tf_op jit(solution)/shard_map/ppermute | solution.py:337
  18.2 5.6 %collective-permute-start.11 = (bf16[272,128]{1,0:T(8,128)(2,1)S(1)}, bf16[272,128]{1,0:T(8,128)(2,1)S(1)}, u32[]{:S(2)}, u32[]{:S(2)}) collective-permute-start(bf16[272,128]{1,0:T(8,128)(2,1)S(1)} %fusion.1), channel_id=1, source_target_pairs={{0,8},{1,9},{2,10},{3,11},{4,12},{5,13},{6,14},{7,15},{8,0},{9,1},... | collective-permute-start | bytes 208904 | tf_op jit(solution)/shard_map/ppermute | solution.py:337
  21.5 5.2 %collective-permute-start.7 = (bf16[256,128]{1,0:T(8,128)(2,1)S(1)}, bf16[256,128]{1,0:T(8,128)(2,1)S(1)}, u32[]{:S(2)}, u32[]{:S(2)}) collective-permute-start(bf16[256,128]{1,0:T(8,128)(2,1)S(1)} %fusion.3), channel_id=1, source_target_pairs={{0,8},{1,9},{2,10},{3,11},{4,12},{5,13},{6,14},{7,15},{8,0},{9,1},... | collective-permute-start | bytes 196616 | tf_op jit(solution)/shard_map/ppermute | solution.py:337
  23.9 2.9 %collective-permute-start.13 = (bf16[272,128]{1,0:T(8,128)(2,1)S(1)}, bf16[272,128]{1,0:T(8,128)(2,1)S(1)}, u32[]{:S(2)}, u32[]{:S(2)}) collective-permute-start(bf16[272,128]{1,0:T(8,128)(2,1)S(1)} %multiply_convert_fusion.amps_ref), channel_id=1, source_target_pairs={{0,16},{16,0},{1,17},{17,1},{2,18},{18,2},{3,19},{19,3},{4,20},{20... | collective-permute-start | bytes 208904 | tf_op jit(solution)/shard_map/ppermute | solution.py:328
  26.8 1.3 %collective-permute-start.12 = (bf16[256,128]{1,0:T(8,128)(2,1)S(1)}, bf16[256,128]{1,0:T(8,128)(2,1)S(1)}, u32[]{:S(2)}, u32[]{:S(2)}) collective-permute-start(bf16[256,128]{1,0:T(8,128)(2,1)S(1)} %multiply_convert_fusion.1.cross_ref), channel_id=1, source_target_pairs={{0,16},{16,0},{1,17},{17,1},{2,18},{18,2},{3,19},{19,3},{4,20},{20... | collective-permute-start | bytes 196616 | tf_op jit(solution)/shard_map/ppermute | solution.py:328
